TPU v7x, 32 devices: a whole 2x2x4 slice. The times are simulated.
32 devices in a mesh: exp: 8 (over z, x), hid: 4 (over y, core).
Axes of the slice: x: 2, y: 2, z: 4, core: 2. Of those that a mesh axis runs over, the one named last changes fastest.
Arguments:
- tokens: bfloat16 [16384, 1024], P(('exp', 'hid')), may hold values from -6 to 6
- token_ids: int32 [16384], P(('exp', 'hid')), may hold values from 0 to 8007
- lengths: int32 [32, 2], P(('exp', 'hid')), may hold values from 0 to 512, as said below
- hash_table: int32 [8008], replicated, may hold values from 0 to 31
- capacity: int32 [32], replicated, may hold values from 16 to 32, as said below
- gain_one: float32 [1024], replicated, may hold values from 0.5 to 1.5
- shift_one: float32 [1024], replicated, may hold values from -0.6 to 0.6
- w_qkv: bfloat16 [1024, 3072], replicated, may hold values from -0.1875 to 0.1875
- w_out: bfloat16 [1024, 1024], replicated, may hold values from -1.5 to 1.5
- gain_two: float32 [1024], replicated, may hold values from 0.5 to 1.5
- shift_two: float32 [1024], replicated, may hold values from -0.6 to 0.6
- w_in: bfloat16 [32, 1024, 4096], P('exp', None, 'hid'), may hold values from -0.1875 to 0.1875
- bias_in: float32 [32, 4096], P('exp', 'hid'), may hold values from -0.6 to 0.6
- w_back: bfloat16 [32, 4096, 1024], P('exp', 'hid'), may hold values from -0.125 to 0.125
- bias_back: float32 [32, 1024], P('exp'), may hold values from -0.6 to 0.6
- cotangent: bfloat16 [16384, 1024], P(('exp', 'hid')), may hold values from -15 to 15, as said below
Outputs:
- output: bfloat16 [16384, 1024], P(('exp', 'hid'))
- grad_tokens: float32 [16384, 1024], P(('exp', 'hid'))
- grad_gain_one: float32 [1024], replicated
- grad_shift_one: float32 [1024], replicated
- grad_qkv: float32 [1024, 3072], replicated
- grad_out: float32 [1024, 1024], replicated
- grad_gain_two: float32 [1024], replicated
- grad_shift_two: float32 [1024], replicated
- grad_in: float32 [32, 1024, 4096], P('exp', None, 'hid')
- grad_bias_in: float32 [32, 4096], P('exp', 'hid')
- grad_back: float32 [32, 4096, 1024], P('exp', 'hid')
- grad_bias_back: float32 [32, 1024], P('exp')
Inputs may be any that keep to these rules, and one draw needn't show every extreme that they name: `cotangent`: cotangent of the block's output. `capacity`: some experts take 32, some 32 // 2. `lengths`: each row is either one sequence of 512 followed by zeros, or 2 sequences of 256; some rows are of each kind.
All inputs are finite; a program needn't handle non-finite values.
Results may differ from a plain program's by a relative error of at most 0.011.
Values may be sent and summed in bfloat16 or wider, within the bound.
A program may use at most 320 MiB of HBM per device.

v0:
```python
import jax
import jax.numpy as jnp
from jax import lax
from jax.sharding import PartitionSpec as P

HEADS = 16


epsilon = 1e-05
masked_score = -1e30


def norm_rows(tok_rows, norm_gain, norm_shift):
    row_mean = jnp.mean(tok_rows, axis=-1, keepdims=True)
    centred = tok_rows - row_mean
    row_var = jnp.mean(centred * centred, axis=-1, keepdims=True)
    inverse = lax.rsqrt(row_var + epsilon)
    unit_rows = centred * inverse
    return (unit_rows * norm_gain + norm_shift, unit_rows, inverse)


def norm_back(upstream, unit_rows, inverse, norm_gain):
    scaled = upstream * norm_gain
    inner = (
        scaled
        - jnp.mean(scaled, axis=-1, keepdims=True)
        - unit_rows * jnp.mean(scaled * unit_rows, axis=-1, keepdims=True)
    )
    return (inner * inverse, jnp.sum(upstream * unit_rows, axis=0), jnp.sum(upstream, axis=0))


def slot_matrix(token_ids, hash_table, capacity):
    tok_count = token_ids.shape[0]
    expert_count = capacity.shape[0]
    slot_cap = 2 * tok_count // expert_count
    chosen = jnp.take(hash_table, token_ids)
    onehot = (chosen[:, None] == jnp.arange(expert_count, dtype=jnp.int32)[None, :]).astype(
        jnp.int32
    )
    before = jnp.cumsum(onehot, axis=0) - onehot
    rank_in = jnp.sum(before * onehot, axis=1)
    limits = jnp.sum(onehot * capacity[None, :], axis=1)
    slot_ids = chosen * slot_cap + rank_in
    slot_range = jnp.arange(expert_count * slot_cap, dtype=jnp.int32)
    matches = (slot_ids[None, :] == slot_range[:, None]) & (rank_in < limits)[None, :]
    return (matches.astype(jnp.bfloat16), slot_cap)


def doc_mask(lengths, tok_count):
    doc_ends = jnp.cumsum(lengths[0])
    places = jnp.arange(tok_count, dtype=jnp.int32)
    doc_ids = jnp.sum((places[:, None] >= doc_ends[None, :]).astype(jnp.int32), axis=1)
    return (doc_ids[:, None] == doc_ids[None, :]) & (places[:, None] >= places[None, :])


def contract_first(left, right):
    return lax.dot_general(
        left, right, (((0,), (0,)), ((), ())), preferred_element_type=jnp.float32
    )


def contract_last(left, right):
    return lax.dot_general(
        left, right, (((1,), (1,)), ((), ())), preferred_element_type=jnp.float32
    )


def per_device(
    tokens,
    token_ids,
    lengths,
    hash_table,
    capacity,
    gain_one,
    shift_one,
    w_qkv,
    w_out,
    gain_two,
    shift_two,
    w_in,
    bias_in,
    w_back,
    bias_back,
    cotangent,
):
    tok_count, width = tokens.shape
    head_dim = width // HEADS
    scale = head_dim ** (-0.5)
    local_count = w_in.shape[0]
    allowed = doc_mask(lengths, tok_count)[None]
    slot_table, slot_cap = slot_matrix(token_ids, hash_table, capacity)
    tok_rows = tokens.astype(jnp.float32)
    normed_one, unit_one, inverse_one = norm_rows(tok_rows, gain_one, shift_one)
    normed_one = normed_one.astype(jnp.bfloat16)
    mixed = jnp.dot(normed_one, w_qkv, preferred_element_type=jnp.float32).astype(jnp.bfloat16)
    qkv_parts = mixed.reshape(tok_count, 3, HEADS, head_dim)
    query_rows = qkv_parts[:, 0]
    key_rows = qkv_parts[:, 1]
    value_rows = qkv_parts[:, 2]
    scores = (
        jnp.einsum("qhd,khd->hqk", query_rows, key_rows, preferred_element_type=jnp.float32) * scale
    )
    scores = jnp.where(allowed, scores, masked_score)
    row_max = jnp.max(scores, axis=-1, keepdims=True)
    exponent = jnp.exp(scores - row_max)
    totals = jnp.sum(exponent, axis=-1, keepdims=True)
    attn_probs = (exponent / totals).astype(jnp.bfloat16)
    log_total = row_max + jnp.log(totals)
    context = jnp.einsum("hqk,khd->qhd", attn_probs, value_rows, preferred_element_type=jnp.float32)
    context = context.reshape(tok_count, width).astype(jnp.bfloat16)
    middle = tok_rows + jnp.dot(context, w_out, preferred_element_type=jnp.float32)
    normed_two, unit_two, inverse_two = norm_rows(middle, gain_two, shift_two)
    normed_two = normed_two.astype(jnp.bfloat16)
    send_rows = jnp.dot(slot_table, normed_two, preferred_element_type=jnp.float32).astype(
        jnp.bfloat16
    )
    received = lax.all_to_all(send_rows, "exp", split_axis=0, concat_axis=0, tiled=True)
    received = received.reshape(-1, local_count, slot_cap, width)
    expert_rows = lax.all_gather(received, "hid", axis=0, tiled=True)
    hidden_pre = (
        jnp.einsum("necd,edf->necf", expert_rows, w_in, preferred_element_type=jnp.float32)
        + bias_in[None, :, None, :]
    )
    hidden = jax.nn.silu(hidden_pre).astype(jnp.bfloat16)
    piece_rows = hidden
    summed = lax.psum_scatter(
        jnp.einsum("necf,efd->necd", piece_rows, w_back, preferred_element_type=jnp.float32).astype(
            jnp.bfloat16
        ),
        "hid",
        scatter_dimension=0,
        tiled=True,
    ).astype(jnp.float32)
    expert_out = (summed + bias_back[None, :, None, :]).astype(jnp.bfloat16)
    returned = lax.all_to_all(
        expert_out.reshape(-1, width), "exp", split_axis=0, concat_axis=0, tiled=True
    )
    output = (middle + contract_first(slot_table, returned)).astype(jnp.bfloat16)
    grad_send = jnp.dot(slot_table, cotangent, preferred_element_type=jnp.float32).astype(
        jnp.bfloat16
    )
    grad_recv = lax.all_to_all(grad_send, "exp", split_axis=0, concat_axis=0, tiled=True)
    grad_recv = grad_recv.reshape(-1, local_count, slot_cap, width)
    grad_expert = lax.all_gather(grad_recv, "hid", axis=0, tiled=True)
    again_pre = (
        jnp.einsum("necd,edf->necf", expert_rows, w_in, preferred_element_type=jnp.float32)
        + bias_in[None, :, None, :]
    )
    sigmoid_pre = jax.nn.sigmoid(again_pre)
    again_hidden = (again_pre * sigmoid_pre).astype(jnp.bfloat16)
    grad_back = jnp.einsum(
        "necf,necd->efd", again_hidden, grad_expert, preferred_element_type=jnp.float32
    )
    grad_bias_back = jnp.sum(grad_expert, axis=(0, 2), dtype=jnp.float32)
    grad_hidden = jnp.einsum(
        "necd,efd->necf", grad_expert, w_back, preferred_element_type=jnp.float32
    )
    grad_pre = (grad_hidden * sigmoid_pre * (1.0 + again_pre * (1.0 - sigmoid_pre))).astype(
        jnp.bfloat16
    )
    grad_in = jnp.einsum(
        "necd,necf->edf", expert_rows, grad_pre, preferred_element_type=jnp.float32
    )
    grad_bias_in = jnp.sum(grad_pre, axis=(0, 2), dtype=jnp.float32)
    piece_rows = grad_pre
    grad_summed = lax.psum_scatter(
        jnp.einsum("necf,edf->necd", piece_rows, w_in, preferred_element_type=jnp.float32),
        "hid",
        scatter_dimension=0,
        tiled=True,
    )
    grad_dispatched = grad_summed.astype(jnp.bfloat16).reshape(-1, width)
    grad_returned = lax.all_to_all(grad_dispatched, "exp", split_axis=0, concat_axis=0, tiled=True)
    grad_normed_two = contract_first(slot_table, grad_returned)
    grad_norm_two, grad_gain_two, grad_shift_two = norm_back(
        grad_normed_two, unit_two, inverse_two, gain_two
    )
    grad_middle = cotangent.astype(jnp.float32) + grad_norm_two
    grad_attn = grad_middle.astype(jnp.bfloat16)
    grad_out = contract_first(context, grad_attn)
    grad_context = (
        contract_last(grad_attn, w_out).astype(jnp.bfloat16).reshape(tok_count, HEADS, head_dim)
    )
    again_scores = (
        jnp.einsum("qhd,khd->hqk", query_rows, key_rows, preferred_element_type=jnp.float32) * scale
    )
    probs_full = jnp.where(allowed, jnp.exp(again_scores - log_total), 0.0)
    probs_low = probs_full.astype(jnp.bfloat16)
    grad_value = jnp.einsum(
        "hqk,qhd->khd", probs_low, grad_context, preferred_element_type=jnp.float32
    )
    grad_probs = jnp.einsum(
        "qhd,khd->hqk", grad_context, value_rows, preferred_element_type=jnp.float32
    )
    inner_sum = jnp.sum(grad_probs * probs_full, axis=-1, keepdims=True)
    grad_scores = (probs_full * (grad_probs - inner_sum) * scale).astype(jnp.bfloat16)
    grad_query = jnp.einsum(
        "hqk,khd->qhd", grad_scores, key_rows, preferred_element_type=jnp.float32
    )
    grad_key = jnp.einsum(
        "hqk,qhd->khd", grad_scores, query_rows, preferred_element_type=jnp.float32
    )
    grad_mixed = (
        jnp.stack([grad_query, grad_key, grad_value], axis=1)
        .reshape(tok_count, 3 * width)
        .astype(jnp.bfloat16)
    )
    grad_qkv = contract_first(normed_one, grad_mixed)
    grad_normed_one = contract_last(grad_mixed, w_qkv)
    grad_norm_one, grad_gain_one, grad_shift_one = norm_back(
        grad_normed_one, unit_one, inverse_one, gain_one
    )
    grad_tokens = grad_middle + grad_norm_one
    grad_qkv, grad_out, grad_gain_one, grad_shift_one, grad_gain_two, grad_shift_two = lax.psum(
        (grad_qkv, grad_out, grad_gain_one, grad_shift_one, grad_gain_two, grad_shift_two),
        ("exp", "hid"),
    )
    return (
        output,
        grad_tokens,
        grad_gain_one,
        grad_shift_one,
        grad_qkv,
        grad_out,
        grad_gain_two,
        grad_shift_two,
        grad_in,
        grad_bias_in,
        grad_back,
        grad_bias_back,
    )


def solution(mesh):
    placed = (
        P(("exp", "hid"), None),
        P(("exp", "hid")),
        P(("exp", "hid"), None),
        P(),
        P(),
        P(),
        P(),
        P(),
        P(),
        P(),
        P(),
        P("exp", None, "hid"),
        P("exp", "hid"),
        P("exp", "hid", None),
        P("exp", None),
        P(("exp", "hid"), None),
    )
    return jax.shard_map(
        per_device,
        mesh=mesh,
        in_specs=placed,
        out_specs=(
            P(("exp", "hid"), None),
            P(("exp", "hid"), None),
            P(),
            P(),
            P(),
            P(),
            P(),
            P(),
            P("exp", None, "hid"),
            P("exp", "hid"),
            P("exp", "hid", None),
            P("exp", None),
        ),
        check_vma=False,
    )
```

profile of v0, /device:TPU:0, one launch (start us, length us, event | category | flops | bytes accessed | tf_op | source)
XLA Modules:
  0.0 898.5 jit_solution(3650877973698361504)
XLA Ops:
  31.8 10.3 %select_reduce_fusion = (f32[16,512]{1,0:T(8,128)S(1)}, f32[16,512,512]{1,2,0:T(8,128)}) fusion(pred[512,512]{0,1:T(8,128)(4,1)S(1)} %fusion.105, bf16[512,3,16,64]{0,3,2,1:T(8,128)(2,1)} %bitcast.161), kind=kOutput, calls=%fused_computation.21 | convolution fusion | flops 549445632 | bytes 19169280 | tf_op jit(solution)/shard_map/qhd,khd->hqk/dot_general | solution.py:101
  42.2 9.2 %fusion.11 = f32[16,512]{1,0:T(8,128)S(1)} fusion(f32[16,512,512]{1,2,0:T(8,128)} %get-tuple-element.29, f32[16,512]{1,0:T(8,128)S(1)} %get-tuple-element.28, pred[512,512]{0,1:T(8,128)(4,1)S(1)} %fusion.105), kind=kLoop, calls=%fused_computation.22 | loop fusion | flops 16769024 | bytes 17104896 | tf_op jit(solution)/shard_map/reduce_sum | solution.py:106
  51.3 8.7 fusion.76
  63.5 55.4 %all_to_all.42 = bf16[8,128,1024]{2,1,0:T(8,128)(2,1)S(1)} all-to-all(bf16[8,128,1024]{2,1,0:T(8,128)(2,1)S(1)} %bitcast.179), channel_id=1, replica_groups=mesh['exp'=8,'hid'=4] {'exp'}, dimensions={0} | all-to-all | bytes 4194304 | tf_op jit(solution)/shard_map/all_to_all | solution.py:117
  121.8 51.4 %all_to_all.43 = bf16[8,128,1024]{2,1,0:T(8,128)(2,1)S(1)} all-to-all(bf16[8,128,1024]{2,1,0:T(8,128)(2,1)S(1)} %bitcast.180), channel_id=1, replica_groups=mesh['exp'=8,'hid'=4] {'exp'}, dimensions={0} | all-to-all | bytes 4194304 | tf_op jit(solution)/shard_map/all_to_all | solution.py:142
  177.9 17.4 %fusion.20 = f32[4,32,32,1024]{3,2,1,0:T(8,128)} fusion(bf16[32,4,32,1024]{3,2,0,1:T(8,128)(2,1)} %all-gather.3.cloned.1.call-done, bf16[4,1024,1024]{2,1,0:T(8,128)(2,1)} %param.27), kind=kOutput, calls=%fused_computation.30 | convolution fusion | flops 8589934592 | bytes 33554432 | tf_op jit(solution)/shard_map/necd,edf->necf/dot_general | solution.py:121
  195.3 43.0 %all-gather.5.cloned.1.call-done = bf16[32,4,32,1024]{3,2,0,1:T(8,128)(2,1)} async-done(((bf16[8,4,32,1024]{3,2,0,1:T(8,128)(2,1)}), bf16[32,4,32,1024]{3,2,0,1:T(8,128)(2,1)}) %all-gather.5.cloned.1.call-update) | async-done | bytes 8388624 | tf_op jit(solution)/shard_map/all_gather | solution.py:144
  238.4 21.6 %convert_reduce_fusion.1 = (f32[4,1024]{1,0:T(4,128)}, bf16[32,4,32,1024]{3,2,0,1:T(8,128)(2,1)}) fusion(f32[4,32,32,1024]{3,2,1,0:T(8,128)} %fusion.20, f32[4,1024]{1,0:T(4,128)S(1)} %copy-done.31, bf16[32,4,32,1024]{3,2,0,1:T(8,128)(2,1)} %all-gather.5.cloned.1.call-done, bf16[4,1024,1024]{2,1,0:T(8,128)(2,1)} %param.29), kind=kOutput, calls=%fused_computation.14 | convolution fusion | flops 8640262144 | bytes 41975808 | tf_op jit(solution)/shard_map/necd,efd->necf/dot_general | solution.py:155
  259.9 17.3 %convolution_bitcast_fusion = f32[32,4,32,1024]{3,2,0,1:T(8,128)} fusion(bf16[32,4,32,1024]{3,2,0,1:T(8,128)(2,1)} %get-tuple-element.35, bf16[4,1024,1024]{2,1,0:T(8,128)(2,1)} %param.27), kind=kOutput, calls=%fused_computation.26 | convolution fusion | flops 8589934592 | bytes 33554432 | tf_op jit(solution)/shard_map/necf,edf->necd/dot_general | solution.py:167
  283.8 11.8 %copy.93 = f32[4,8,128,1024]{3,1,2,0:T(8,128)} copy(f32[4,8,128,1024]{3,2,1,0:T(8,128)S(1)} %bitcast.158) | data formatting | bytes 33554432
  295.7 17.9 %convert_bitcast_fusion = bf16[32,4,32,1024]{3,2,0,1:T(8,128)(2,1)} fusion(bf16[4,1024,1024]{2,1,0:T(8,128)(2,1)} %param.29, f32[4,32,32,1024]{3,2,1,0:T(8,128)} %fusion.20, f32[4,1024]{1,0:T(4,128)S(1)} %copy-done.31), kind=kOutput, calls=%fused_computation.39 | convolution fusion | flops 8619294720 | bytes 33570816 | tf_op jit(solution)/shard_map/necf,efd->necd/dot_general | solution.py:127
  313.6 10.4 %copy.86 = bf16[32,4,32,1024]{3,2,1,0:T(8,128)(2,1)} copy(bf16[32,4,32,1024]{3,2,0,1:T(8,128)(2,1)} %convert_bitcast_fusion) | data formatting | bytes 16777216
  324.1 11.6 %copy.91 = bf16[4,8,128,1024]{3,1,2,0:T(8,128)(2,1)} copy(bf16[4,8,128,1024]{3,2,1,0:T(8,128)(2,1)} %bitcast.160) | data formatting | bytes 16777216
  335.7 86.2 %reduce-scatter.11.cloned.1.call-done = f32[8,131072]{1,0:T(8,128)} async-done(((f32[32,131072]{1,0:T(8,128)}), f32[8,131072]{1,0:T(8,128)}) %reduce-scatter.11.cloned.1.call-update) | async-done | bytes 4194320
  433.7 21.1 %convolution_bitcast_fusion.1 = f32[4,1024,1024]{2,1,0:T(8,128)} fusion(bf16[32,4,32,1024]{3,2,0,1:T(8,128)(2,1)} %all-gather.5.cloned.1.call-done, f32[4,32,32,1024]{3,2,1,0:T(8,128)} %fusion.20, f32[4,1024]{1,0:T(4,128)S(1)} %copy-done.31), kind=kOutput, calls=%fused_computation.27 | convolution fusion | flops 8615100416 | bytes 41959424 | tf_op jit(solution)/shard_map/necf,necd->efd/dot_general | solution.py:151
  460.8 36.1 %reduce-scatter.9.cloned.1.call-done = bf16[8,131072]{1,0:T(8,128)(2,1)} async-done(((bf16[32,131072]{1,0:T(8,128)(2,1)}), bf16[8,131072]{1,0:T(8,128)(2,1)}) %reduce-scatter.9.cloned.1.call-update) | async-done | bytes 2097168
  519.5 9.4 %fusion.110 = f32[16,512,512]{1,2,0:T(8,128)} fusion(bf16[512,16,64]{0,2,1:T(8,128)(2,1)S(1)} %bitcast.173, bf16[512,3,16,64]{0,3,2,1:T(8,128)(2,1)} %bitcast.163), kind=kOutput, calls=%fused_computation.109 | convolution fusion | flops 536870912 | bytes 18874368 | tf_op jit(solution)/shard_map/qhd,khd->hqk/dot_general | solution.py:192
  528.8 8.6 fusion.88
  537.5 24.6 %fusion.94 = bf16[512,1,16,64]{0,3,2,1:T(8,128)(2,1)} fusion(f32[16,512,512]{1,2,0:T(8,128)} %fusion.110, f32[16,512,512]{1,2,0:T(8,128)} %get-tuple-element.29, f32[16,512]{1,0:T(8,128)S(1)} %log_add_fusion, pred[512,512]{0,1:T(8,128)(4,1)S(1)} %copy-done.12, bf16[512,3,16,64]{0,3,2,1:T(8,128)(2,1)} %bitcast.164), kind=kOutput, calls=%fused_computation.91 | convolution fusion | flops 583541248 | bytes 69795840 | tf_op jit(solution)/shard_map/hqk,khd->qhd/dot_general | solution.py:197
  562.1 24.8 %fusion.91 = bf16[512,1,16,64]{0,3,2,1:T(8,128)(2,1)} fusion(f32[16,512,512]{1,2,0:T(8,128)} %fusion.110, f32[16,512,512]{1,2,0:T(8,128)} %get-tuple-element.29, f32[16,512]{1,0:T(8,128)S(1)} %log_add_fusion, pred[512,512]{0,1:T(8,128)(4,1)S(1)} %copy-done.12, bf16[512,3,16,64]{0,3,2,1:T(8,128)(2,1)} %bitcast.165), kind=kOutput, calls=%fused_computation.90 | convolution fusion | flops 583541248 | bytes 69795840 | tf_op jit(solution)/shard_map/hqk,qhd->khd/dot_general | solution.py:200
  597.9 17.3 %convolution_bitcast_fusion.2 = f32[4,1024,1024]{2,1,0:T(8,128)} fusion(bf16[32,4,32,1024]{3,2,0,1:T(8,128)(2,1)} %all-gather.3.cloned.1.call-done, bf16[32,4,32,1024]{3,2,0,1:T(8,128)(2,1)} %get-tuple-element.35), kind=kOutput, calls=%fused_computation.28 | convolution fusion | flops 8589934592 | bytes 33554432 | tf_op jit(solution)/shard_map/necd,necf->edf/dot_general | solution.py:161
  628.4 41.6 %all-reduce = (f32[1024]{0:T(1024)}, f32[1024]{0:T(1024)}, f32[1024]{0:T(1024)}, f32[1024]{0:T(1024)}) all-reduce(f32[1024]{0:T(1024)S(1)} %get-tuple-element.14, f32[1024]{0:T(1024)S(1)} %get-tuple-element.19, f32[1024]{0:T(1024)S(1)} %get-tuple-element.12, ...), channel_id=1, replica_groups=mesh['exp'=8,'hid'=4] {'exp','hid'}, use_global_device_ids=true, to_apply=%region_20.21 | all-reduce | flops 4096 | bytes 32768 | tf_op jit(solution)/shard_map/psum | solution.py:214
  674.3 204.2 %all-reduce.4.cloned.1.call-done = (f32[1024,3072]{1,0:T(8,128)}, f32[1024,1024]{1,0:T(8,128)}) async-done(((f32[1024,3072]{1,0:T(8,128)}, f32[1024,1024]{1,0:T(8,128)}), (f32[1024,3072]{1,0:T(8,128)}, f32[1024,1024]{1,0:T(8,128)})) %all-reduce.4.cloned.1.call-update) | async-done | bytes 16777232 | tf_op jit(solution)/shard_map/psum | solution.py:214
  878.5 11.1 %copy.98 = f32[1024,3072]{1,0:T(8,128)} copy(f32[1024,3072]{1,0:T(8,128)} %get-tuple-element.42) | data formatting | bytes 25165824
  (132 shorter events, 112.7 us)
Async XLA Ops:
  7.2 52.9 %copy-start = (bf16[1024,1024]{1,0:T(8,128)(2,1)S(1)}, bf16[1024,1024]{1,0:T(8,128)(2,1)}, u32[]{:S(2)}) copy-start(bf16[1024,1024]{1,0:T(8,128)(2,1)} %param.24) | copy-start | bytes 6291460
  7.2 170.7 %all-gather.3.cloned.1.call-start = ((), (), s32[]{:S(2)}) async-start(), calls=%async_computation.6 | async-start | bytes 10485760 | tf_op jit(solution)/shard_map/all_gather | solution.py:119
  14.6 12.6 %copy-start.15 = (f32[512]{0:T(512)}, f32[512]{0:T(512)S(1)}, u32[]{:S(2)}) copy-start(f32[512]{0:T(512)S(1)} %broadcast_multiply_fusion.5) | copy-start | bytes 6148
  16.2 10.9 %copy-start.20 = (f32[512]{0:T(512)}, f32[512]{0:T(512)S(1)}, u32[]{:S(2)}) copy-start(f32[512]{0:T(512)S(1)} %add_rsqrt_fusion.1) | copy-start | bytes 6148
  18.5 102.0 %copy-start.27 = (s32[512]{0:T(512)}, s32[512]{0:T(512)S(1)}, u32[]{:S(2)}) copy-start(s32[512]{0:T(512)S(1)} %multiply_add_fusion.1) | copy-start | bytes 6148
  18.5 102.0 %copy-start.29 = (pred[512]{0:T(512)(128)(4,1)}, pred[512]{0:T(512)(128)(4,1)S(1)}, u32[]{:S(2)}) copy-start(pred[512]{0:T(512)(128)(4,1)S(1)} %lt.17) | copy-start | bytes 1540
  18.7 32.6 %copy-start.11 = (pred[512,512]{0,1:T(8,128)(4,1)}, pred[512,512]{0,1:T(8,128)(4,1)S(1)}, u32[]{:S(2)}) copy-start(pred[512,512]{0,1:T(8,128)(4,1)S(1)} %fusion.105) | copy-start | bytes 786436
  61.5 57.4 %copy-start.1 = (f32[512,1024]{1,0:T(8,128)}, f32[512,1024]{1,0:T(8,128)S(1)}, u32[]{:S(2)}) copy-start(f32[512,1024]{1,0:T(8,128)S(1)} %get-tuple-element.31) | copy-start | bytes 6291460
  63.5 57.0 %copy-start.13 = (bf16[512,1024]{1,0:T(8,128)(2,1)S(1)}, bf16[512,1024]{1,0:T(8,128)(2,1)}, u32[]{:S(2)}) copy-start(bf16[512,1024]{1,0:T(8,128)(2,1)} %param.31) | copy-start | bytes 3145732
  120.4 117.9 %all-gather.5.cloned.1.call-start = ((), (), s32[]{:S(2)}) async-start(), calls=%async_computation.7 | async-start | bytes 10485760 | tf_op jit(solution)/shard_map/all_gather | solution.py:144
  174.7 63.7 %copy-start.31 = (f32[4,1024]{1,0:T(4,128)S(1)}, f32[4,1024]{1,0:T(4,128)}, u32[]{:S(2)}) copy-start(f32[4,1024]{1,0:T(4,128)} %param.28) | copy-start | bytes 49156
  174.7 247.3 %reduce-scatter.11.cloned.1.call-start = ((), (), s32[]{:S(2)}) async-start(), calls=%async_computation.9 | async-start | bytes 20971520
  295.7 201.2 %reduce-scatter.9.cloned.1.call-start = ((), (), s32[]{:S(2)}) async-start(), calls=%async_computation.8 | async-start | bytes 10485760
  427.7 73.9 %all-to-all-start.3 = ((bf16[8,128,1024]{2,1,0:T(8,128)(2,1)}), bf16[8,128,1024]{2,1,0:T(8,128)(2,1)}, u32[]{:S(2)}, u32[]{:S(2)}) async-start(bf16[8,128,1024]{2,1,0:T(8,128)(2,1)} %bitcast.166), calls=%async_computation.3 | async-start | bytes 4194304 | tf_op jit(solution)/shard_map/all_to_all | solution.py:173
  454.7 45.0 %copy-start.19 = (f32[4,1024]{1,0:T(4,128)S(1)}, f32[4,1024]{1,0:T(4,128)}, u32[]{:S(2)}) copy-start(f32[4,1024]{1,0:T(4,128)} %param.30) | copy-start | bytes 49156
  496.9 10.3 %copy-start.18 = (f32[512]{0:T(512)S(1)}, f32[512]{0:T(512)}, u32[]{:S(2)}) copy-start(f32[512]{0:T(512)} %copy-done.17) | copy-start | bytes 6148
  496.9 10.3 %copy-start.23 = (f32[512]{0:T(512)S(1)}, f32[512]{0:T(512)}, u32[]{:S(2)}) copy-start(f32[512]{0:T(512)} %copy-done.22) | copy-start | bytes 6148
  496.9 10.3 %copy-start.25 = (f32[1024]{0:T(1024)S(1)}, f32[1024]{0:T(1024)}, u32[]{:S(2)}) copy-start(f32[1024]{0:T(1024)} %param.25) | copy-start | bytes 12292
  496.9 10.3 %copy-start.28 = (s32[512]{0:T(512)S(1)}, s32[512]{0:T(512)}, u32[]{:S(2)}) copy-start(s32[512]{0:T(512)} %copy-done.27) | copy-start | bytes 6148
  496.9 10.3 %copy-start.30 = (pred[512]{0:T(512)(128)(4,1)S(1)}, pred[512]{0:T(512)(128)(4,1)}, u32[]{:S(2)}) copy-start(pred[512]{0:T(512)(128)(4,1)} %copy-done.29) | copy-start | bytes 1540
  501.6 113.6 %all-to-all-start.1 = ((bf16[8,128,1024]{2,1,0:T(8,128)(2,1)}), bf16[8,128,1024]{2,1,0:T(8,128)(2,1)}, u32[]{:S(2)}, u32[]{:S(2)}) async-start(bf16[8,128,1024]{2,1,0:T(8,128)(2,1)} %bitcast.167), calls=%async_computation.1 | async-start | bytes 4194304 | tf_op jit(solution)/shard_map/all_to_all | solution.py:135
  507.1 371.4 %all-reduce.4.cloned.1.call-start = ((), (), s32[]{:S(2)}) async-start(), calls=%async_computation.10 | async-start | bytes 33554432 | tf_op jit(solution)/shard_map/psum | solution.py:214
  519.5 9.4 %copy-start.12 = (pred[512,512]{0,1:T(8,128)(4,1)S(1)}, pred[512,512]{0,1:T(8,128)(4,1)}, u32[]{:S(2)}) copy-start(pred[512,512]{0,1:T(8,128)(4,1)} %copy-done.11) | copy-start | bytes 786436
  878.5 11.1 %copy-start.8 = (f32[1024,1024]{1,0:T(8,128)S(1)}, f32[1024,1024]{1,0:T(8,128)}, u32[]{:S(2)}) copy-start(f32[1024,1024]{1,0:T(8,128)} %get-tuple-element.43) | copy-start | bytes 12582916
  (17 other events, 59.2 us)
Sparse Core Ops, SparseCore 0:
  120.6 57.3 all-gather.2
  180.1 58.2 all-gather.4
  295.8 126.1 reduce-scatter.10
  425.1 71.7 reduce-scatter.8
  598.0 280.4 all-reduce.3
where the time goes:
time: 908 us; the launch traced here: 898 us
  waiting for transfers between devices  373 us (41%)
  matrix products  242 us (27%)
  blocking collectives  148 us (16%)
  local copies, waits for them, and re-layouts  76.8 us (8%)
  other arithmetic  32.5 us (4%)
  between operations  14.6 us (2%)
  starting transfers between devices  11.7 us (1%)
    psum x1, waiting for transfers between devices, per_device(): lax.psum((grad_qkv, grad_out, grad_gain_one, grad_shift_one, grad_gain_tw...  204 us
    unnamed x7, waiting for transfers between devices  122 us
    unnamed x76, local copies, waits for them, and re-layouts  63.9 us
    all_to_all x1, blocking collectives, per_device(): lax.all_to_all(send_rows, 'exp', split_axis=0, concat_axis=0, tiled=True)  55.4 us
    all_to_all x1, blocking collectives, per_device(): lax.all_to_all(grad_send, 'exp', split_axis=0, concat_axis=0, tiled=True)  51.4 us
    all_gather x1, waiting for transfers between devices, per_device(): grad_expert = lax.all_gather(grad_recv, 'hid', axis=0, tiled=True)  43 us
    psum x1, blocking collectives, per_device(): lax.psum((grad_qkv, grad_out, grad_gain_one, grad_shift_one, grad_gain_tw...  41.6 us
    dot_general x1, matrix products, per_device(): jnp.einsum('hqk,qhd->khd', grad_scores, query_rows, preferred_element_typ...  24.8 us
  transfers between devices with their start and end apart: 7, of which 5 were waited for; matrix products, arithmetic and copies ran while one was open for 25% of the time, Pallas kernels for 0%

commit v1 on v0

v1 whole, which is shorter than its diff:
```python
import functools

import jax
import jax.numpy as jnp
from jax import lax
from jax.experimental import pallas as pl
from jax.experimental.pallas import tpu as pltpu
from jax.sharding import PartitionSpec as P

HEADS = 16
MESH = pl.DeviceIdType.MESH
BF = jnp.bfloat16
F32 = jnp.float32
epsilon = 1e-05
masked_score = -1e30
DMA = pltpu.SemaphoreType.DMA
VM = pl.BlockSpec(memory_space=pltpu.VMEM)
SM = pl.BlockSpec(memory_space=pltpu.SMEM)
HB = pl.BlockSpec(memory_space=pl.ANY)
MIB = 1 << 20


def mm(a, b):
    return lax.dot_general(a, b, (((1,), (0,)), ((), ())), preferred_element_type=F32)


def mm_nt(a, b):
    return lax.dot_general(a, b, (((1,), (1,)), ((), ())), preferred_element_type=F32)


def mm_tn(a, b):
    return lax.dot_general(a, b, (((0,), (0,)), ((), ())), preferred_element_type=F32)


def place():
    e = lax.axis_index("exp")
    h = lax.axis_index("hid")
    return e, h, lax.div(h, 2), lax.rem(h, 2)


def rcopy(src, dst, send, recv, dev):
    return pltpu.make_async_remote_copy(
        src_ref=src, dst_ref=dst, send_sem=send, recv_sem=recv, device_id=dev, device_id_type=MESH
    )


def greet(n_exp, n_y):
    e, h, y, c = place()
    sem = pltpu.get_barrier_semaphore()
    for k in range(1, n_exp):
        pl.semaphore_signal(sem, inc=1, device_id=(e ^ k, h), device_id_type=MESH)
    for d in range(1, n_y):
        pl.semaphore_signal(
            sem, inc=1, device_id=(e, lax.rem(y + d, n_y) * 2 + c), device_id_type=MESH
        )
    pl.semaphore_signal(sem, inc=1, device_id=(e, y * 2 + 1 - c), device_id_type=MESH)
    pl.semaphore_wait(sem, n_exp - 1 + n_y)


class Spread:
    def __init__(self, n_exp, n_y, rows, land, sems):
        self.n_exp, self.n_y, self.rows, self.land = n_exp, n_y, rows, land
        self.es, self.er, self.ys, self.yr, self.cs, self.cr = sems
        self.e, self.h, self.y, self.c = place()

    @staticmethod
    def sems(n_exp, n_y):
        return [DMA((n_exp,)), DMA((n_exp,))] + [DMA((n_exp, n_y))] * 4

    def over_exp(self, k):
        return rcopy(
            self.rows.at[self.e ^ k], self.land.at[:, self.e, self.h],
            self.es.at[k], self.er.at[k], (self.e ^ k, self.h),
        )

    def block(self, k, hid):
        return self.land.at[:, self.e ^ k, hid]

    def over_y(self, k, d):
        blk = self.block(k, self.h)
        dev = (self.e, lax.rem(self.y + d, self.n_y) * 2 + self.c)
        return rcopy(blk, blk, self.ys.at[k, d], self.yr.at[k, d], dev)

    def over_core(self, k, d):
        blk = self.block(k, lax.rem(self.y + self.n_y - d, self.n_y) * 2 + self.c)
        dev = (self.e, self.y * 2 + 1 - self.c)
        return rcopy(blk, blk, self.cs.at[k, d], self.cr.at[k, d], dev)

    def pass_on(self, k):
        @pl.when(k > 0)
        def _():
            self.over_exp(k).wait_recv()

        for d in range(1, self.n_y):
            self.over_y(k, d).start()
        self.over_core(k, 0).start()

    def pass_y(self, k):
        for d in range(1, self.n_y):
            self.over_y(k, d).wait_recv()
            self.over_core(k, d).start()

    def landed(self, k):
        for d in range(self.n_y):
            self.over_core(k, d).wait_recv()

    def sent(self, k):
        @pl.when(k > 0)
        def _():
            self.over_exp(k).wait_send()

        for d in range(1, self.n_y):
            self.over_y(k, d).wait_send()
        for d in range(self.n_y):
            self.over_core(k, d).wait_send()


class Gather:
    def __init__(self, n_exp, n_y, other, mine, pairs, from_y, back, sems):
        self.n_exp, self.n_y, self.other, self.mine = n_exp, n_y, other, mine
        self.pairs, self.from_y, self.back = pairs, from_y, back
        self.es, self.er, self.ys, self.yr, self.cs, self.cr = sems
        self.e, self.h, self.y, self.c = place()

    @staticmethod
    def sems(n_exp, n_y):
        return [DMA((n_exp,)), DMA((n_exp,)), DMA((n_exp, n_y)), DMA((n_exp, n_y)), DMA((n_exp,)), DMA((n_exp,))]

    @staticmethod
    def scratch(n_exp, n_y, lc, cap, d):
        return [
            pltpu.VMEM((n_exp, lc, n_y, cap, d), BF),
            pltpu.VMEM((n_exp, n_y - 1, lc, cap, d), BF),
        ]

    def over_core(self, k):
        t = self.e ^ k
        dev = (self.e, self.y * 2 + 1 - self.c)
        return rcopy(self.other(k), self.pairs.at[t], self.cs.at[k], self.cr.at[k], dev)

    def over_y(self, k, d):
        t = self.e ^ k
        dev = (self.e, lax.rem(self.y + d, self.n_y) * 2 + self.c)
        yy = lax.rem(self.y + d, self.n_y)
        return rcopy(self.pairs.at[t, :, yy], self.from_y.at[t, d - 1], self.ys.at[k, d], self.yr.at[k, d], dev)

    def over_exp(self, k):
        t = self.e ^ k
        return rcopy(self.pairs.at[t, :, self.y], self.back.at[self.e], self.es.at[k], self.er.at[k], (t, self.h))

    def pair(self, k, yy):
        t = self.e ^ k
        return self.mine(k, yy).astype(F32) + self.pairs[t, :, yy].astype(F32)

    def step_core(self, k):
        self.over_core(k).start()

    def step_y(self, k):
        t = self.e ^ k
        self.over_core(k).wait_recv()
        for d in range(1, self.n_y):
            yy = lax.rem(self.y + d, self.n_y)
            self.pairs[t, :, yy] = self.pair(k, yy).astype(BF)
            self.over_y(k, d).start()

    def step_exp(self, k, extra=None):
        t = self.e ^ k
        total = self.pair(k, self.y)
        for d in range(1, self.n_y):
            self.over_y(k, d).wait_recv()
            total = total + self.from_y[t, d - 1].astype(F32)
        if extra is not None:
            total = total + extra
        total = total.astype(BF)

        @pl.when(k == 0)
        def _():
            self.back[t] = total

        @pl.when(k > 0)
        def _():
            self.pairs[t, :, self.y] = total
            self.over_exp(k).start()

    def finish(self, k):
        for d in range(1, self.n_y):
            self.over_y(k, d).wait_send()

        @pl.when(k > 0)
        def _():
            self.over_exp(k).wait_send()
            self.over_exp(k).wait_recv()


def norm_rows(rows, gain, shift):
    mean = jnp.mean(rows, axis=-1, keepdims=True)
    centred = rows - mean
    var = jnp.mean(centred * centred, axis=-1, keepdims=True)
    inverse = lax.rsqrt(var + epsilon)
    unit = centred * inverse
    return unit * gain + shift, unit, inverse


def norm_back(upstream, unit, inverse, gain):
    scaled = upstream * gain
    inner = (
        scaled
        - jnp.mean(scaled, axis=-1, keepdims=True)
        - unit * jnp.mean(scaled * unit, axis=-1, keepdims=True)
    )
    return inner * inverse


def slot_block(slot_row, first, count):
    tok = slot_row.shape[1]
    ids = lax.broadcasted_iota(jnp.int32, (count, tok), 0) + first
    return jnp.where(slot_row == ids, 1.0, 0.0).astype(BF)


def tok_block(slot_col, first, count):
    ids = lax.broadcasted_iota(jnp.int32, (slot_col.shape[0], count), 1) + first
    return jnp.where(slot_col == ids, 1.0, 0.0).astype(BF)


def doc_bias(lens, tok):
    q = lax.broadcasted_iota(jnp.int32, (tok, tok), 0)
    k = lax.broadcasted_iota(jnp.int32, (tok, tok), 1)
    dq = jnp.zeros((tok, tok), jnp.int32)
    dk = jnp.zeros((tok, tok), jnp.int32)
    end = 0
    for j in range(lens.shape[1]):
        end = end + lens[0, j]
        dq = dq + jnp.where(q >= end, 1, 0)
        dk = dk + jnp.where(k >= end, 1, 0)
    return jnp.where((dq == dk) & (q >= k), 0.0, masked_score)


def attend_kernel(
    n_exp, n_y, lens, slot_row, tokens, gain1, shift1, w_qkv, w_out, gain2, shift2, cot,
    mixed, context, middle, lse, send, land,
    cot_rows, normed, bias, own_sem, *sems,
):
    tok, width = tokens.shape
    e, h, y, c = place()
    lc, cap = send.shape[1], send.shape[2]
    per = lc * cap
    hd = width // HEADS
    spread = Spread(n_exp, n_y, cot_rows, land, sems)
    greet(n_exp, n_y)

    def pick(source, dst):
        rows = mm(slot_block(slot_row[...], dst * per, per), source)
        return rows.astype(BF).reshape(lc, cap, width)

    @pl.loop(1, n_exp)
    def _(k):
        cot_rows[e ^ k] = pick(cot[...], e ^ k)
        spread.over_exp(k).start()

    cot_rows[e] = pick(cot[...], e)
    own = pltpu.make_async_copy(cot_rows.at[e], land.at[:, e, h], own_sem)
    own.start()

    @pl.loop(0, tok // 128)
    def _(i):
        rows = pl.ds(i * 128, 128)
        out, _, _ = norm_rows(tokens[rows].astype(F32), gain1[...], shift1[...])
        normed[rows] = out.astype(BF)

    bias[...] = doc_bias(lens, tok)
    own.wait()

    @pl.loop(0, 3 * width // 512)
    def _(i):
        cols = pl.ds(pl.multiple_of(i * 512, 512), 512)
        mixed[:, cols] = mm(normed[...], w_qkv[:, cols]).astype(BF)

    lse[...] = jnp.zeros_like(lse)
    lane = lax.broadcasted_iota(jnp.int32, (1, 128), 1)
    n_pairs = width // 128
    steps = n_exp // n_pairs
    half = tok // 2
    heads_in = 128 // hd

    @pl.loop(0, n_pairs)
    def _(p):
        for j in range(steps):
            k = p * steps + j
            spread.pass_on(k)

            @pl.when(k > 0)
            def _():
                spread.pass_y(k - 1)

        def cols(part):
            return pl.ds(pl.multiple_of(part * width + p * 128, 128), 128)

        q, key, val = mixed[:, cols(0)], mixed[:, cols(1)], mixed[:, cols(2)]
        for blk in range(2):
            rows = slice(blk * half, (blk + 1) * half)
            n_keys = (blk + 1) * half
            total = jnp.zeros((half, 128), F32)
            lses = lse[rows, :]
            for hh in range(heads_in):
                own_lanes = (lane >= hh * hd) & (lane < (hh + 1) * hd)
                qh = jnp.where(own_lanes, q[rows] * BF(hd**-0.5), BF(0))
                vh = jnp.where(own_lanes, val[:n_keys], BF(0))
                s = mm_nt(qh, key[:n_keys]) + bias[rows, :n_keys]
                top = jnp.max(s, axis=-1, keepdims=True)
                ex = jnp.exp(s - top)
                tot = jnp.sum(ex, axis=-1, keepdims=True)
                probs = (ex * (1.0 / tot)).astype(BF)
                total = total + mm(probs, vh)
                lses = jnp.where(lane == p * heads_in + hh, top + jnp.log(tot), lses)
            lse[rows, :] = lses
            context[rows, pl.ds(pl.multiple_of(p * 128, 128), 128)] = total.astype(BF)

    spread.pass_y(n_exp - 1)

    @pl.loop(0, tok // 256)
    def _(i):
        rows = pl.ds(i * 256, 256)
        mid = tokens[rows].astype(F32) + mm(context[rows], w_out[...])
        middle[rows] = mid
        out, _, _ = norm_rows(mid, gain2[...], shift2[...])
        normed[rows] = out.astype(BF)

    @pl.loop(0, n_exp)
    def _(k):
        send[k] = pick(normed[...], k)

    @pl.loop(0, n_exp)
    def _(k):
        spread.landed(k)
        spread.sent(k)


def attend(n_exp, n_hid, lc, cap, lens, slot_row, tokens, gain1, shift1, w_qkv, w_out, gain2, shift2, cot):
    n_y = n_hid // 2
    tok, width = tokens.shape
    shape = jax.ShapeDtypeStruct
    return pl.pallas_call(
        functools.partial(attend_kernel, n_exp, n_y),
        name="attend",
        out_shape=(
            shape((tok, 3 * width), BF),
            shape((tok, width), BF),
            shape((tok, width), F32),
            shape((tok, 128), F32),
            shape((n_exp, lc, cap, width), BF),
            shape((lc, n_exp, n_hid, cap, width), BF),
        ),
        in_specs=[SM] + [VM] * 9,
        out_specs=[VM] * 6,
        scratch_shapes=[
            pltpu.VMEM((n_exp, lc, cap, width), BF),
            pltpu.VMEM((tok, width), BF),
            pltpu.VMEM((tok, tok), F32),
            DMA,
            *Spread.sems(n_exp, n_y),
        ],
        compiler_params=pltpu.CompilerParams(
            collective_id=0, has_side_effects=True, vmem_limit_bytes=56 * MIB
        ),
    )(lens, slot_row, tokens, gain1, shift1, w_qkv, w_out, gain2, shift2, cot)


def expert_kernel(
    n_exp, n_y, rows, grads, w_in, bias_in, w_back,
    back, x_out, h_out, gp_out, f_out, gb_in, gb_back,
    land, part, win_v, wback_v, g_v, h_v, gp_v, f_v,
    w_sem, g_sem, o_sem, x_sem, own_sem, *rest,
):
    e, h, y, c = place()
    n_gather = len(Gather.scratch(1, 2, 1, 1, 1))
    n_spread = len(Spread.sems(1, 1))
    scr, sp_sems, ga_sems = rest[:n_gather], rest[n_gather : n_gather + n_spread], rest[n_gather + n_spread :]
    spread = Spread(n_exp, n_y, rows, land, sp_sems)


    def part_of(k):
        return part.at[lax.rem(lax.div(k, 2), 2), :, lax.rem(e ^ k, 2)]

    gather = Gather(
        n_exp, n_y, lambda k: part_of(k).at[:, :, 1 - c], lambda k, yy: part_of(k)[:, yy, c],
        *scr, back, ga_sems,
    )
    n_hid = 2 * n_y
    lc, cap, width = rows.shape[1:]
    ff = w_in.shape[2]
    count = 2 * n_hid * cap
    n_chunks = n_exp // 2
    step_f = min(512, ff)

    def weights(ex):
        return (
            pltpu.make_async_copy(w_in.at[ex], win_v.at[ex], w_sem.at[0, ex]),
            pltpu.make_async_copy(w_back.at[ex], wback_v.at[ex], w_sem.at[1, ex]),
        )

    for ex in range(lc):
        for cp in weights(ex):
            cp.start()

    def base_of(i):
        t = e ^ (2 * lax.div(i, lc))
        return t - lax.rem(t, 2)

    def g_copy(i):
        src = grads.at[lax.rem(i, lc), pl.ds(base_of(i), 2)]
        return pltpu.make_async_copy(src, g_v.at[lax.rem(i, 2)], g_sem.at[lax.rem(i, 2)])

    def out_copies(i):
        ex, slot, to = lax.rem(i, lc), lax.rem(i, 2), pl.ds(base_of(i), 2)
        return (
            pltpu.make_async_copy(h_v.at[slot], h_out.at[ex, to], o_sem.at[0, slot]),
            pltpu.make_async_copy(gp_v.at[slot], gp_out.at[ex, to], o_sem.at[1, slot]),
            pltpu.make_async_copy(f_v.at[slot], f_out.at[ex, to], o_sem.at[2, slot]),
        )

    def x_copy(i):
        ex, to = lax.rem(i, lc), pl.ds(base_of(i), 2)
        return pltpu.make_async_copy(land.at[ex, to], x_out.at[ex, to], x_sem.at[i])

    g_copy(0).start()
    own = pltpu.make_async_copy(rows.at[e], land.at[:, e, h], own_sem)
    own.start()
    greet(n_exp, n_y)

    @pl.loop(1, n_exp)
    def _(k):
        spread.over_exp(k).start()

    gb_in[...] = jnp.zeros_like(gb_in)
    gb_back[...] = jnp.zeros_like(gb_back)
    own.wait()
    spread.pass_on(0)
    spread.pass_on(1)
    spread.pass_y(0)
    spread.pass_y(1)

    n_steps = n_chunks * lc

    @pl.loop(0, n_steps)
    def _(i):
        j, ex = lax.div(i, lc), lax.rem(i, lc)
        slot = lax.rem(i, 2)
        base = base_of(i)

        @pl.when(i + 1 < n_steps)
        def _():
            g_copy(i + 1).start()

        @pl.when(ex == 0)
        def _():
            spread.landed(2 * j)
            spread.landed(2 * j + 1)

            @pl.when(j >= 2)
            def _():
                gather.over_core(2 * j - 4).wait_send()
                gather.over_core(2 * j - 3).wait_send()

        @pl.when(j == 0)
        def _():
            for cp in weights(ex):
                cp.wait()

        x_copy(i).start()
        g_copy(i).wait()

        @pl.when(i >= 2)
        def _():
            for cp in out_copies(i - 2):
                cp.wait()

        x = land[ex, pl.ds(base, 2)].reshape(count, width)
        g = g_v[slot].reshape(count, width)
        gb_back[ex] += jnp.sum(g.astype(F32), axis=0, keepdims=True)
        hs, gps = [], []
        for f in range(ff // step_f):
            cols = slice(f * step_f, (f + 1) * step_f)
            pre = mm(x, win_v[ex, :, cols]) + bias_in[ex, :, cols]
            sig = jax.nn.sigmoid(pre)
            hid = (pre * sig).astype(BF)
            gh = mm_nt(g, wback_v[ex, cols, :])
            gp = (gh * sig * (1.0 + pre * (1.0 - sig))).astype(BF)
            gb_in[ex, :, cols] += jnp.sum(gp.astype(F32), axis=0, keepdims=True)
            h_v[slot, :, :, cols] = hid.reshape(2, n_hid * cap, step_f)
            gp_v[slot, :, :, cols] = gp.reshape(2, n_hid * cap, step_f)
        gpv = gp_v[slot].reshape(count, ff)
        gd = mm_nt(gpv, win_v[ex])
        part[lax.rem(j, 2), ex] = gd.astype(BF).reshape(2, n_y, 2, cap, width)
        hv = h_v[slot].reshape(count, ff)
        f_v[slot] = mm(hv, wback_v[ex]).astype(BF).reshape(2, n_y, 2, cap, width)
        for cp in out_copies(i):
            cp.start()

        @pl.when(j + 1 < n_chunks)
        def _():
            @pl.when(ex == 0)
            def _():
                spread.pass_on(2 * j + 2)

            @pl.when(ex == 1)
            def _():
                spread.pass_y(2 * j + 2)
                spread.pass_on(2 * j + 3)

            @pl.when(ex == 2)
            def _():
                spread.pass_y(2 * j + 3)

        @pl.when(j > 0)
        def _():
            @pl.when(ex == 0)
            def _():
                gather.step_y(2 * j - 2)
                gather.step_y(2 * j - 1)

            @pl.when(ex == lc - 1)
            def _():
                gather.step_exp(2 * j - 2)
                gather.step_exp(2 * j - 1)

        @pl.when(ex == lc - 1)
        def _():
            gather.step_core(2 * j)
            gather.step_core(2 * j + 1)

    gather.step_y(n_exp - 2)
    gather.step_y(n_exp - 1)
    gather.step_exp(n_exp - 2)
    gather.step_exp(n_exp - 1)

    for k in range(n_exp - 4, n_exp):
        gather.over_core(k).wait_send()
    for i in (n_steps - 2, n_steps - 1):
        for cp in out_copies(i):
            cp.wait()

    @pl.loop(0, n_steps)
    def _(i):
        x_copy(i).wait()

    @pl.loop(0, n_exp)
    def _(k):
        spread.sent(k)
        gather.finish(k)


def experts(n_exp, n_hid, rows, grads, w_in, bias_in, w_back):
    n_y = n_hid // 2
    _, lc, cap, width = rows.shape
    ff = w_in.shape[2]
    shape = jax.ShapeDtypeStruct
    per = n_hid * cap
    n_steps = n_exp // 2 * lc
    return pl.pallas_call(
        functools.partial(expert_kernel, n_exp, n_y),
        name="experts",
        out_shape=(
            shape((n_exp, lc, cap, width), BF),
            shape((lc, n_exp, n_hid, cap, width), BF),
            shape((lc, n_exp, per, ff), BF),
            shape((lc, n_exp, per, ff), BF),
            shape((lc, n_exp, n_y, 2, cap, width), BF),
            shape((lc, 1, ff), F32),
            shape((lc, 1, width), F32),
        ),
        in_specs=[VM, HB, HB, VM, HB],
        out_specs=[VM, HB, HB, HB, HB, VM, VM],
        scratch_shapes=[
            pltpu.VMEM((lc, n_exp, n_hid, cap, width), BF),
            pltpu.VMEM((2, lc, 2, n_y, 2, cap, width), BF),
            pltpu.VMEM(w_in.shape, BF),
            pltpu.VMEM(w_back.shape, BF),
            pltpu.VMEM((2, 2, n_hid, cap, width), BF),
            pltpu.VMEM((2, 2, per, ff), BF),
            pltpu.VMEM((2, 2, per, ff), BF),
            pltpu.VMEM((2, 2, n_y, 2, cap, width), BF),
            DMA((2, lc)), DMA((2,)), DMA((3, 2)), DMA((n_steps,)), DMA,
            *Gather.scratch(n_exp, n_y, lc, cap, width),
            *Spread.sems(n_exp, n_y),
            *Gather.sems(n_exp, n_y),
        ],
        compiler_params=pltpu.CompilerParams(
            collective_id=1, has_side_effects=True, vmem_limit_bytes=62 * MIB
        ),
    )(rows, grads, w_in, bias_in, w_back)


def wgrad_kernel(x, gp, h, g, g_in, g_back):
    g_in[0] = mm_tn(x[0], gp[0])
    g_back[0] = mm_tn(h[0], g[0])


def wgrad(x, gp, h, g):
    lc, n, width = x.shape
    ff = gp.shape[2]
    cut = 2
    shape = jax.ShapeDtypeStruct
    return pl.pallas_call(
        wgrad_kernel,
        name="wgrad",
        grid=(lc, cut),
        out_shape=(shape((lc, width, ff), F32), shape((lc, ff, width), F32)),
        in_specs=[
            pl.BlockSpec((1, n, width), lambda i, j: (i, 0, 0)),
            pl.BlockSpec((1, n, ff // cut), lambda i, j: (i, 0, j)),
            pl.BlockSpec((1, n, ff), lambda i, j: (i, 0, 0)),
            pl.BlockSpec((1, n, width // cut), lambda i, j: (i, 0, j)),
        ],
        out_specs=[
            pl.BlockSpec((1, width, ff // cut), lambda i, j: (i, 0, j)),
            pl.BlockSpec((1, ff, width // cut), lambda i, j: (i, 0, j)),
        ],
        compiler_params=pltpu.CompilerParams(vmem_limit_bytes=56 * MIB),
    )(x, gp, h, g)


def attend_back_kernel(
    n_exp, n_y, lens, slot_col, tokens, middle, cot, mixed, context, lse, back,
    gain1, shift1, w_qkv, w_out, gain2, bias_back, f_part,
    output, g_tokens, g_mats, g_norms,
    bias, gm, gattn, gctx, gmixed, n1t, lse_t, mine_v, f_back, mine_sem, *rest,
):
    tok, width = tokens.shape
    hd = width // HEADS
    e, h, y, c = place()
    n_gather = len(Gather.scratch(1, 2, 1, 1, 1))
    lc, cap = f_back.shape[1:3]
    gather = Gather(
        n_exp, n_y, lambda k: f_part.at[:, e ^ k, :, 1 - c], lambda k, yy: mine_v[lax.rem(k, 4), :, yy],
        *rest[:n_gather], f_back, rest[n_gather:],
    )

    def fetch(k):
        slot = lax.rem(k, 4)
        return pltpu.make_async_copy(f_part.at[:, e ^ k, :, c], mine_v.at[slot], mine_sem.at[slot])

    for k in range(3):
        fetch(k).start()
    greet(n_exp, n_y)

    @pl.loop(0, n_exp)
    def _(k):
        gather.step_core(k)

    g_norms[...] = jnp.zeros_like(g_norms)
    n_slots = n_exp * lc * cap

    def fold(values):
        return jnp.sum(values, axis=0, keepdims=True)

    @pl.loop(0, tok // 256)
    def _(i):
        rows = pl.ds(pl.multiple_of(i * 256, 256), 256)
        table = tok_block(slot_col[rows], 0, n_slots)
        up = mm(table, back[...].reshape(n_slots, width))
        _, unit, inverse = norm_rows(middle[rows], gain2[...], 0.0)
        g_norms[2:3] += fold(up * unit)
        g_norms[3:4] += fold(up)
        g_mid = cot[rows].astype(F32) + norm_back(up, unit, inverse, gain2[...])
        gm[rows] = g_mid
        gattn[rows] = g_mid.astype(BF)
        gctx[rows] = mm_nt(gattn[rows], w_out[...]).astype(BF)
        out, _, _ = norm_rows(tokens[rows].astype(F32), gain1[...], shift1[...])
        n1t[:, rows] = out.astype(BF).T

    def step_y(k):
        fetch(k).wait()
        gather.step_y(k)

    step_y(0)
    step_y(1)

    @pl.loop(0, width // 256)
    def _(i):
        cols = pl.ds(pl.multiple_of(i * 256, 256), 256)
        part = mm_tn(context[:, cols], gattn[...]).astype(BF)
        g_mats[3, pl.ds(i * 16, 16)] = part.reshape(16, 16, width)

    key_i = lax.broadcasted_iota(jnp.int32, (tok, tok), 0)
    qry_i = lax.broadcasted_iota(jnp.int32, (tok, tok), 1)
    dk_, dq_ = jnp.zeros((tok, tok), jnp.int32), jnp.zeros((tok, tok), jnp.int32)
    end = 0
    for j in range(lens.shape[1]):
        end = end + lens[0, j]
        dk_ = dk_ + jnp.where(key_i >= end, 1, 0)
        dq_ = dq_ + jnp.where(qry_i >= end, 1, 0)
    bias[...] = jnp.where((dk_ == dq_) & (qry_i >= key_i), 0.0, masked_score)
    lse_t[...] = lse[...].T

    lane = lax.broadcasted_iota(jnp.int32, (1, 128), 1)
    n_pairs = width // 128
    steps = n_exp // n_pairs
    half = tok // 2
    heads_in = 128 // hd

    @pl.loop(0, n_pairs)
    def _(p):
        for j in range(steps):
            k = p * steps + j

            @pl.when(k + 3 < n_exp)
            def _():
                fetch(k + 3).start()

            @pl.when(k + 2 < n_exp)
            def _():
                step_y(k + 2)

            gather.step_exp(k, bias_back[...])

        def cols(part):
            return pl.ds(pl.multiple_of(part * width + p * 128, 128), 128)

        q, key, val, do = mixed[:, cols(0)], mixed[:, cols(1)], mixed[:, cols(2)], gctx[:, cols(0)]
        dq = [jnp.zeros((half, 128), F32) for _ in range(2)]
        dkey = [jnp.zeros((half, 128), F32) for _ in range(2)]
        dval = [jnp.zeros((half, 128), F32) for _ in range(2)]
        for hh in range(heads_in):
            own_lanes = (lane >= hh * hd) & (lane < (hh + 1) * hd)
            qh = jnp.where(own_lanes, q * BF(hd**-0.5), BF(0))
            kh = jnp.where(own_lanes, key * BF(hd**-0.5), BF(0))
            doh = jnp.where(own_lanes, do, BF(0))
            lrow = lse_t[pl.ds(p * heads_in + hh, 1), :]
            for qb in range(2):
                rows = slice(qb * half, (qb + 1) * half)
                n = (qb + 1) * half
                s = mm_nt(key[:n], qh[rows]) + (bias[:n, rows] - lrow[:, rows])
                pt = jnp.exp(s)
                dp = mm_nt(val[:n], doh[rows])
                inner = jnp.sum(dp * pt, axis=0, keepdims=True)
                ds = (pt * (dp - inner)).astype(BF)
                ptb = pt.astype(BF)
                dv_, dk2 = mm(ptb, doh[rows]), mm(ds, qh[rows])
                for kb in range(qb + 1):
                    part = slice(kb * half, (kb + 1) * half)
                    dval[kb] = dval[kb] + dv_[part]
                    dkey[kb] = dkey[kb] + dk2[part]
                dq[qb] = dq[qb] + mm_tn(ds, kh[:n])
        for b in range(2):
            rows = slice(b * half, (b + 1) * half)
            gmixed[rows, cols(0)] = dq[b].astype(BF)
            gmixed[rows, cols(1)] = dkey[b].astype(BF)
            gmixed[rows, cols(2)] = dval[b].astype(BF)

    @pl.loop(0, tok // 256)
    def _(i):
        rows = pl.ds(pl.multiple_of(i * 256, 256), 256)
        up = mm_nt(gmixed[rows], w_qkv[...])
        _, unit, inverse = norm_rows(tokens[rows].astype(F32), gain1[...], 0.0)
        g_norms[0:1] += fold(up * unit)
        g_norms[1:2] += fold(up)
        g_tokens[rows] = gm[rows] + norm_back(up, unit, inverse, gain1[...])

    for part in range(3):

        @pl.loop(0, width // 256)
        def _(i):
            rows = pl.ds(pl.multiple_of(i * 256, 256), 256)
            piece = mm(n1t[rows], gmixed[:, part * width : (part + 1) * width])
            g_mats[part, pl.ds(i * 16, 16)] = piece.astype(BF).reshape(16, 16, width)

    @pl.loop(0, n_exp)
    def _(k):
        gather.over_core(k).wait_send()
        gather.finish(k)

    @pl.loop(0, tok // 256)
    def _(i):
        rows = pl.ds(pl.multiple_of(i * 256, 256), 256)
        table = tok_block(slot_col[rows], 0, n_slots)
        output[rows] = (middle[rows] + mm(table, f_back[...].reshape(n_slots, width))).astype(BF)


def attend_back(
    n_exp, n_hid, lens, slot_col, tokens, middle, cot, mixed, context, lse, back,
    gain1, shift1, w_qkv, w_out, gain2, bias_back, f_part,
):
    n_y = n_hid // 2
    tok, width = tokens.shape
    _, lc, cap, _ = back.shape
    shape = jax.ShapeDtypeStruct
    return pl.pallas_call(
        functools.partial(attend_back_kernel, n_exp, n_y),
        name="attend_back",
        out_shape=(
            shape((tok, width), BF),
            shape((tok, width), F32),
            shape((4, width // 16, 16, width), BF),
            shape((8, width), F32),
        ),
        in_specs=[SM] + [VM] * 14 + [HB],
        out_specs=[VM] * 4,
        scratch_shapes=[
            pltpu.VMEM((tok, tok), F32),
            pltpu.VMEM((tok, width), F32),
            pltpu.VMEM((tok, width), BF),
            pltpu.VMEM((tok, width), BF),
            pltpu.VMEM((tok, 3 * width), BF),
            pltpu.VMEM((width, tok), BF),
            pltpu.VMEM((128, tok), F32),
            pltpu.VMEM((4, lc, n_y, cap, width), BF),
            pltpu.VMEM((n_exp, lc, cap, width), BF),
            DMA((4,)),
            *Gather.scratch(n_exp, n_y, lc, cap, width),
            *Gather.sems(n_exp, n_y),
        ],
        compiler_params=pltpu.CompilerParams(
            collective_id=2, has_side_effects=True, vmem_limit_bytes=62 * MIB
        ),
    )(
        lens, slot_col, tokens, middle, cot, mixed, context, lse, back,
        gain1, shift1, w_qkv, w_out, gain2, bias_back, f_part,
    )


def reduce_all(n_exp, n_hid, mats, norms):
    return lax.psum(mats, ("exp", "hid")), lax.psum(norms, ("exp", "hid"))


def token_slots(token_ids, hash_table, capacity, cap):
    chosen = jnp.take(hash_table, token_ids, mode="clip")
    places = jnp.arange(chosen.shape[0], dtype=jnp.int32)
    earlier = (chosen[:, None] == chosen[None, :]) & (places[:, None] > places[None, :])
    rank = jnp.sum(earlier.astype(jnp.int32), axis=1)
    experts_ids = jnp.arange(capacity.shape[0], dtype=jnp.int32)
    limit = jnp.sum(jnp.where(chosen[:, None] == experts_ids[None, :], capacity[None, :], 0), axis=1)
    return jnp.where(rank < limit, chosen * cap + rank, -1)


def per_device(
    tokens, token_ids, lengths, hash_table, capacity, gain_one, shift_one, w_qkv, w_out,
    gain_two, shift_two, w_in, bias_in, w_back, bias_back, cotangent,
):
    n_exp, n_hid = lax.axis_size("exp"), lax.axis_size("hid")
    tok, width = tokens.shape
    lc, _, ff = w_in.shape
    cap = 2 * tok // capacity.shape[0]
    slot = token_slots(token_ids, hash_table, capacity, cap)
    gain1, shift1, gain2, shift2 = (v[None] for v in (gain_one, shift_one, gain_two, shift_two))
    mixed, context, middle, lse, send, grads = attend(
        n_exp, n_hid, lc, cap, lengths, slot[None], tokens, gain1, shift1, w_qkv, w_out, gain2, shift2, cotangent
    )
    back, x, hid, gp, f_part, gb_in, gb_back = experts(
        n_exp, n_hid, send, grads, w_in, bias_in[:, None], w_back
    )
    output, g_tokens, mats, norms = attend_back(
        n_exp, n_hid, lengths, slot[:, None], tokens, middle, cotangent, mixed, context, lse, back,
        gain1, shift1, w_qkv, w_out, gain2, bias_back[:, None], f_part,
    )
    mats, norms = reduce_all(n_exp, n_hid, mats, norms)
    n_rows = n_exp * n_hid * cap
    g_in, g_back = wgrad(
        x.reshape(lc, n_rows, width), gp.reshape(lc, n_rows, ff),
        hid.reshape(lc, n_rows, ff), grads.reshape(lc, n_rows, width),
    )
    mats = mats.reshape(4, width, width).astype(F32)
    g_qkv = jnp.concatenate([mats[0], mats[1], mats[2]], axis=1)
    return (
        output, g_tokens, norms[0], norms[1], g_qkv, mats[3], norms[2], norms[3],
        g_in, gb_in[:, 0], g_back, gb_back[:, 0],
    )


def solution(mesh):
    both = P(("exp", "hid"))
    rows = P(("exp", "hid"), None)
    placed = (
        rows, both, rows, P(), P(), P(), P(), P(), P(), P(), P(),
        P("exp", None, "hid"), P("exp", "hid"), P("exp", "hid", None), P("exp", None), rows,
    )
    return jax.shard_map(
        per_device,
        mesh=mesh,
        in_specs=placed,
        out_specs=(
            rows, rows, P(), P(), P(), P(), P(), P(),
            P("exp", None, "hid"), P("exp", "hid"), P("exp", "hid", None), P("exp", None),
        ),
        check_vma=False,
    )
```

time: 908 us -> 549 us (0.60)
  Pallas kernels: 0 us -> 350 us
  waiting for transfers between devices: 373 us -> 105 us
  matrix products: 242 us -> 0 us
  blocking collectives: 148 us -> 49.1 us
  local copies, waits for them, and re-layouts: 76.8 us -> 19.1 us
  other arithmetic: 32.5 us -> 11.2 us
  starting transfers between devices: 11.7 us -> 0.04 us
    pallas_call x0 -> x4, Pallas kernels: none -> 350 us  [the longest x1 145 us: experts(): pl.pallas_call(functools.partial(expert_kernel, n_exp, n_y), name='expert...]
    dot_general x22 -> x0, matrix products: 242 us -> none  [the longest x1 24.8 us: per_device(): jnp.einsum('hqk,qhd->khd', grad_scores, query_rows, preferred_element_typ...]
    unnamed x7 -> x1, waiting for transfers between devices: 122 us -> 0.02 us
    all_to_all x2 -> x0, blocking collectives: 107 us -> none  [the longest x1 55.4 us: per_device(): lax.all_to_all(send_rows, 'exp', split_axis=0, concat_axis=0, tiled=True)]
    psum x1, waiting for transfers between devices: 204 us -> 105 us  [reduce_all(): return (lax.psum(mats, ('exp', 'hid')), lax.psum(norms, ('exp', 'hid')))]
    unnamed x76 -> x19, local copies, waits for them, and re-layouts: 63.9 us -> 2.96 us
    all_gather x2 -> x0, waiting for transfers between devices: 46.2 us -> none  [the longest x1 43 us: per_device(): grad_expert = lax.all_gather(grad_recv, 'hid', axis=0, tiled=True)]
    reduce_sum x7 -> x2, other arithmetic: 19.5 us -> 1 us  [the longest x1 0.75 us: token_slots(): jnp.sum(jnp.where(chosen[:, None] == experts_ids[None, :], capacity[None,...]
  transfers between devices with their start and end apart: 7 -> 1, of which waited for: 5 -> 1; matrix products, arithmetic and copies ran while one was open for 25% -> 0% of each run, Pallas kernels for 0% -> 6%
where the time goes in v1:
time: 549 us; the launch traced here: 548 us
  Pallas kernels  350 us (64%)
  waiting for transfers between devices  105 us (19%)
  blocking collectives  49.1 us (9%)
  local copies, waits for them, and re-layouts  19.1 us (3%)
  between operations  14.1 us (3%)
  other arithmetic  11.2 us (2%)
    pallas_call x1, Pallas kernels, experts(): pl.pallas_call(functools.partial(expert_kernel, n_exp, n_y), name='expert...  145 us
    psum x1, waiting for transfers between devices, reduce_all(): return (lax.psum(mats, ('exp', 'hid')), lax.psum(norms, ('exp', 'hid')))  105 us
    pallas_call x1, Pallas kernels, attend_back(): pl.pallas_call(functools.partial(attend_back_kernel, n_exp, n_y), name='a...  97.4 us
    pallas_call x1, Pallas kernels, attend(): pl.pallas_call(functools.partial(attend_kernel, n_exp, n_y), name='attend...  76.2 us
    psum x1, blocking collectives, reduce_all(): return (lax.psum(mats, ('exp', 'hid')), lax.psum(norms, ('exp', 'hid')))  49.1 us
    pallas_call x1, Pallas kernels, wgrad(): pl.pallas_call(wgrad_kernel, name='wgrad', grid=(lc, cut), out_shape=(sha...  31.4 us
  transfers between devices with their start and end apart: 1, of which 1 were waited for; matrix products, arithmetic and copies ran while one was open for 0% of the time, Pallas kernels for 6%

profile of v1, /device:TPU:0, one launch (start us, length us, event | category | flops | bytes accessed | tf_op | source)
XLA Modules:
  0.0 548.5 jit_solution(13623802431326410113)
XLA Ops:
  7.2 0.0 copy-start
  7.2 0.0 all-reduce.2.cloned.1.call-start
  7.2 0.7 pad_clamp_fusion
  7.9 0.0 copy-done
  7.9 3.1 gather_fusion
  11.1 0.2 convert_reduce_fusion
  11.3 0.7 select_reduce_fusion
  12.1 1.3 broadcast_in_dim.55.bias_in
  13.4 0.9 copy.29.slot_col
  14.3 1.3 broadcast_in_dim.56.bias_back
  15.6 76.2 %attend.1 = (bf16[512,3072]{1,0:T(8,128)(2,1)}, bf16[512,1024]{1,0:T(8,128)(2,1)}, f32[512,1024]{1,0:T(8,128)}, f32[512,128]{1,0:T(8,128)}, bf16[8,4,32,1024]{3,...) custom-call(s32[1,2]{1,0:T(1,128)} %lens.3, s32[1,512]{1,0:T(1,128)} %bitcast.31, bf16[512,1024]{1,0:T(8,128)(2,1)} %tokens.3, ...), custom_call_target="tpu_custom_call" | custom-call | tf_op jit(solution)/shard_map/attend/pallas_call | solution.py:342
  91.8 145.4 %experts.1 = (bf16[8,4,32,1024]{3,2,1,0:T(8,128)(2,1)}, bf16[4,8,4,32,1024]{4,3,2,1,0:T(8,128)(2,1)}, bf16[4,8,128,1024]{3,2,1,0:T(8,128)(2,1)}, bf16[4,8,128,10...) custom-call(bf16[8,4,32,1024]{3,2,1,0:T(8,128)(2,1)} %get-tuple-elem, ...), custom_call_target="tpu_custom_call" | custom-call | tf_op jit(solution)/shard_map/experts/pallas_call | solution.py:559
  237.2 97.4 %attend_back.1 = (bf16[512,1024]{1,0:T(8,128)(2,1)}, f32[512,1024]{1,0:T(8,128)}, bf16[4,64,16,1024]{3,2,1,0:T(8,128)(2,1)}, f32[8,1024]{1,0:T(8,128)}) custom-call(s32[1,2]{1,0:T(1,128)} %lens.3, s32[512,1]{1,0:T(8,128)} %copy.29.slot_col, bf16[512,1024]{1,0:T(8,128)(2,1)} %tokens.3, f32[512,1024]{1,0:T(8,128)} %get-tuple-element.31.middle, ...), custom_call_target="tpu_custom_call" | custom-call | tf_op jit(solution)/shard_map/attend_back/pallas_call | solution.py:787
  334.6 0.0 all-reduce.2.cloned.1.call-update
  334.6 31.4 %wgrad.1 = (f32[4,1024,1024]{2,1,0:T(8,128)}, f32[4,1024,1024]{2,1,0:T(8,128)}) custom-call(bf16[4,1024,1024]{2,1,0:T(8,128)(2,1)} %bitcast.26, bf16[4,1024,1024]{2,1,0:T(8,128)(2,1)} %bitcast.28, bf16[4,1024,1024]{2,1,0:T(8,128)(2,1)} %bitcast.27, bf16[4,1024,1024]{2,1,0:T(8,128)(2,1)} %bitcast.22), custom_call_target="tpu_custom_call" | custom-call | tf_op jit(solution)/shard_map/wgrad/pallas_call | solution.py:603
  366.0 0.0 copy-done.4
  366.1 49.1 %psum.14 = f32[8,1024]{1,0:T(8,128)S(1)} all-reduce(f32[8,1024]{1,0:T(8,128)S(1)} %copy-done.4), channel_id=1, replica_groups=mesh['exp'=8,'hid'=4] {'exp','hid'}, use_global_device_ids=true, to_apply=%region_2.3 | all-reduce | flops 8192 | bytes 65536 | tf_op jit(solution)/shard_map/psum | solution.py:822
  415.1 0.6 fusion.2
  415.8 0.6 copy_bitcast_fusion
  416.4 104.5 %all-reduce.2.cloned.1.call-done = bf16[4,64,16,1024]{3,2,1,0:T(8,128)(2,1)} async-done(((bf16[4,64,16,1024]{3,2,1,0:T(8,128)(2,1)}), bf16[4,64,16,1024]{3,2,1,0:T(8,128)(2,1)}) %all-reduce.2.cloned.1.call-update) | async-done | bytes 8388624 | tf_op jit(solution)/shard_map/psum | solution.py:822
  520.9 8.9 %fusion.1 = (f32[1,64,16,1024]{3,2,1,0:T(8,128)}, f32[1,64,16,1024]{3,2,1,0:T(8,128)S(1)}, f32[1,64,16,1024]{3,2,1,0:T(8,128)}, f32[1,64,16,1024]{3,2,1,0:T(8,128)}) fusion(bf16[4,64,16,1024]{3,2,1,0:T(8,128)(2,1)} %all-reduce.2.cloned.1.call-done), kind=kLoop, calls=%fused_computation.11 | loop fusion | bytes 33554432 | tf_op jit(solution)/shard_map/slice | solution.py:864
  529.8 9.5 %pad_maximum_fusion = f32[1024,3072]{1,0:T(8,128)} fusion(f32[1024,1024]{1,0:T(8,128)} %bitcast.25, f32[1024,1024]{1,0:T(8,128)} %bitcast.24, f32[1024,1024]{1,0:T(8,128)S(1)} %bitcast.23), kind=kLoop, calls=%fused_computation.1 | loop fusion | flops 6291456 | bytes 25165824 | tf_op jit(solution)/shard_map/concatenate | solution.py:862
  539.3 1.0 copy.37
  540.3 1.3 copy.38
  (14 shorter events, 0.0 us)
Async XLA Ops:
  7.2 0.8 copy-start
  7.2 513.7 %all-reduce.2.cloned.1.call-start = ((), (), s32[]{:S(2)}) async-start(), calls=%async_computation | async-start | bytes 16777216 | tf_op jit(solution)/shard_map/psum | solution.py:822
  13.4 2.2 copy-start.5
  334.6 31.4 %copy-start.4 = (f32[8,1024]{1,0:T(8,128)S(1)}, f32[8,1024]{1,0:T(8,128)}, u32[]{:S(2)}) copy-start(f32[8,1024]{1,0:T(8,128)} %get-tuple-element.41) | copy-start | bytes 98308
  334.6 81.2 %copy-start.6 = (f32[4,1,1024]{2,1,0:T(1,128)S(1)}, f32[4,1,1024]{2,1,0:T(1,128)}, u32[]{:S(2)}) copy-start(f32[4,1,1024]{2,1,0:T(1,128)} %get-tuple-element.47) | copy-start | bytes 49156
  334.6 81.1 %copy-start.7 = (f32[4,1,1024]{2,1,0:T(1,128)S(1)}, f32[4,1,1024]{2,1,0:T(1,128)}, u32[]{:S(2)}) copy-start(f32[4,1,1024]{2,1,0:T(1,128)} %get-tuple-element.49) | copy-start | bytes 49156
  529.8 9.5 %copy-start.3 = (bf16[512,1024]{1,0:T(8,128)(2,1)S(1)}, bf16[512,1024]{1,0:T(8,128)(2,1)}, u32[]{:S(2)}) copy-start(bf16[512,1024]{1,0:T(8,128)(2,1)} %get-tuple-element.72) | copy-start | bytes 3145732
  529.8 10.5 %copy-start.2 = (f32[512,1024]{1,0:T(8,128)S(1)}, f32[512,1024]{1,0:T(8,128)}, u32[]{:S(2)}) copy-start(f32[512,1024]{1,0:T(8,128)} %get-tuple-element.73) | copy-start | bytes 6291460
  529.8 11.8 %copy-start.1 = (s32[8008]{0:T(1024)S(1)}, s32[8008]{0:T(1024)}, u32[]{:S(2)}) copy-start(s32[8008]{0:T(1024)} %param.19) | copy-start | bytes 96100
Sparse Core Ops, SparseCore 0:
  334.7 186.1 all-reduce.1

commit v2 on v1

--- a/solution.py
+++ b/solution.py
@@ -476,16 +476,16 @@
 
         x = land[ex, pl.ds(base, 2)].reshape(count, width)
         g = g_v[slot].reshape(count, width)
-        gb_back[ex] += jnp.sum(g.astype(F32), axis=0, keepdims=True)
+        gb_back[pl.ds(ex, 1)] += jnp.sum(g.astype(F32), axis=0, keepdims=True)
         hs, gps = [], []
         for f in range(ff // step_f):
             cols = slice(f * step_f, (f + 1) * step_f)
-            pre = mm(x, win_v[ex, :, cols]) + bias_in[ex, :, cols]
+            pre = mm(x, win_v[ex, :, cols]) + bias_in[pl.ds(ex, 1), cols]
             sig = jax.nn.sigmoid(pre)
             hid = (pre * sig).astype(BF)
             gh = mm_nt(g, wback_v[ex, cols, :])
             gp = (gh * sig * (1.0 + pre * (1.0 - sig))).astype(BF)
-            gb_in[ex, :, cols] += jnp.sum(gp.astype(F32), axis=0, keepdims=True)
+            gb_in[pl.ds(ex, 1), cols] += jnp.sum(gp.astype(F32), axis=0, keepdims=True)
             h_v[slot, :, :, cols] = hid.reshape(2, n_hid * cap, step_f)
             gp_v[slot, :, :, cols] = gp.reshape(2, n_hid * cap, step_f)
         gpv = gp_v[slot].reshape(count, ff)
@@ -565,8 +565,8 @@
             shape((lc, n_exp, per, ff), BF),
             shape((lc, n_exp, per, ff), BF),
             shape((lc, n_exp, n_y, 2, cap, width), BF),
-            shape((lc, 1, ff), F32),
-            shape((lc, 1, width), F32),
+            shape((lc, ff), F32),
+            shape((lc, width), F32),
         ),
         in_specs=[VM, HB, HB, VM, HB],
         out_specs=[VM, HB, HB, HB, HB, VM, VM],
@@ -590,33 +590,45 @@
     )(rows, grads, w_in, bias_in, w_back)
 
 
-def wgrad_kernel(x, gp, h, g, g_in, g_back):
+def finish_kernel(x, gp, h, g, mats, g_in, g_back, g_qkv, g_out):
     g_in[0] = mm_tn(x[0], gp[0])
     g_back[0] = mm_tn(h[0], g[0])
-
-
-def wgrad(x, gp, h, g):
+    rows, width = g_out.shape
+    for part in range(3):
+        g_qkv[:, part * width : (part + 1) * width] = mats[part].reshape(rows, width).astype(F32)
+    g_out[...] = mats[3].reshape(rows, width).astype(F32)
+
+
+def finish(x, gp, h, g, mats):
     lc, n, width = x.shape
     ff = gp.shape[2]
     cut = 2
+    rows = width // (lc * cut)
+    mats = mats.reshape(4, width // 16, 16, width)
     shape = jax.ShapeDtypeStruct
     return pl.pallas_call(
-        wgrad_kernel,
-        name="wgrad",
+        finish_kernel,
+        name="finish",
         grid=(lc, cut),
-        out_shape=(shape((lc, width, ff), F32), shape((lc, ff, width), F32)),
+        out_shape=(
+            shape((lc, width, ff), F32), shape((lc, ff, width), F32),
+            shape((width, 3 * width), F32), shape((width, width), F32),
+        ),
         in_specs=[
             pl.BlockSpec((1, n, width), lambda i, j: (i, 0, 0)),
             pl.BlockSpec((1, n, ff // cut), lambda i, j: (i, 0, j)),
             pl.BlockSpec((1, n, ff), lambda i, j: (i, 0, 0)),
             pl.BlockSpec((1, n, width // cut), lambda i, j: (i, 0, j)),
+            pl.BlockSpec((4, rows // 16, 16, width), lambda i, j: (0, i * cut + j, 0, 0)),
         ],
         out_specs=[
             pl.BlockSpec((1, width, ff // cut), lambda i, j: (i, 0, j)),
             pl.BlockSpec((1, ff, width // cut), lambda i, j: (i, 0, j)),
+            pl.BlockSpec((rows, 3 * width), lambda i, j: (i * cut + j, 0)),
+            pl.BlockSpec((rows, width), lambda i, j: (i * cut + j, 0)),
         ],
         compiler_params=pltpu.CompilerParams(vmem_limit_bytes=56 * MIB),
-    )(x, gp, h, g)
+    )(x, gp, h, g, mats)
 
 
 def attend_back_kernel(
@@ -711,7 +723,7 @@
             def _():
                 step_y(k + 2)
 
-            gather.step_exp(k, bias_back[...])
+            gather.step_exp(k, bias_back[...].reshape(lc, 1, width))
 
         def cols(part):
             return pl.ds(pl.multiple_of(part * width + p * 128, 128), 128)
@@ -818,8 +830,217 @@
     )
 
 
+def reduce_kernel(
+    n_x, n_y, n_z, mats, norms, out, norms_out,
+    acc, core_in, in1, in2, in3, n_acc, n_in,
+    c_s, c_r, s1, r1, s2, r2, s3, r3, t3, u3, t2, u2, t1, u1, d_s, d_r, n_s, n_r,
+):
+    e, h, y, c = place()
+    x, z = lax.rem(e, n_x), lax.div(e, n_x)
+    sub = n_x * n_y * n_z
+    half = mats.shape[0] // 2
+    piece = half // 2
+    n_sub = piece // sub
+    at = {"x": (n_x, x), "y": (n_y, y), "z": (n_z, z)}
+    orders = (("y", "x", "z"), ("x", "y", "z"))
+    sibling = (e, y * 2 + 1 - c)
+
+    def device(axis, o):
+        return {"x": (z * n_x + o, h), "y": (e, o * 2 + c), "z": (o * n_x + x, h)}[axis]
+
+    sem = pltpu.get_barrier_semaphore()
+    for axis in "xyz":
+        n, i = at[axis]
+        for d in range(1, n):
+            pl.semaphore_signal(sem, inc=1, device_id=device(axis, lax.rem(i + d, n)), device_id_type=MESH)
+    pl.semaphore_signal(sem, inc=1, device_id=sibling, device_id_type=MESH)
+    pl.semaphore_wait(sem, n_x + n_y + n_z - 2)
+
+    def units(p, b, depth):
+        first, count = p * piece + b * sub, sub
+        for axis in orders[p][:depth]:
+            n, i = at[axis]
+            count = count // n
+            first = first + i * count
+        return first, count
+
+    def core_copy(p, b):
+        first = p * piece + b * sub
+        return rcopy(
+            mats.at[pl.ds((1 - c) * half + first, sub)], core_in.at[pl.ds(first, sub)],
+            c_s.at[p, b], c_r.at[p, b], sibling,
+        )
+
+    lands = (in1, in2, in3)
+    sends, recvs = (s1, s2, s3), (r1, r2, r3)
+
+    def down(p, b, stage, d):
+        n, i = at[orders[p][stage]]
+        first, count = units(p, b, stage)
+        count = count // n
+        o = lax.rem(i + d, n)
+        return rcopy(
+            acc.at[pl.ds(first + o * count, count)], lands[stage].at[p, b, d - 1, pl.ds(0, count)],
+            sends[stage].at[p, b, d - 1], recvs[stage].at[p, b, d - 1], device(orders[p][stage], o),
+        )
+
+    ups, upr = (t1, t2, t3), (u1, u2, u3)
+
+    def up(p, b, stage, d):
+        n, i = at[orders[p][stage]]
+        first, count = units(p, b, stage + 1)
+        region = out.at[pl.ds(c * half + first, count)]
+        o = lax.rem(i + d, n)
+        return rcopy(
+            region, region, ups[stage].at[p, b, d - 1], upr[stage].at[p, b, d - 1], device(orders[p][stage], o)
+        )
+
+    def core_up(p, b):
+        region = out.at[pl.ds(c * half + p * piece + b * sub, sub)]
+        return rcopy(region, region, d_s.at[p, b], d_r.at[p, b], sibling)
+
+    def peers(p, stage):
+        return range(1, at[orders[p][stage]][0])
+
+    def event(p, b, q):
+        if q == 0:
+            core_copy(p, b).wait_recv()
+            first = p * piece + b * sub
+            mine = mats[pl.ds(c * half + first, sub)].astype(F32)
+            acc[pl.ds(first, sub)] = (mine + core_in[pl.ds(first, sub)].astype(F32)).astype(BF)
+        elif q <= 3:
+            first, count = units(p, b, q)
+            total = acc[pl.ds(first, count)].astype(F32)
+            for d in peers(p, q - 1):
+                down(p, b, q - 1, d).wait_recv()
+                total = total + lands[q - 1][p, b, d - 1, :count].astype(F32)
+            if q < 3:
+                acc[pl.ds(first, count)] = total.astype(BF)
+            else:
+                out[pl.ds(c * half + first, count)] = total.astype(BF)
+        else:
+            for d in peers(p, 6 - q):
+                up(p, b, 6 - q, d).wait_recv()
+        if q < 3:
+            for d in peers(p, q):
+                down(p, b, q, d).start()
+        elif q < 6:
+            for d in peers(p, 5 - q):
+                up(p, b, 5 - q, d).start()
+        else:
+            core_up(p, b).start()
+
+    for b in range(n_sub):
+        for p in range(2):
+            core_copy(p, b).start()
+
+    n_axes = (None, "y", "x", "z")
+
+    def n_copy(stage, d):
+        if stage == 0:
+            dev = sibling
+        else:
+            n, i = at[n_axes[stage]]
+            dev = device(n_axes[stage], lax.rem(i + d, n))
+        return rcopy(n_acc.at[stage], n_in.at[stage, d - 1], n_s.at[stage, d - 1], n_r.at[stage, d - 1], dev)
+
+    def n_peers(stage):
+        return range(1, 2 if stage == 0 else at[n_axes[stage]][0])
+
+    def n_total(stage):
+        for d in n_peers(stage):
+            n_copy(stage, d).wait_recv()
+        own = n_acc[stage]
+        if stage == 0:
+            return own + n_in[0, 0]
+        n, i = at[n_axes[stage]]
+        total = jnp.zeros_like(own)
+        for m in range(n):
+            term = own
+            for d in range(1, n):
+                term = jnp.where(lax.rem(i + n - d, n) == m, n_in[stage, d - 1], term)
+            total = total + term
+        return total
+
+    n_acc[0] = norms[...]
+    n_copy(0, 1).start()
+
+    @pl.loop(0, n_sub + 6)
+    def _(s):
+        for q in range(7):
+
+            @pl.when((s >= q) & (s - q < n_sub))
+            def _():
+                for p in range(2):
+                    event(p, s - q, q)
+
+        for stage in range(1, 4):
+
+            @pl.when(s == stage)
+            def _():
+                n_acc[stage] = n_total(stage - 1)
+                for d in n_peers(stage):
+                    n_copy(stage, d).start()
+
+    norms_out[...] = n_total(3)
+    for stage in range(4):
+        for d in n_peers(stage):
+            n_copy(stage, d).wait_send()
+
+    @pl.loop(0, n_sub)
+    def _(b):
+        for p in range(2):
+            core_up(p, b).wait_recv()
+            core_copy(p, b).wait_send()
+            core_up(p, b).wait_send()
+            for stage in range(3):
+                for d in peers(p, stage):
+                    down(p, b, stage, d).wait_send()
+                    up(p, b, stage, d).wait_send()
+
+
 def reduce_all(n_exp, n_hid, mats, norms):
-    return lax.psum(mats, ("exp", "hid")), lax.psum(norms, ("exp", "hid"))
+    n_y = n_hid // 2
+    n_x = n_y
+    n_z = n_exp // n_x
+    sub = n_x * n_y * n_z
+    width = norms.shape[1]
+    flat = mats.reshape(-1, 16, width)
+    half = flat.shape[0] // 2
+    n_sub = half // 2 // sub
+    most = max(n_x, n_y)
+    shape = jax.ShapeDtypeStruct
+
+    def land(n, count):
+        return pltpu.VMEM((2, n_sub, n - 1, count, 16, width), BF)
+
+    def sems(n):
+        return [DMA((2, n_sub, n - 1))] * 2
+
+    mats, norms = pl.pallas_call(
+        functools.partial(reduce_kernel, n_x, n_y, n_z),
+        name="reduce_all",
+        out_shape=(shape(flat.shape, BF), shape(norms.shape, F32)),
+        in_specs=[VM] * 2,
+        out_specs=[VM] * 2,
+        scratch_shapes=[
+            pltpu.VMEM((half, 16, width), BF),
+            pltpu.VMEM((half, 16, width), BF),
+            land(most, sub // min(n_x, n_y)),
+            land(most, sub // (n_x * n_y)),
+            land(n_z, 1),
+            pltpu.VMEM((4, *norms.shape), F32),
+            pltpu.VMEM((4, max(most, n_z) - 1, *norms.shape), F32),
+            DMA((2, n_sub)), DMA((2, n_sub)),
+            *sems(most), *sems(most), *sems(n_z), *sems(n_z), *sems(most), *sems(most),
+            DMA((2, n_sub)), DMA((2, n_sub)),
+            *[DMA((4, max(most, n_z) - 1))] * 2,
+        ],
+        compiler_params=pltpu.CompilerParams(
+            collective_id=3, has_side_effects=True, vmem_limit_bytes=50 * MIB
+        ),
+    )(flat, norms)
+    return mats, norms
 
 
 def token_slots(token_ids, hash_table, capacity, cap):
@@ -846,23 +1067,21 @@
         n_exp, n_hid, lc, cap, lengths, slot[None], tokens, gain1, shift1, w_qkv, w_out, gain2, shift2, cotangent
     )
     back, x, hid, gp, f_part, gb_in, gb_back = experts(
-        n_exp, n_hid, send, grads, w_in, bias_in[:, None], w_back
+        n_exp, n_hid, send, grads, w_in, bias_in, w_back
     )
     output, g_tokens, mats, norms = attend_back(
         n_exp, n_hid, lengths, slot[:, None], tokens, middle, cotangent, mixed, context, lse, back,
-        gain1, shift1, w_qkv, w_out, gain2, bias_back[:, None], f_part,
+        gain1, shift1, w_qkv, w_out, gain2, bias_back, f_part,
     )
     mats, norms = reduce_all(n_exp, n_hid, mats, norms)
     n_rows = n_exp * n_hid * cap
-    g_in, g_back = wgrad(
+    g_in, g_back, g_qkv, g_out = finish(
         x.reshape(lc, n_rows, width), gp.reshape(lc, n_rows, ff),
-        hid.reshape(lc, n_rows, ff), grads.reshape(lc, n_rows, width),
+        hid.reshape(lc, n_rows, ff), grads.reshape(lc, n_rows, width), mats,
     )
-    mats = mats.reshape(4, width, width).astype(F32)
-    g_qkv = jnp.concatenate([mats[0], mats[1], mats[2]], axis=1)
     return (
-        output, g_tokens, norms[0], norms[1], g_qkv, mats[3], norms[2], norms[3],
-        g_in, gb_in[:, 0], g_back, gb_back[:, 0],
+        output, g_tokens, norms[0], norms[1], g_qkv, g_out, norms[2], norms[3],
+        g_in, gb_in, g_back, gb_back,
     )
 
 

time: 549 us -> 481 us (0.88)
  Pallas kernels: 350 us -> 468 us
  waiting for transfers between devices: 105 us -> 0 us
  blocking collectives: 49.1 us -> 0 us
  between operations: 14.1 us -> 0.74 us
  local copies, waits for them, and re-layouts: 19.1 us -> 8.95 us
  other arithmetic: 11.2 us -> 1.7 us
    pallas_call x1 -> x2, Pallas kernels: 31.4 us -> 149 us  [the longest x1 110 us: reduce_all(): pl.pallas_call(functools.partial(reduce_kernel, n_x, n_y, n_z), name='red...]
    psum x1 -> x0, waiting for transfers between devices: 105 us -> none  [reduce_all(): return (lax.psum(mats, ('exp', 'hid')), lax.psum(norms, ('exp', 'hid')))]
    psum x1 -> x0, blocking collectives: 49.1 us -> none  [reduce_all(): return (lax.psum(mats, ('exp', 'hid')), lax.psum(norms, ('exp', 'hid')))]
    concatenate x1 -> x0, other arithmetic: 9.51 us -> none  [per_device(): g_qkv = jnp.concatenate([mats[0], mats[1], mats[2]], axis=1)]
    slice x1 -> x0, local copies, waits for them, and re-layouts: 8.92 us -> none  [per_device(): mats[3]]
  transfers between devices with their start and end apart: 1 -> 0, of which waited for: 1 -> 0; matrix products, arithmetic and copies ran while one was open for 0% -> 0% of each run, Pallas kernels for 6% -> 0%
where the time goes in v2:
time: 481 us; the launch traced here: 479 us
  Pallas kernels  468 us (97%)
  local copies, waits for them, and re-layouts  8.95 us (2%)
    pallas_call x1, Pallas kernels, experts(): pl.pallas_call(functools.partial(expert_kernel, n_exp, n_y), name='expert...  145 us
    pallas_call x1, Pallas kernels, reduce_all(): pl.pallas_call(functools.partial(reduce_kernel, n_x, n_y, n_z), name='red...  110 us
    pallas_call x1, Pallas kernels, attend_back(): pl.pallas_call(functools.partial(attend_back_kernel, n_exp, n_y), name='a...  97.3 us
    pallas_call x1, Pallas kernels, attend(): pl.pallas_call(functools.partial(attend_kernel, n_exp, n_y), name='attend...  76.2 us
    pallas_call x1, Pallas kernels, finish(): pl.pallas_call(finish_kernel, name='finish', grid=(lc, cut), out_shape=(s...  38.6 us

profile of v2, /device:TPU:0, one launch (start us, length us, event | category | flops | bytes accessed | tf_op | source)
XLA Modules:
  0.0 479.1 jit_solution(7629357189080604091)
XLA Ops:
  0.6 0.0 copy-start
  0.7 0.7 pad_clamp_fusion
  1.4 0.1 copy-done
  1.4 3.1 gather_fusion
  4.6 0.2 convert_reduce_fusion
  4.8 0.7 select_reduce_fusion
  5.6 0.0 copy-start.5
  5.6 0.9 copy.29.slot_col
  6.4 76.2 %attend.1 = (bf16[512,3072]{1,0:T(8,128)(2,1)}, bf16[512,1024]{1,0:T(8,128)(2,1)}, f32[512,1024]{1,0:T(8,128)}, f32[512,128]{1,0:T(8,128)}, bf16[8,4,32,1024]{3,...) custom-call(s32[1,2]{1,0:T(1,128)} %lens.3, s32[1,512]{1,0:T(1,128)} %bitcast.23, bf16[512,1024]{1,0:T(8,128)(2,1)} %tokens.3, ...), custom_call_target="tpu_custom_call" | custom-call | tf_op jit(solution)/shard_map/attend/pallas_call | solution.py:342
  82.7 145.3 %experts.1 = (bf16[8,4,32,1024]{3,2,1,0:T(8,128)(2,1)}, bf16[4,8,4,32,1024]{4,3,2,1,0:T(8,128)(2,1)}, bf16[4,8,128,1024]{3,2,1,0:T(8,128)(2,1)}, bf16[4,8,128,10...) custom-call(bf16[8,4,32,1024]{3,2,1,0:T(8,128)(2,1)} %get-tuple-element.39, ...), custom_call_target="tpu_custom_call" | custom-call | tf_op jit(solution)/shard_map/experts/pallas_call | solution.py:559
  228.0 97.3 %attend_back.1 = (bf16[512,1024]{1,0:T(8,128)(2,1)}, f32[512,1024]{1,0:T(8,128)}, bf16[4,64,16,1024]{3,2,1,0:T(8,128)(2,1)}, f32[8,1024]{1,0:T(8,128)}) custom-call(s32[1,2]{1,0:T(1,128)} %lens.3, s32[512,1]{1,0:T(8,128)} %copy.29.slot_col, bf16[512,1024]{1,0:T(8,128)(2,1)} %tokens.3, f32[512,1024]{1,0:T(8,128)} %get-tuple-element.35.middle, ...), custom_call_target="tpu_custom_call" | custom-call | tf_op jit(solution)/shard_map/attend_back/pallas_call | solution.py:799
  325.3 0.0 copy-start.2
  325.4 0.7 copy-done.2
  326.1 110.2 %reduce_all.1 = (bf16[256,16,1024]{2,1,0:T(8,128)(2,1)}, f32[8,1024]{1,0:T(8,128)S(1)}) custom-call(bf16[256,16,1024]{2,1,0:T(8,128)(2,1)} %bitcast.21, f32[8,1024]{1,0:T(8,128)S(1)} %copy-done.2), custom_call_target="tpu_custom_call" | custom-call | tf_op jit(solution)/shard_map/reduce_all/pallas_call | solution.py:1020
  436.3 0.6 fusion.1
  437.0 0.0 copy-start.1
  437.0 38.6 %finish.1 = (f32[4,1024,1024]{2,1,0:T(8,128)}, f32[4,1024,1024]{2,1,0:T(8,128)}, f32[1024,3072]{1,0:T(8,128)}, f32[1024,1024]{1,0:T(8,128)}) custom-call(bf16[4,1024,1024]{2,1,0:T(8,128)(2,1)} %bitcast.17, bf16[4,1024,1024]{2,1,0:T(8,128)(2,1)} %bitcast.19, bf16[4,1024,1024]{2,1,0:T(8,128)(2,1)} %bitcast.18, bf16[4,1024,1024]{2,1,0:T(8,128)(2,1)} %bitcast.16, ...), custom_call_target="tpu_custom_call" | custom-call | tf_op jit(solution)/shard_map/finish/pallas_call | solution.py:609
  475.6 1.0 copy.34
  476.6 1.3 copy.35
  477.9 0.0 copy-done.7
  477.9 0.6 copy.36
  478.5 0.0 copy-done.6
  478.5 0.6 copy.37
  479.1 0.0 copy-done.1
  (8 shorter events, 0.0 us)
Async XLA Ops:
  0.6 0.8 copy-start
  5.6 0.9 copy-start.5
  325.3 0.8 copy-start.2
  436.9 38.7 %copy-start.4 = (bf16[512,1024]{1,0:T(8,128)(2,1)S(1)}, bf16[512,1024]{1,0:T(8,128)(2,1)}, u32[]{:S(2)}) copy-start(bf16[512,1024]{1,0:T(8,128)(2,1)} %get-tuple-element.74) | copy-start | bytes 3145732
  436.9 39.6 %copy-start.3 = (f32[512,1024]{1,0:T(8,128)S(1)}, f32[512,1024]{1,0:T(8,128)}, u32[]{:S(2)}) copy-start(f32[512,1024]{1,0:T(8,128)} %get-tuple-element.75) | copy-start | bytes 6291460
  436.9 40.9 %copy-start.7 = (f32[4,1024]{1,0:T(4,128)S(1)}, f32[4,1024]{1,0:T(4,128)}, u32[]{:S(2)}) copy-start(f32[4,1024]{1,0:T(4,128)} %get-tuple-element.83) | copy-start | bytes 49156
  437.0 41.6 %copy-start.6 = (f32[4,1024]{1,0:T(4,128)S(1)}, f32[4,1024]{1,0:T(4,128)}, u32[]{:S(2)}) copy-start(f32[4,1024]{1,0:T(4,128)} %get-tuple-element.85) | copy-start | bytes 49156
  437.0 42.2 %copy-start.1 = (s32[8008]{0:T(1024)S(1)}, s32[8008]{0:T(1024)}, u32[]{:S(2)}) copy-start(s32[8008]{0:T(1024)} %param.19) | copy-start | bytes 96100

commit v3 on v2

--- a/solution.py
+++ b/solution.py
@@ -73,6 +73,13 @@
             self.es.at[k], self.er.at[k], (self.e ^ k, self.h),
         )
 
+    def start(self):
+        @pl.loop(1, self.n_exp)
+        def _(i):
+            low, high = lax.div(i + 1, 2), self.n_exp // 2 + lax.div(i, 2) - 1
+            k = jnp.where(i == self.n_exp - 1, self.n_exp - 1, jnp.where(lax.rem(i, 2) == 1, low, high))
+            self.over_exp(k).start()
+
     def block(self, k, hid):
         return self.land.at[:, self.e ^ k, hid]
 
@@ -148,24 +155,23 @@
         t = self.e ^ k
         return rcopy(self.pairs.at[t, :, self.y], self.back.at[self.e], self.es.at[k], self.er.at[k], (t, self.h))
 
-    def pair(self, k, yy):
-        t = self.e ^ k
-        return self.mine(k, yy).astype(F32) + self.pairs[t, :, yy].astype(F32)
-
     def step_core(self, k):
         self.over_core(k).start()
 
-    def step_y(self, k):
+    def fold(self, at, k):
         t = self.e ^ k
         self.over_core(k).wait_recv()
+        for yy in range(self.n_y):
+            pair = self.pairs[t, :, yy].astype(F32) + self.mine(at, yy).astype(F32)
+            self.pairs[t, :, yy] = pair.astype(BF)
+
+    def send_y(self, k):
         for d in range(1, self.n_y):
-            yy = lax.rem(self.y + d, self.n_y)
-            self.pairs[t, :, yy] = self.pair(k, yy).astype(BF)
             self.over_y(k, d).start()
 
     def step_exp(self, k, extra=None):
         t = self.e ^ k
-        total = self.pair(k, self.y)
+        total = self.pairs[t, :, self.y].astype(F32)
         for d in range(1, self.n_y):
             self.over_y(k, d).wait_recv()
             total = total + self.from_y[t, d - 1].astype(F32)
@@ -237,8 +243,8 @@
 
 def attend_kernel(
     n_exp, n_y, lens, slot_row, tokens, gain1, shift1, w_qkv, w_out, gain2, shift2, cot,
-    mixed, context, middle, lse, send, land,
-    cot_rows, normed, bias, own_sem, *sems,
+    mixed_h, context_h, middle_h, lse, send_h, land,
+    mixed, context, middle, send, cot_rows, normed, bias, wq_v, wo_v, in_sem, out_sem, own_sem, *sems,
 ):
     tok, width = tokens.shape
     e, h, y, c = place()
@@ -246,20 +252,40 @@
     per = lc * cap
     hd = width // HEADS
     spread = Spread(n_exp, n_y, cot_rows, land, sems)
-    greet(n_exp, n_y)
+    loads = [
+        pltpu.make_async_copy(w_qkv, wq_v, in_sem.at[0]),
+        pltpu.make_async_copy(w_out, wo_v, in_sem.at[1]),
+    ]
+    stores = [
+        pltpu.make_async_copy(a, b, out_sem.at[i])
+        for i, (a, b) in enumerate(
+            ((mixed, mixed_h), (context, context_h), (middle, middle_h), (send, send_h))
+        )
+    ]
+    for cp in loads:
+        cp.start()
 
     def pick(source, dst):
         rows = mm(slot_block(slot_row[...], dst * per, per), source)
         return rows.astype(BF).reshape(lc, cap, width)
 
-    @pl.loop(1, n_exp)
+    def advance(k):
+        spread.pass_on(k)
+
+        @pl.when(k > 0)
+        def _():
+            spread.pass_y(k - 1)
+
+    @pl.loop(0, n_exp)
     def _(k):
-        cot_rows[e ^ k] = pick(cot[...], e ^ k)
-        spread.over_exp(k).start()
-
-    cot_rows[e] = pick(cot[...], e)
+        cot_rows[k] = pick(cot[...], k)
+
     own = pltpu.make_async_copy(cot_rows.at[e], land.at[:, e, h], own_sem)
     own.start()
+    greet(n_exp, n_y)
+    spread.start()
+    own.wait()
+    spread.pass_on(0)
 
     @pl.loop(0, tok // 128)
     def _(i):
@@ -268,29 +294,31 @@
         normed[rows] = out.astype(BF)
 
     bias[...] = doc_bias(lens, tok)
-    own.wait()
-
-    @pl.loop(0, 3 * width // 512)
+    loads[0].wait()
+
+    @pl.loop(0, 3)
     def _(i):
-        cols = pl.ds(pl.multiple_of(i * 512, 512), 512)
-        mixed[:, cols] = mm(normed[...], w_qkv[:, cols]).astype(BF)
-
+        @pl.when(i > 0)
+        def _():
+            advance(i)
+
+        for j in range(width // 512):
+            cols = pl.ds(pl.multiple_of(i * width + j * 512, 512), 512)
+            mixed[:, cols] = mm(normed[...], wq_v[:, cols]).astype(BF)
+
+    stores[0].start()
+    advance(3)
     lse[...] = jnp.zeros_like(lse)
     lane = lax.broadcasted_iota(jnp.int32, (1, 128), 1)
     n_pairs = width // 128
-    steps = n_exp // n_pairs
     half = tok // 2
     heads_in = 128 // hd
 
     @pl.loop(0, n_pairs)
     def _(p):
-        for j in range(steps):
-            k = p * steps + j
-            spread.pass_on(k)
-
-            @pl.when(k > 0)
-            def _():
-                spread.pass_y(k - 1)
+        @pl.when((lax.rem(p, 2) == 1) & (p < 6))
+        def _():
+            advance(4 + lax.div(p, 2))
 
         def cols(part):
             return pl.ds(pl.multiple_of(part * width + p * 128, 128), 128)
@@ -315,19 +343,32 @@
             lse[rows, :] = lses
             context[rows, pl.ds(pl.multiple_of(p * 128, 128), 128)] = total.astype(BF)
 
-    spread.pass_y(n_exp - 1)
+    stores[1].start()
+    loads[1].wait()
 
     @pl.loop(0, tok // 256)
     def _(i):
-        rows = pl.ds(i * 256, 256)
-        mid = tokens[rows].astype(F32) + mm(context[rows], w_out[...])
+        rows = pl.ds(pl.multiple_of(i * 256, 256), 256)
+        mid = tokens[rows].astype(F32) + mm(context[rows], wo_v[...])
         middle[rows] = mid
         out, _, _ = norm_rows(mid, gain2[...], shift2[...])
         normed[rows] = out.astype(BF)
 
+    stores[2].start()
+
     @pl.loop(0, n_exp)
     def _(k):
         send[k] = pick(normed[...], k)
+
+    stores[3].start()
+
+    @pl.loop(7, n_exp)
+    def _(k):
+        advance(k)
+
+    spread.pass_y(n_exp - 1)
+    for cp in stores:
+        cp.wait()
 
     @pl.loop(0, n_exp)
     def _(k):
@@ -350,12 +391,20 @@
             shape((n_exp, lc, cap, width), BF),
             shape((lc, n_exp, n_hid, cap, width), BF),
         ),
-        in_specs=[SM] + [VM] * 9,
-        out_specs=[VM] * 6,
+        in_specs=[SM, VM, VM, VM, VM, HB, HB, VM, VM, VM],
+        out_specs=[HB, HB, HB, VM, HB, HB],
         scratch_shapes=[
+            pltpu.VMEM((tok, 3 * width), BF),
+            pltpu.VMEM((tok, width), BF),
+            pltpu.VMEM((tok, width), F32),
+            pltpu.VMEM((n_exp, lc, cap, width), BF),
             pltpu.VMEM((n_exp, lc, cap, width), BF),
             pltpu.VMEM((tok, width), BF),
             pltpu.VMEM((tok, tok), F32),
+            pltpu.VMEM(w_qkv.shape, BF),
+            pltpu.VMEM(w_out.shape, BF),
+            DMA((2,)),
+            DMA((4,)),
             DMA,
             *Spread.sems(n_exp, n_y),
         ],
@@ -427,16 +476,14 @@
     own.start()
     greet(n_exp, n_y)
 
-    @pl.loop(1, n_exp)
-    def _(k):
-        spread.over_exp(k).start()
-
+    spread.start()
     gb_in[...] = jnp.zeros_like(gb_in)
     gb_back[...] = jnp.zeros_like(gb_back)
     own.wait()
     spread.pass_on(0)
     spread.pass_on(1)
     spread.pass_y(0)
+    spread.pass_on(2)
     spread.pass_y(1)
 
     n_steps = n_chunks * lc
@@ -496,42 +543,59 @@
         for cp in out_copies(i):
             cp.start()
 
-        @pl.when(j + 1 < n_chunks)
-        def _():
-            @pl.when(ex == 0)
+        @pl.when(i == 0)
+        def _():
+            spread.pass_y(2)
+            spread.pass_on(3)
+
+        @pl.when(i == 1)
+        def _():
+            spread.pass_y(3)
+
+        @pl.when((i >= 2) & (lax.rem(i, 2) == 0) & (lax.div(i, 2) + 3 < n_exp))
+        def _():
+            spread.pass_on(lax.div(i, 2) + 3)
+
+            @pl.when(i == 2 * (n_exp - 4))
             def _():
-                spread.pass_on(2 * j + 2)
-
-            @pl.when(ex == 1)
+                gather.send_y(0)
+                gather.send_y(1)
+
+        @pl.when((i >= 3) & (lax.rem(i, 2) == 1) & (lax.div(i, 2) + 3 < n_exp))
+        def _():
+            spread.pass_y(lax.div(i, 2) + 3)
+
+        @pl.when((j >= 1) & (ex == 0))
+        def _():
+            gather.fold(2 * j - 2, 2 * j - 2)
+
+        @pl.when((j >= 1) & (ex == 1))
+        def _():
+            gather.fold(2 * j - 1, 2 * j - 1)
+
+            @pl.when(j >= 2)
             def _():
-                spread.pass_y(2 * j + 2)
-                spread.pass_on(2 * j + 3)
-
-            @pl.when(ex == 2)
+                gather.send_y(2 * j - 2)
+                gather.send_y(2 * j - 1)
+
+        @pl.when((j >= 3) & (ex == 2))
+        def _():
+            gather.step_exp(2 * j - 4)
+
+        @pl.when(ex == lc - 1)
+        def _():
+            @pl.when(j >= 3)
             def _():
-                spread.pass_y(2 * j + 3)
-
-        @pl.when(j > 0)
-        def _():
-            @pl.when(ex == 0)
-            def _():
-                gather.step_y(2 * j - 2)
-                gather.step_y(2 * j - 1)
-
-            @pl.when(ex == lc - 1)
-            def _():
-                gather.step_exp(2 * j - 2)
-                gather.step_exp(2 * j - 1)
-
-        @pl.when(ex == lc - 1)
-        def _():
+                gather.step_exp(2 * j - 3)
+
             gather.step_core(2 * j)
             gather.step_core(2 * j + 1)
 
-    gather.step_y(n_exp - 2)
-    gather.step_y(n_exp - 1)
-    gather.step_exp(n_exp - 2)
-    gather.step_exp(n_exp - 1)
+    for k in (n_exp - 2, n_exp - 1):
+        gather.fold(k, k)
+        gather.send_y(k)
+    for k in (*range(n_exp - 4, n_exp), 0, 1):
+        gather.step_exp(k)
 
     for k in range(n_exp - 4, n_exp):
         gather.over_core(k).wait_send()
@@ -632,10 +696,11 @@
 
 
 def attend_back_kernel(
-    n_exp, n_y, lens, slot_col, tokens, middle, cot, mixed, context, lse, back,
-    gain1, shift1, w_qkv, w_out, gain2, bias_back, f_part,
+    n_exp, n_y, lens, slot_col, tokens_h, middle_h, cot_h, mixed_h, context_h, lse, back_h,
+    gain1, shift1, w_qkv_h, w_out_h, gain2, bias_back, f_part,
     output, g_tokens, g_mats, g_norms,
-    bias, gm, gattn, gctx, gmixed, n1t, lse_t, mine_v, f_back, mine_sem, *rest,
+    tokens, middle, cot, mixed, context, back, w_qkv, w_out,
+    bias, gm, gattn, gctx, gmixed, n1t, lse_t, mine_v, f_back, mine_sem, in_sem, *rest,
 ):
     tok, width = tokens.shape
     hd = width // HEADS
@@ -643,21 +708,50 @@
     n_gather = len(Gather.scratch(1, 2, 1, 1, 1))
     lc, cap = f_back.shape[1:3]
     gather = Gather(
-        n_exp, n_y, lambda k: f_part.at[:, e ^ k, :, 1 - c], lambda k, yy: mine_v[lax.rem(k, 4), :, yy],
+        n_exp, n_y, lambda k: f_part.at[:, e ^ k, :, 1 - c], lambda m, yy: mine_v[lax.rem(m, 4), :, yy],
         *rest[:n_gather], f_back, rest[n_gather:],
     )
 
-    def fetch(k):
-        slot = lax.rem(k, 4)
-        return pltpu.make_async_copy(f_part.at[:, e ^ k, :, c], mine_v.at[slot], mine_sem.at[slot])
-
-    for k in range(3):
-        fetch(k).start()
+    def order(m):
+        return jnp.where(m < n_exp // 2, m + n_exp // 2, n_exp - 1 - m)
+
+    def fetch(m):
+        slot = lax.rem(m, 4)
+        return pltpu.make_async_copy(
+            f_part.at[:, e ^ order(m), :, c], mine_v.at[slot], mine_sem.at[slot]
+        )
+
+    loads = [
+        pltpu.make_async_copy(a, b, in_sem.at[i])
+        for i, (a, b) in enumerate((
+            (back_h, back), (middle_h, middle), (cot_h, cot), (w_out_h, w_out), (tokens_h, tokens),
+            (context_h, context), (mixed_h, mixed), (w_qkv_h, w_qkv),
+        ))
+    ]
     greet(n_exp, n_y)
 
     @pl.loop(0, n_exp)
-    def _(k):
-        gather.step_core(k)
+    def _(m):
+        gather.step_core(order(m))
+
+    for m in range(4):
+        fetch(m).start()
+    for cp in loads:
+        cp.start()
+
+    def leave(m):
+        fetch(m).wait()
+        gather.fold(m, order(m))
+        gather.send_y(order(m))
+
+        @pl.when(m + 4 < n_exp)
+        def _():
+            fetch(m + 4).start()
+
+    leave(0)
+    leave(1)
+    for cp in loads[:5]:
+        cp.wait()
 
     g_norms[...] = jnp.zeros_like(g_norms)
     n_slots = n_exp * lc * cap
@@ -680,12 +774,10 @@
         out, _, _ = norm_rows(tokens[rows].astype(F32), gain1[...], shift1[...])
         n1t[:, rows] = out.astype(BF).T
 
-    def step_y(k):
-        fetch(k).wait()
-        gather.step_y(k)
-
-    step_y(0)
-    step_y(1)
+    leave(2)
+    leave(3)
+    for cp in loads[5:]:
+        cp.wait()
 
     @pl.loop(0, width // 256)
     def _(i):
@@ -706,24 +798,18 @@
 
     lane = lax.broadcasted_iota(jnp.int32, (1, 128), 1)
     n_pairs = width // 128
-    steps = n_exp // n_pairs
     half = tok // 2
     heads_in = 128 // hd
 
     @pl.loop(0, n_pairs)
     def _(p):
-        for j in range(steps):
-            k = p * steps + j
-
-            @pl.when(k + 3 < n_exp)
-            def _():
-                fetch(k + 3).start()
-
-            @pl.when(k + 2 < n_exp)
-            def _():
-                step_y(k + 2)
-
-            gather.step_exp(k, bias_back[...].reshape(lc, 1, width))
+        @pl.when(p + 4 < n_exp)
+        def _():
+            leave(p + 4)
+
+        @pl.when((p >= 2) & (lax.rem(p, 2) == 0))
+        def _():
+            gather.step_exp(order(lax.div(p, 2) - 1), bias_back[...].reshape(lc, 1, width))
 
         def cols(part):
             return pl.ds(pl.multiple_of(part * width + p * 128, 128), 128)
@@ -759,6 +845,8 @@
             gmixed[rows, cols(1)] = dkey[b].astype(BF)
             gmixed[rows, cols(2)] = dval[b].astype(BF)
 
+    gather.step_exp(order(3), bias_back[...].reshape(lc, 1, width))
+
     @pl.loop(0, tok // 256)
     def _(i):
         rows = pl.ds(pl.multiple_of(i * 256, 256), 256)
@@ -768,6 +856,8 @@
         g_norms[1:2] += fold(up)
         g_tokens[rows] = gm[rows] + norm_back(up, unit, inverse, gain1[...])
 
+    gather.step_exp(order(4), bias_back[...].reshape(lc, 1, width))
+
     for part in range(3):
 
         @pl.loop(0, width // 256)
@@ -775,6 +865,14 @@
             rows = pl.ds(pl.multiple_of(i * 256, 256), 256)
             piece = mm(n1t[rows], gmixed[:, part * width : (part + 1) * width])
             g_mats[part, pl.ds(i * 16, 16)] = piece.astype(BF).reshape(16, 16, width)
+
+    @pl.loop(n_pairs + 4, max(n_exp, n_pairs + 4))
+    def _(m):
+        leave(m)
+
+    @pl.loop(5, n_exp)
+    def _(m):
+        gather.step_exp(order(m), bias_back[...].reshape(lc, 1, width))
 
     @pl.loop(0, n_exp)
     def _(k):
@@ -805,9 +903,10 @@
             shape((4, width // 16, 16, width), BF),
             shape((8, width), F32),
         ),
-        in_specs=[SM] + [VM] * 14 + [HB],
+        in_specs=[SM, VM, HB, HB, HB, HB, HB, VM, HB, VM, VM, HB, HB, VM, VM, HB],
         out_specs=[VM] * 4,
         scratch_shapes=[
+            *[pltpu.VMEM(a.shape, a.dtype) for a in (tokens, middle, cot, mixed, context, back, w_qkv, w_out)],
             pltpu.VMEM((tok, tok), F32),
             pltpu.VMEM((tok, width), F32),
             pltpu.VMEM((tok, width), BF),
@@ -818,6 +917,7 @@
             pltpu.VMEM((4, lc, n_y, cap, width), BF),
             pltpu.VMEM((n_exp, lc, cap, width), BF),
             DMA((4,)),
+            DMA((8,)),
             *Gather.scratch(n_exp, n_y, lc, cap, width),
             *Gather.sems(n_exp, n_y),
         ],

time: 481 us -> 441 us (0.917)
  Pallas kernels: 468 us -> 429 us
    pallas_call x1, Pallas kernels: 97.3 us -> 81.1 us  [attend_back(): pl.pallas_call(functools.partial(attend_back_kernel, n_exp, n_y), name='a...]
    pallas_call x1, Pallas kernels: 76.2 us -> 67.5 us  [attend(): pl.pallas_call(functools.partial(attend_kernel, n_exp, n_y), name='attend...]
    pallas_call x1, Pallas kernels: 110 us -> 103 us  [reduce_all(): pl.pallas_call(functools.partial(reduce_kernel, n_x, n_y, n_z), name='red...]
    pallas_call x1, Pallas kernels: 145 us -> 139 us  [experts(): pl.pallas_call(functools.partial(expert_kernel, n_exp, n_y), name='expert...]
where the time goes in v3:
time: 441 us; the launch traced here: 440 us
  Pallas kernels  429 us (97%)
  local copies, waits for them, and re-layouts  8.95 us (2%)
    pallas_call x1, Pallas kernels, experts(): pl.pallas_call(functools.partial(expert_kernel, n_exp, n_y), name='expert...  139 us
    pallas_call x1, Pallas kernels, reduce_all(): pl.pallas_call(functools.partial(reduce_kernel, n_x, n_y, n_z), name='red...  103 us
    pallas_call x1, Pallas kernels, attend_back(): pl.pallas_call(functools.partial(attend_back_kernel, n_exp, n_y), name='a...  81.1 us
    pallas_call x1, Pallas kernels, attend(): pl.pallas_call(functools.partial(attend_kernel, n_exp, n_y), name='attend...  67.5 us
    pallas_call x1, Pallas kernels, finish(): pl.pallas_call(finish_kernel, name='finish', grid=(lc, cut), out_shape=(s...  38.6 us

profile of v3, /device:TPU:0, one launch (start us, length us, event | category | flops | bytes accessed | tf_op | source)
XLA Modules:
  0.0 440.1 jit_solution(2779465705032905003)
XLA Ops:
  0.6 0.0 copy-start
  0.7 0.7 pad_clamp_fusion
  1.4 0.1 copy-done
  1.4 3.1 gather_fusion
  4.6 0.2 convert_reduce_fusion
  4.8 0.7 select_reduce_fusion
  5.6 0.0 copy-start.5
  5.6 0.9 copy.29.slot_col
  6.4 0.0 copy-done.5
  6.4 67.5 %attend.1 = (bf16[512,3072]{1,0:T(8,128)(2,1)}, bf16[512,1024]{1,0:T(8,128)(2,1)}, f32[512,1024]{1,0:T(8,128)}, f32[512,128]{1,0:T(8,128)}, bf16[8,4,32,1024]{3,...) custom-call(s32[1,2]{1,0:T(1,128)} %lens.3, s32[1,512]{1,0:T(1,128)} %bitcast.23, bf16[512,1024]{1,0:T(8,128)(2,1)} %tokens_h.1, ...), custom_call_target="tpu_custom_call" | custom-call | tf_op jit(solution)/shard_map/attend/pallas_call | solution.py:383
  73.9 138.7 %experts.1 = (bf16[8,4,32,1024]{3,2,1,0:T(8,128)(2,1)}, bf16[4,8,4,32,1024]{4,3,2,1,0:T(8,128)(2,1)}, bf16[4,8,128,1024]{3,2,1,0:T(8,128)(2,1)}, bf16[4,8,128,10...) custom-call(bf16[8,4,32,1024]{3,2,1,0:T(8,128)(2,1)} %get-tuple-element.39, ...), custom_call_target="tpu_custom_call" | custom-call | tf_op jit(solution)/shard_map/experts/pallas_call | solution.py:623
  212.7 81.1 %attend_back.1 = (bf16[512,1024]{1,0:T(8,128)(2,1)}, f32[512,1024]{1,0:T(8,128)}, bf16[4,64,16,1024]{3,2,1,0:T(8,128)(2,1)}, f32[8,1024]{1,0:T(8,128)}) custom-call(s32[1,2]{1,0:T(1,128)} %lens.3, s32[512,1]{1,0:T(8,128)} %copy.29.slot_col, bf16[512,1024]{1,0:T(8,128)(2,1)} %tokens_h.1, f32[512,1024]{1,0:T(8,128)} %get-tuple-element.35.middle_h, ...), custom_call_target="tpu_custom_call" | custom-call | tf_op jit(solution)/shard_map/attend_back/pallas_call | solution.py:897
  293.8 0.7 copy-done.2
  294.5 102.7 %reduce_all.1 = (bf16[256,16,1024]{2,1,0:T(8,128)(2,1)}, f32[8,1024]{1,0:T(8,128)S(1)}) custom-call(bf16[256,16,1024]{2,1,0:T(8,128)(2,1)} %bitcast.21, f32[8,1024]{1,0:T(8,128)S(1)} %copy-done.2), custom_call_target="tpu_custom_call" | custom-call | tf_op jit(solution)/shard_map/reduce_all/pallas_call | solution.py:1120
  397.3 0.6 fusion.1
  397.9 0.0 copy-start.1
  397.9 38.6 %finish.1 = (f32[4,1024,1024]{2,1,0:T(8,128)}, f32[4,1024,1024]{2,1,0:T(8,128)}, f32[1024,3072]{1,0:T(8,128)}, f32[1024,1024]{1,0:T(8,128)}) custom-call(bf16[4,1024,1024]{2,1,0:T(8,128)(2,1)} %bitcast.17, bf16[4,1024,1024]{2,1,0:T(8,128)(2,1)} %bitcast.19, bf16[4,1024,1024]{2,1,0:T(8,128)(2,1)} %bitcast.18, bf16[4,1024,1024]{2,1,0:T(8,128)(2,1)} %bitcast.16, ...), custom_call_target="tpu_custom_call" | custom-call | tf_op jit(solution)/shard_map/finish/pallas_call | solution.py:673
  436.6 1.0 copy.34
  437.5 1.3 copy.35
  438.9 0.0 copy-done.7
  438.9 0.6 copy.36
  439.5 0.0 copy-done.6
  439.5 0.6 copy.37
  440.1 0.0 copy-done.1
  (8 shorter events, 0.0 us)
Async XLA Ops:
  0.6 0.8 copy-start
  5.6 0.9 copy-start.5
  293.8 0.8 copy-start.2
  397.9 38.7 %copy-start.4 = (bf16[512,1024]{1,0:T(8,128)(2,1)S(1)}, bf16[512,1024]{1,0:T(8,128)(2,1)}, u32[]{:S(2)}) copy-start(bf16[512,1024]{1,0:T(8,128)(2,1)} %get-tuple-element.74) | copy-start | bytes 3145732
  397.9 39.6 %copy-start.3 = (f32[512,1024]{1,0:T(8,128)S(1)}, f32[512,1024]{1,0:T(8,128)}, u32[]{:S(2)}) copy-start(f32[512,1024]{1,0:T(8,128)} %get-tuple-element.75) | copy-start | bytes 6291460
  397.9 41.0 %copy-start.7 = (f32[4,1024]{1,0:T(4,128)S(1)}, f32[4,1024]{1,0:T(4,128)}, u32[]{:S(2)}) copy-start(f32[4,1024]{1,0:T(4,128)} %get-tuple-element.83) | copy-start | bytes 49156
  397.9 41.6 %copy-start.6 = (f32[4,1024]{1,0:T(4,128)S(1)}, f32[4,1024]{1,0:T(4,128)}, u32[]{:S(2)}) copy-start(f32[4,1024]{1,0:T(4,128)} %get-tuple-element.85) | copy-start | bytes 49156
  397.9 42.2 %copy-start.1 = (s32[8008]{0:T(1024)S(1)}, s32[8008]{0:T(1024)}, u32[]{:S(2)}) copy-start(s32[8008]{0:T(1024)} %param.19) | copy-start | bytes 96100

commit v4 on v3

--- a/solution.py
+++ b/solution.py
@@ -414,203 +414,341 @@
     )(lens, slot_row, tokens, gain1, shift1, w_qkv, w_out, gain2, shift2, cot)
 
 
+STEP_W = 512
+
+
+class Halves:
+    def __init__(self, n_exp, n_y):
+        self.n_exp, self.n_y, self.half = n_exp, n_y, n_exp // 2
+        self.e, self.h, self.y, self.c = place()
+        self.sibling = (self.e, self.y * 2 + 1 - self.c)
+
+    def range(self, g):
+        first = lax.div(self.e, self.half) * self.half
+        return pl.ds(pl.multiple_of(first if g == 0 else self.half - first, self.half), self.half)
+
+    def y_peer(self, d):
+        return (self.e, lax.rem(self.y + d, self.n_y) * 2 + self.c)
+
+
+class SpreadExpert(Halves):
+    def __init__(self, n_exp, n_y, rows, land, sems):
+        super().__init__(n_exp, n_y)
+        self.rows, self.land = rows, land
+        self.es, self.er, self.ys, self.yr, self.cs, self.cr = sems
+
+    @staticmethod
+    def sems(lc, n_exp, n_y):
+        return [DMA((lc, n_exp))] * 2 + [DMA((lc, 2, n_y))] * 4
+
+    def over_exp(self, ex, k):
+        return rcopy(
+            self.rows.at[self.e ^ k, ex], self.land.at[ex, self.e, self.h],
+            self.es.at[ex, k], self.er.at[ex, k], (self.e ^ k, self.h),
+        )
+
+    def start(self, ex):
+        half = self.half
+        for i in range(1, self.n_exp):
+            self.over_exp(ex, half + i // 2 - 1 if i % 2 == 0 else ((i + 1) // 2 if i < self.n_exp - 1 else i)).start()
+
+    def over_y(self, ex, g, d):
+        blk = self.land.at[ex, self.range(g), self.h]
+        return rcopy(blk, blk, self.ys.at[ex, g, d], self.yr.at[ex, g, d], self.y_peer(d))
+
+    def over_core(self, ex, g, d):
+        hid = lax.rem(self.y + self.n_y - d, self.n_y) * 2 + self.c
+        blk = self.land.at[ex, self.range(g), hid]
+        return rcopy(blk, blk, self.cs.at[ex, g, d], self.cr.at[ex, g, d], self.sibling)
+
+    def pass_on(self, ex, g):
+        for k in range(max(1, g * self.half), (g + 1) * self.half):
+            self.over_exp(ex, k).wait_recv()
+        for d in range(1, self.n_y):
+            self.over_y(ex, g, d).start()
+        self.over_core(ex, g, 0).start()
+
+    def pass_y(self, ex, g):
+        for d in range(1, self.n_y):
+            self.over_y(ex, g, d).wait_recv()
+            self.over_core(ex, g, d).start()
+
+    def landed(self, ex, g):
+        for d in range(self.n_y):
+            self.over_core(ex, g, d).wait_recv()
+
+    def sent(self, ex):
+        for k in range(1, self.n_exp):
+            self.over_exp(ex, k).wait_send()
+        for g in range(2):
+            for d in range(1, self.n_y):
+                self.over_y(ex, g, d).wait_send()
+            for d in range(self.n_y):
+                self.over_core(ex, g, d).wait_send()
+
+
+class GatherExpert(Halves):
+    def __init__(self, n_exp, n_y, part, pairs, from_y, back, sems):
+        super().__init__(n_exp, n_y)
+        self.part, self.pairs, self.from_y, self.back = part, pairs, from_y, back
+        self.es, self.er, self.ys, self.yr, self.cs, self.cr = sems
+
+    @staticmethod
+    def sems(lc, n_exp, n_y):
+        return [DMA((lc, n_exp))] * 2 + [DMA((lc, 2, n_y))] * 2 + [DMA((lc, 2))] * 2
+
+    def over_core(self, ex, b):
+        return rcopy(
+            self.part.at[self.range(b), :, 1 - self.c], self.pairs.at[ex, self.range(b)],
+            self.cs.at[ex, b], self.cr.at[ex, b], self.sibling,
+        )
+
+    def over_y(self, ex, b, d):
+        yy = lax.rem(self.y + d, self.n_y)
+        return rcopy(
+            self.pairs.at[ex, self.range(b), yy], self.from_y.at[d - 1, ex, self.range(b)],
+            self.ys.at[ex, b, d], self.yr.at[ex, b, d], self.y_peer(d),
+        )
+
+    def over_exp(self, ex, k):
+        t = self.e ^ k
+        return rcopy(
+            self.pairs.at[ex, t, self.y], self.back.at[self.e, ex], self.es.at[ex, k], self.er.at[ex, k], (t, self.h)
+        )
+
+    def stay(self, ex):
+        return pltpu.make_async_copy(self.pairs.at[ex, self.e, self.y], self.back.at[self.e, ex], self.es.at[ex, 0])
+
+    def fold(self, ex, b):
+        self.over_core(ex, b).wait_recv()
+        rows = self.range(b)
+        for yy in range(self.n_y):
+            pair = self.pairs[ex, rows, yy].astype(F32) + self.part[rows, yy, self.c].astype(F32)
+            self.pairs[ex, rows, yy] = pair.astype(BF)
+        for d in range(1, self.n_y):
+            self.over_y(ex, b, d).start()
+        self.over_core(ex, b).wait_send()
+
+    def step_exp(self, ex, b):
+        rows = self.range(b)
+        total = self.pairs[ex, rows, self.y].astype(F32)
+        for d in range(1, self.n_y):
+            self.over_y(ex, b, d).wait_recv()
+            total = total + self.from_y[d - 1, ex, rows].astype(F32)
+        self.pairs[ex, rows, self.y] = total.astype(BF)
+        for i in range(self.half):
+            k = b * self.half + i
+            if k == 0:
+                self.stay(ex).start()
+            else:
+                self.over_exp(ex, k).start()
+
+    def finish(self, ex):
+        self.stay(ex).wait()
+        for b in range(2):
+            for d in range(1, self.n_y):
+                self.over_y(ex, b, d).wait_send()
+        for k in range(1, self.n_exp):
+            self.over_exp(ex, k).wait_send()
+            self.over_exp(ex, k).wait_recv()
+
+
 def expert_kernel(
     n_exp, n_y, rows, grads, w_in, bias_in, w_back,
-    back, x_out, h_out, gp_out, f_out, gb_in, gb_back,
-    land, part, win_v, wback_v, g_v, h_v, gp_v, f_v,
-    w_sem, g_sem, o_sem, x_sem, own_sem, *rest,
+    back, f_out, wi_out, wb_out, gb_in, gb_back,
+    land, part, pairs, from_y, wi_v, wb_v, g_v, h_v, gp_v, f_v, wi_st, wb_st,
+    w_sem, g_sem, f_sem, o_sem, own_sem, *rest,
 ):
     e, h, y, c = place()
-    n_gather = len(Gather.scratch(1, 2, 1, 1, 1))
-    n_spread = len(Spread.sems(1, 1))
-    scr, sp_sems, ga_sems = rest[:n_gather], rest[n_gather : n_gather + n_spread], rest[n_gather + n_spread :]
-    spread = Spread(n_exp, n_y, rows, land, sp_sems)
-
-
-    def part_of(k):
-        return part.at[lax.rem(lax.div(k, 2), 2), :, lax.rem(e ^ k, 2)]
-
-    gather = Gather(
-        n_exp, n_y, lambda k: part_of(k).at[:, :, 1 - c], lambda k, yy: part_of(k)[:, yy, c],
-        *scr, back, ga_sems,
-    )
+    n_spread = len(SpreadExpert.sems(1, 1, 1))
+    spread = SpreadExpert(n_exp, n_y, rows, land, rest[:n_spread])
+    gather = GatherExpert(n_exp, n_y, part, pairs, from_y, back, rest[n_spread:])
     n_hid = 2 * n_y
     lc, cap, width = rows.shape[1:]
     ff = w_in.shape[2]
-    count = 2 * n_hid * cap
-    n_chunks = n_exp // 2
+    n_src = 4
+    block = n_src * n_hid * cap
+    n_rb = n_exp // n_src
     step_f = min(512, ff)
+    step_w = STEP_W
 
     def weights(ex):
+        slot = lax.rem(ex, 2)
         return (
-            pltpu.make_async_copy(w_in.at[ex], win_v.at[ex], w_sem.at[0, ex]),
-            pltpu.make_async_copy(w_back.at[ex], wback_v.at[ex], w_sem.at[1, ex]),
+            pltpu.make_async_copy(w_in.at[ex], wi_v.at[slot], w_sem.at[0, slot]),
+            pltpu.make_async_copy(w_back.at[ex], wb_v.at[slot], w_sem.at[1, slot]),
         )
 
-    for ex in range(lc):
-        for cp in weights(ex):
-            cp.start()
-
-    def base_of(i):
-        t = e ^ (2 * lax.div(i, lc))
-        return t - lax.rem(t, 2)
-
-    def g_copy(i):
-        src = grads.at[lax.rem(i, lc), pl.ds(base_of(i), 2)]
-        return pltpu.make_async_copy(src, g_v.at[lax.rem(i, 2)], g_sem.at[lax.rem(i, 2)])
-
-    def out_copies(i):
-        ex, slot, to = lax.rem(i, lc), lax.rem(i, 2), pl.ds(base_of(i), 2)
-        return (
-            pltpu.make_async_copy(h_v.at[slot], h_out.at[ex, to], o_sem.at[0, slot]),
-            pltpu.make_async_copy(gp_v.at[slot], gp_out.at[ex, to], o_sem.at[1, slot]),
-            pltpu.make_async_copy(f_v.at[slot], f_out.at[ex, to], o_sem.at[2, slot]),
-        )
-
-    def x_copy(i):
-        ex, to = lax.rem(i, lc), pl.ds(base_of(i), 2)
-        return pltpu.make_async_copy(land.at[ex, to], x_out.at[ex, to], x_sem.at[i])
-
-    g_copy(0).start()
+    def g_copy(ex):
+        slot = lax.rem(ex, 2)
+        return pltpu.make_async_copy(grads.at[ex], g_v.at[slot], g_sem.at[slot])
+
+    def f_copy(ex, rb):
+        return pltpu.make_async_copy(f_v, f_out.at[ex, sources(rb)], f_sem)
+
+    def wi_copy(ex, i):
+        return pltpu.make_async_copy(wi_st, wi_out.at[ex, pl.ds(i * step_w, step_w)], o_sem.at[0])
+
+    def wb_copy(ex, i):
+        return pltpu.make_async_copy(wb_st, wb_out.at[ex, pl.ds(i * step_w, step_w)], o_sem.at[1])
+
+    def sources(rb):
+        return pl.ds(lax.rem(lax.div(e, n_exp // 2) * (n_rb // 2) + rb, n_rb) * n_src, n_src)
+
     own = pltpu.make_async_copy(rows.at[e], land.at[:, e, h], own_sem)
     own.start()
     greet(n_exp, n_y)
 
-    spread.start()
+    spread.start(0)
+    for ex in range(2):
+        for cp in weights(ex):
+            cp.start()
+    g_copy(0).start()
     gb_in[...] = jnp.zeros_like(gb_in)
     gb_back[...] = jnp.zeros_like(gb_back)
     own.wait()
-    spread.pass_on(0)
-    spread.pass_on(1)
-    spread.pass_y(0)
-    spread.pass_on(2)
-    spread.pass_y(1)
-
-    n_steps = n_chunks * lc
-
-    @pl.loop(0, n_steps)
-    def _(i):
-        j, ex = lax.div(i, lc), lax.rem(i, lc)
-        slot = lax.rem(i, 2)
-        base = base_of(i)
-
-        @pl.when(i + 1 < n_steps)
-        def _():
-            g_copy(i + 1).start()
-
-        @pl.when(ex == 0)
-        def _():
-            spread.landed(2 * j)
-            spread.landed(2 * j + 1)
-
-            @pl.when(j >= 2)
+    spread.pass_on(0, 0)
+    spread.start(1)
+    spread.pass_on(0, 1)
+    spread.pass_y(0, 0)
+
+    def weight_grads(ex, after):
+        slot = lax.rem(ex, 2)
+
+        @pl.loop(0, width // step_w)
+        def _(i):
+            cols = pl.ds(pl.multiple_of(i * step_w, step_w), step_w)
+            x = land[ex, :, :, :, cols].reshape(n_exp * n_hid * cap, step_w)
+            piece = mm_tn(x, gp_v[slot].reshape(n_exp * n_hid * cap, ff)).astype(BF)
+
+            @pl.when(i > 0)
             def _():
-                gather.over_core(2 * j - 4).wait_send()
-                gather.over_core(2 * j - 3).wait_send()
-
-        @pl.when(j == 0)
-        def _():
-            for cp in weights(ex):
-                cp.wait()
-
-        x_copy(i).start()
-        g_copy(i).wait()
-
-        @pl.when(i >= 2)
-        def _():
-            for cp in out_copies(i - 2):
-                cp.wait()
-
-        x = land[ex, pl.ds(base, 2)].reshape(count, width)
-        g = g_v[slot].reshape(count, width)
-        gb_back[pl.ds(ex, 1)] += jnp.sum(g.astype(F32), axis=0, keepdims=True)
-        hs, gps = [], []
-        for f in range(ff // step_f):
-            cols = slice(f * step_f, (f + 1) * step_f)
-            pre = mm(x, win_v[ex, :, cols]) + bias_in[pl.ds(ex, 1), cols]
-            sig = jax.nn.sigmoid(pre)
-            hid = (pre * sig).astype(BF)
-            gh = mm_nt(g, wback_v[ex, cols, :])
-            gp = (gh * sig * (1.0 + pre * (1.0 - sig))).astype(BF)
-            gb_in[pl.ds(ex, 1), cols] += jnp.sum(gp.astype(F32), axis=0, keepdims=True)
-            h_v[slot, :, :, cols] = hid.reshape(2, n_hid * cap, step_f)
-            gp_v[slot, :, :, cols] = gp.reshape(2, n_hid * cap, step_f)
-        gpv = gp_v[slot].reshape(count, ff)
-        gd = mm_nt(gpv, win_v[ex])
-        part[lax.rem(j, 2), ex] = gd.astype(BF).reshape(2, n_y, 2, cap, width)
-        hv = h_v[slot].reshape(count, ff)
-        f_v[slot] = mm(hv, wback_v[ex]).astype(BF).reshape(2, n_y, 2, cap, width)
-        for cp in out_copies(i):
-            cp.start()
-
+                wi_copy(ex, i).wait()
+
+            wi_st[...] = piece
+            wi_copy(ex, i).start()
+            after(i)
+
+        @pl.loop(0, ff // step_w)
+        def _(i):
+            cols = pl.ds(pl.multiple_of(i * step_w, step_w), step_w)
+            hid = h_v[slot, :, :, cols].reshape(n_exp * n_hid * cap, step_w)
+            piece = mm_tn(hid, g_v[slot].reshape(n_exp * n_hid * cap, width)).astype(BF)
+
+            @pl.when(i > 0)
+            def _():
+                wb_copy(ex, i).wait()
+
+            wb_st[...] = piece
+            wb_copy(ex, i).start()
+
+        wi_copy(ex, 0).wait()
+        wb_copy(ex, 0).wait()
+
+    @pl.loop(0, lc)
+    def _(ex):
+        slot = lax.rem(ex, 2)
+        g_copy(ex).wait()
+        for cp in weights(ex):
+            cp.wait()
+
+        @pl.loop(0, n_rb)
+        def _(rb):
+            at = sources(rb)
+            for b in range(2):
+
+                @pl.when(rb == b * (n_rb // 2))
+                def _():
+                    spread.landed(ex, b)
+
+            x = land[ex, at].reshape(block, width)
+            g = g_v[slot, at].reshape(block, width)
+            gb_back[pl.ds(ex, 1)] += jnp.sum(g.astype(F32), axis=0, keepdims=True)
+            for f in range(ff // step_f):
+                cols = slice(f * step_f, (f + 1) * step_f)
+                pre = mm(x, wi_v[slot, :, cols]) + bias_in[pl.ds(ex, 1), cols]
+                sig = jax.nn.sigmoid(pre)
+                hid = (pre * sig).astype(BF)
+                gh = mm_nt(g, wb_v[slot, cols, :])
+                gp = (gh * sig * (1.0 + pre * (1.0 - sig))).astype(BF)
+                gb_in[pl.ds(ex, 1), cols] += jnp.sum(gp.astype(F32), axis=0, keepdims=True)
+                h_v[slot, at, :, cols] = hid.reshape(n_src, n_hid * cap, step_f)
+                gp_v[slot, at, :, cols] = gp.reshape(n_src, n_hid * cap, step_f)
+            gd = mm_nt(gp_v[slot, at].reshape(block, ff), wi_v[slot])
+            part[at] = gd.astype(BF).reshape(n_src, n_y, 2, cap, width)
+
+            for b in range(2):
+
+                @pl.when(rb == (b + 1) * (n_rb // 2) - 1)
+                def _():
+                    gather.over_core(ex, b).start()
+
+                    if b == 0:
+
+                        @pl.when(ex == 0)
+                        def _():
+                            spread.pass_y(0, 1)
+
+                        @pl.when(ex + 2 < lc)
+                        def _():
+                            spread.start(ex + 2)
+
+                    @pl.when(ex + 1 < lc)
+                    def _():
+                        spread.pass_on(ex + 1, b)
+
+                    @pl.when(ex > 0)
+                    def _():
+                        gather.step_exp(ex - 1, b)
+
+        @pl.loop(0, n_rb)
+        def _(rb):
+            hv = h_v[slot, sources(rb)].reshape(block, ff)
+            f = mm(hv, wb_v[slot]).astype(BF).reshape(n_src, n_y, 2, cap, width)
+
+            @pl.when((ex > 0) | (rb > 0))
+            def _():
+                f_copy(ex, rb).wait()
+
+            f_v[...] = f
+            f_copy(ex, rb).start()
+
+            for b in range(2):
+
+                @pl.when(rb == (b + 1) * (n_rb // 2) - 1)
+                def _():
+                    gather.fold(ex, b)
+
+                    @pl.when(ex + 1 < lc)
+                    def _():
+                        spread.pass_y(ex + 1, b)
+
+        @pl.when(ex + 2 < lc)
+        def _():
+            for cp in weights(ex + 2):
+                cp.start()
+
+        @pl.when(ex > 0)
+        def _():
+            weight_grads(ex - 1, lambda i: None)
+
+        @pl.when(ex + 1 < lc)
+        def _():
+            g_copy(ex + 1).start()
+
+    def last(i):
         @pl.when(i == 0)
         def _():
-            spread.pass_y(2)
-            spread.pass_on(3)
-
-        @pl.when(i == 1)
-        def _():
-            spread.pass_y(3)
-
-        @pl.when((i >= 2) & (lax.rem(i, 2) == 0) & (lax.div(i, 2) + 3 < n_exp))
-        def _():
-            spread.pass_on(lax.div(i, 2) + 3)
-
-            @pl.when(i == 2 * (n_exp - 4))
-            def _():
-                gather.send_y(0)
-                gather.send_y(1)
-
-        @pl.when((i >= 3) & (lax.rem(i, 2) == 1) & (lax.div(i, 2) + 3 < n_exp))
-        def _():
-            spread.pass_y(lax.div(i, 2) + 3)
-
-        @pl.when((j >= 1) & (ex == 0))
-        def _():
-            gather.fold(2 * j - 2, 2 * j - 2)
-
-        @pl.when((j >= 1) & (ex == 1))
-        def _():
-            gather.fold(2 * j - 1, 2 * j - 1)
-
-            @pl.when(j >= 2)
-            def _():
-                gather.send_y(2 * j - 2)
-                gather.send_y(2 * j - 1)
-
-        @pl.when((j >= 3) & (ex == 2))
-        def _():
-            gather.step_exp(2 * j - 4)
-
-        @pl.when(ex == lc - 1)
-        def _():
-            @pl.when(j >= 3)
-            def _():
-                gather.step_exp(2 * j - 3)
-
-            gather.step_core(2 * j)
-            gather.step_core(2 * j + 1)
-
-    for k in (n_exp - 2, n_exp - 1):
-        gather.fold(k, k)
-        gather.send_y(k)
-    for k in (*range(n_exp - 4, n_exp), 0, 1):
-        gather.step_exp(k)
-
-    for k in range(n_exp - 4, n_exp):
-        gather.over_core(k).wait_send()
-    for i in (n_steps - 2, n_steps - 1):
-        for cp in out_copies(i):
-            cp.wait()
-
-    @pl.loop(0, n_steps)
-    def _(i):
-        x_copy(i).wait()
-
-    @pl.loop(0, n_exp)
-    def _(k):
-        spread.sent(k)
-        gather.finish(k)
+            gather.step_exp(lc - 1, 0)
+
+    weight_grads(lc - 1, last)
+    gather.step_exp(lc - 1, 1)
+    f_copy(lc - 1, 0).wait()
+
+    @pl.loop(0, lc)
+    def _(ex):
+        spread.sent(ex)
+        gather.finish(ex)
 
 
 def experts(n_exp, n_hid, rows, grads, w_in, bias_in, w_back):
@@ -619,80 +757,78 @@
     ff = w_in.shape[2]
     shape = jax.ShapeDtypeStruct
     per = n_hid * cap
-    n_steps = n_exp // 2 * lc
     return pl.pallas_call(
         functools.partial(expert_kernel, n_exp, n_y),
         name="experts",
         out_shape=(
             shape((n_exp, lc, cap, width), BF),
-            shape((lc, n_exp, n_hid, cap, width), BF),
-            shape((lc, n_exp, per, ff), BF),
-            shape((lc, n_exp, per, ff), BF),
             shape((lc, n_exp, n_y, 2, cap, width), BF),
+            shape(w_in.shape, BF),
+            shape(w_back.shape, BF),
             shape((lc, ff), F32),
             shape((lc, width), F32),
         ),
-        in_specs=[VM, HB, HB, VM, HB],
-        out_specs=[VM, HB, HB, HB, HB, VM, VM],
+        in_specs=[HB, HB, HB, VM, HB],
+        out_specs=[HB, HB, HB, HB, VM, VM],
         scratch_shapes=[
             pltpu.VMEM((lc, n_exp, n_hid, cap, width), BF),
-            pltpu.VMEM((2, lc, 2, n_y, 2, cap, width), BF),
-            pltpu.VMEM(w_in.shape, BF),
-            pltpu.VMEM(w_back.shape, BF),
-            pltpu.VMEM((2, 2, n_hid, cap, width), BF),
-            pltpu.VMEM((2, 2, per, ff), BF),
-            pltpu.VMEM((2, 2, per, ff), BF),
-            pltpu.VMEM((2, 2, n_y, 2, cap, width), BF),
-            DMA((2, lc)), DMA((2,)), DMA((3, 2)), DMA((n_steps,)), DMA,
-            *Gather.scratch(n_exp, n_y, lc, cap, width),
-            *Spread.sems(n_exp, n_y),
-            *Gather.sems(n_exp, n_y),
+            pltpu.VMEM((n_exp, n_y, 2, cap, width), BF),
+            pltpu.VMEM((lc, n_exp, n_y, cap, width), BF),
+            pltpu.VMEM((n_y - 1, lc, n_exp, cap, width), BF),
+            pltpu.VMEM((2, *w_in.shape[1:]), BF),
+            pltpu.VMEM((2, *w_back.shape[1:]), BF),
+            pltpu.VMEM((2, n_exp, n_hid, cap, width), BF),
+            pltpu.VMEM((2, n_exp, per, ff), BF),
+            pltpu.VMEM((2, n_exp, per, ff), BF),
+            pltpu.VMEM((4, n_y, 2, cap, width), BF),
+            pltpu.VMEM((STEP_W, ff), BF),
+            pltpu.VMEM((STEP_W, width), BF),
+            DMA((2, 2)), DMA((2,)), DMA, DMA((2,)), DMA,
+            *SpreadExpert.sems(lc, n_exp, n_y),
+            *GatherExpert.sems(lc, n_exp, n_y),
         ],
         compiler_params=pltpu.CompilerParams(
-            collective_id=1, has_side_effects=True, vmem_limit_bytes=62 * MIB
+            collective_id=1, has_side_effects=True, vmem_limit_bytes=63 * MIB
         ),
     )(rows, grads, w_in, bias_in, w_back)
 
 
-def finish_kernel(x, gp, h, g, mats, g_in, g_back, g_qkv, g_out):
-    g_in[0] = mm_tn(x[0], gp[0])
-    g_back[0] = mm_tn(h[0], g[0])
+def finish_kernel(wi, wb, mats, g_in, g_back, g_qkv, g_out):
+    g_in[...] = wi[...].astype(F32)
+    g_back[...] = wb[...].astype(F32)
     rows, width = g_out.shape
     for part in range(3):
         g_qkv[:, part * width : (part + 1) * width] = mats[part].reshape(rows, width).astype(F32)
     g_out[...] = mats[3].reshape(rows, width).astype(F32)
 
 
-def finish(x, gp, h, g, mats):
-    lc, n, width = x.shape
-    ff = gp.shape[2]
+def finish(wi, wb, mats):
+    lc, width, ff = wi.shape
     cut = 2
     rows = width // (lc * cut)
     mats = mats.reshape(4, width // 16, 16, width)
     shape = jax.ShapeDtypeStruct
+    wi_spec = pl.BlockSpec((1, width // cut, ff), lambda i, j: (i, j, 0))
+    wb_spec = pl.BlockSpec((1, ff // cut, width), lambda i, j: (i, j, 0))
     return pl.pallas_call(
         finish_kernel,
         name="finish",
         grid=(lc, cut),
         out_shape=(
-            shape((lc, width, ff), F32), shape((lc, ff, width), F32),
+            shape(wi.shape, F32), shape(wb.shape, F32),
             shape((width, 3 * width), F32), shape((width, width), F32),
         ),
         in_specs=[
-            pl.BlockSpec((1, n, width), lambda i, j: (i, 0, 0)),
-            pl.BlockSpec((1, n, ff // cut), lambda i, j: (i, 0, j)),
-            pl.BlockSpec((1, n, ff), lambda i, j: (i, 0, 0)),
-            pl.BlockSpec((1, n, width // cut), lambda i, j: (i, 0, j)),
+            wi_spec, wb_spec,
             pl.BlockSpec((4, rows // 16, 16, width), lambda i, j: (0, i * cut + j, 0, 0)),
         ],
         out_specs=[
-            pl.BlockSpec((1, width, ff // cut), lambda i, j: (i, 0, j)),
-            pl.BlockSpec((1, ff, width // cut), lambda i, j: (i, 0, j)),
+            wi_spec, wb_spec,
             pl.BlockSpec((rows, 3 * width), lambda i, j: (i * cut + j, 0)),
             pl.BlockSpec((rows, width), lambda i, j: (i * cut + j, 0)),
         ],
         compiler_params=pltpu.CompilerParams(vmem_limit_bytes=56 * MIB),
-    )(x, gp, h, g, mats)
+    )(wi, wb, mats)
 
 
 def attend_back_kernel(
@@ -1166,7 +1302,7 @@
     mixed, context, middle, lse, send, grads = attend(
         n_exp, n_hid, lc, cap, lengths, slot[None], tokens, gain1, shift1, w_qkv, w_out, gain2, shift2, cotangent
     )
-    back, x, hid, gp, f_part, gb_in, gb_back = experts(
+    back, f_part, wi, wb, gb_in, gb_back = experts(
         n_exp, n_hid, send, grads, w_in, bias_in, w_back
     )
     output, g_tokens, mats, norms = attend_back(
@@ -1174,11 +1310,7 @@
         gain1, shift1, w_qkv, w_out, gain2, bias_back, f_part,
     )
     mats, norms = reduce_all(n_exp, n_hid, mats, norms)
-    n_rows = n_exp * n_hid * cap
-    g_in, g_back, g_qkv, g_out = finish(
-        x.reshape(lc, n_rows, width), gp.reshape(lc, n_rows, ff),
-        hid.reshape(lc, n_rows, ff), grads.reshape(lc, n_rows, width), mats,
-    )
+    g_in, g_back, g_qkv, g_out = finish(wi, wb, mats)
     return (
         output, g_tokens, norms[0], norms[1], g_qkv, g_out, norms[2], norms[3],
         g_in, gb_in, g_back, gb_back,

time: 441 us -> 418 us (0.948)
  Pallas kernels: 429 us -> 406 us
    pallas_call x1, Pallas kernels: 38.6 us -> 26.8 us  [finish(): pl.pallas_call(finish_kernel, name='finish', grid=(lc, cut), out_shape=(s...]
    pallas_call x1, Pallas kernels: 81.1 us -> 71.7 us  [attend_back(): pl.pallas_call(functools.partial(attend_back_kernel, n_exp, n_y), name='a...]
where the time goes in v4:
time: 418 us; the launch traced here: 417 us
  Pallas kernels  406 us (97%)
  local copies, waits for them, and re-layouts  8.95 us (2%)
    pallas_call x1, Pallas kernels, experts(): pl.pallas_call(functools.partial(expert_kernel, n_exp, n_y), name='expert...  136 us
    pallas_call x1, Pallas kernels, reduce_all(): pl.pallas_call(functools.partial(reduce_kernel, n_x, n_y, n_z), name='red...  104 us
    pallas_call x1, Pallas kernels, attend_back(): pl.pallas_call(functools.partial(attend_back_kernel, n_exp, n_y), name='a...  71.7 us
    pallas_call x1, Pallas kernels, attend(): pl.pallas_call(functools.partial(attend_kernel, n_exp, n_y), name='attend...  67.5 us
    pallas_call x1, Pallas kernels, finish(): pl.pallas_call(finish_kernel, name='finish', grid=(lc, cut), out_shape=(s...  26.8 us

profile of v4, /device:TPU:0, one launch (start us, length us, event | category | flops | bytes accessed | tf_op | source)
XLA Modules:
  0.0 417.4 jit_solution(4226894154299368971)
XLA Ops:
  0.6 0.0 copy-start
  0.7 0.7 pad_clamp_fusion
  1.4 0.1 copy-done
  1.4 3.1 gather_fusion
  4.6 0.2 convert_reduce_fusion
  4.8 0.7 select_reduce_fusion
  5.6 0.0 copy-start.5
  5.6 0.9 copy.29.slot_col
  6.4 0.0 copy-done.5
  6.4 67.5 %attend.1 = (bf16[512,3072]{1,0:T(8,128)(2,1)}, bf16[512,1024]{1,0:T(8,128)(2,1)}, f32[512,1024]{1,0:T(8,128)}, f32[512,128]{1,0:T(8,128)}, bf16[8,4,32,1024]{3,...) custom-call(s32[1,2]{1,0:T(1,128)} %lens.3, s32[1,512]{1,0:T(1,128)} %bitcast.15, bf16[512,1024]{1,0:T(8,128)(2,1)} %tokens_h.1, ...), custom_call_target="tpu_custom_call" | custom-call | tf_op jit(solution)/shard_map/attend/pallas_call | solution.py:383
  73.9 136.2 %experts.1 = (bf16[8,4,32,1024]{3,2,1,0:T(8,128)(2,1)}, bf16[4,8,2,2,32,1024]{5,4,3,2,1,0:T(8,128)(2,1)}, bf16[4,1024,1024]{2,1,0:T(8,128)(2,1)}, bf16[4,1024,10...) custom-call(bf16[8,4,32,1024]{3,2,1,0:T(8,128)(2,1)} %get-tuple-element.38.rows, ...), custom_call_target="tpu_custom_call" | custom-call | tf_op jit(solution)/shard_map/experts/pallas_call | solution.py:760
  210.2 71.7 %attend_back.1 = (bf16[512,1024]{1,0:T(8,128)(2,1)}, f32[512,1024]{1,0:T(8,128)}, bf16[4,64,16,1024]{3,2,1,0:T(8,128)(2,1)}, f32[8,1024]{1,0:T(8,128)}) custom-call(s32[1,2]{1,0:T(1,128)} %lens.3, s32[512,1]{1,0:T(8,128)} %copy.29.slot_col, bf16[512,1024]{1,0:T(8,128)(2,1)} %tokens_h.1, f32[512,1024]{1,0:T(8,128)} %get-tuple-element.34.middle_h, ...), custom_call_target="tpu_custom_call" | custom-call | tf_op jit(solution)/shard_map/attend_back/pallas_call | solution.py:1033
  281.9 0.0 copy-start.2
  281.9 0.7 copy-done.2
  282.6 103.8 %reduce_all.1 = (bf16[256,16,1024]{2,1,0:T(8,128)(2,1)}, f32[8,1024]{1,0:T(8,128)S(1)}) custom-call(bf16[256,16,1024]{2,1,0:T(8,128)(2,1)} %bitcast.13, f32[8,1024]{1,0:T(8,128)S(1)} %copy-done.2), custom_call_target="tpu_custom_call" | custom-call | tf_op jit(solution)/shard_map/reduce_all/pallas_call | solution.py:1256
  386.5 0.6 fusion.1
  387.1 0.0 copy-start.6
  387.1 0.0 copy-start.1
  387.1 26.8 %finish.1 = (f32[4,1024,1024]{2,1,0:T(8,128)}, f32[4,1024,1024]{2,1,0:T(8,128)}, f32[1024,3072]{1,0:T(8,128)}, f32[1024,1024]{1,0:T(8,128)}) custom-call(bf16[4,1024,1024]{2,1,0:T(8,128)(2,1)} %get-tuple-element.47.wi, bf16[4,1024,1024]{2,1,0:T(8,128)(2,1)} %get-tuple-element.48.wb, bf16[4,64,16,1024]{3,2,1,0:T(8,128)(2,1)} %bitcast.12), custom_call_target="tpu_custom_call" | custom-call | tf_op jit(solution)/shard_map/finish/pallas_call | solution.py:813
  413.9 0.0 copy-done.4
  413.9 1.0 copy.34
  414.9 1.3 copy.35
  416.2 0.6 copy.36
  416.8 0.6 copy.37
  (8 shorter events, 0.0 us)
Async XLA Ops:
  0.6 0.8 copy-start
  5.6 0.9 copy-start.5
  281.9 0.8 copy-start.2
  387.1 26.8 %copy-start.4 = (bf16[512,1024]{1,0:T(8,128)(2,1)S(1)}, bf16[512,1024]{1,0:T(8,128)(2,1)}, u32[]{:S(2)}) copy-start(bf16[512,1024]{1,0:T(8,128)(2,1)} %get-tuple-element.72) | copy-start | bytes 3145732
  387.1 27.8 %copy-start.3 = (f32[512,1024]{1,0:T(8,128)S(1)}, f32[512,1024]{1,0:T(8,128)}, u32[]{:S(2)}) copy-start(f32[512,1024]{1,0:T(8,128)} %get-tuple-element.73) | copy-start | bytes 6291460
  387.1 29.1 %copy-start.7 = (f32[4,1024]{1,0:T(4,128)S(1)}, f32[4,1024]{1,0:T(4,128)}, u32[]{:S(2)}) copy-start(f32[4,1024]{1,0:T(4,128)} %get-tuple-element.81) | copy-start | bytes 49156
  387.1 29.7 %copy-start.6 = (f32[4,1024]{1,0:T(4,128)S(1)}, f32[4,1024]{1,0:T(4,128)}, u32[]{:S(2)}) copy-start(f32[4,1024]{1,0:T(4,128)} %get-tuple-element.83) | copy-start | bytes 49156
  387.1 30.3 %copy-start.1 = (s32[8008]{0:T(1024)S(1)}, s32[8008]{0:T(1024)}, u32[]{:S(2)}) copy-start(s32[8008]{0:T(1024)} %param.19) | copy-start | bytes 96100

commit v5 on v4

--- a/solution.py
+++ b/solution.py
@@ -188,14 +188,13 @@
             self.pairs[t, :, self.y] = total
             self.over_exp(k).start()
 
-    def finish(self, k):
+    def sent(self, k):
         for d in range(1, self.n_y):
             self.over_y(k, d).wait_send()
 
         @pl.when(k > 0)
         def _():
             self.over_exp(k).wait_send()
-            self.over_exp(k).wait_recv()
 
 
 def norm_rows(rows, gain, shift):
@@ -831,22 +830,236 @@
     )(wi, wb, mats)
 
 
+class Reduce:
+    def __init__(self, n_exp, n_y, mats, out, norms, scratch):
+        (self.core_in, in1, in2, in3, self.n_acc, self.n_in, self.c_s, self.c_r,
+         s1, r1, s2, r2, s3, r3, t3, u3, t2, u2, t1, u1, self.d_s, self.d_r, self.n_s, self.n_r, self.l_s) = scratch
+        self.mats, self.out, self.norms = mats, out, norms
+        self.e, self.h, self.y, self.c = place()
+        self.n_x, self.n_z, self.sub, self.half, self.n_sub = self.sizes(n_exp, n_y, mats.shape[0])
+        x, z = lax.rem(self.e, self.n_x), lax.div(self.e, self.n_x)
+        self.x, self.z = x, z
+        self.piece = self.half // 2
+        self.at = {"x": (self.n_x, x), "y": (n_y, self.y), "z": (self.n_z, z)}
+        self.orders = (("y", "x", "z"), ("x", "y", "z"))
+        self.n_axes = (None, "y", "x", "z")
+        self.sibling = (self.e, self.y * 2 + 1 - self.c)
+        self.lands = (in1, in2, in3)
+        self.sends, self.recvs = (s1, s2, s3), (r1, r2, r3)
+        self.ups, self.upr = (t1, t2, t3), (u1, u2, u3)
+
+    @staticmethod
+    def sizes(n_exp, n_y, n_units):
+        n_x = n_y
+        n_z = n_exp // n_x
+        sub = n_x * n_y * n_z
+        half = n_units // 2
+        return n_x, n_z, sub, half, half // 2 // sub
+
+    @classmethod
+    def scratch(cls, n_exp, n_y, n_units, norms_shape):
+        n_x, n_z, sub, half, n_sub = cls.sizes(n_exp, n_y, n_units)
+        most = max(n_x, n_y)
+        width = norms_shape[1]
+
+        def land(n, count):
+            return pltpu.VMEM((2, n_sub, n - 1, count, 16, width), BF)
+
+        def sems(n):
+            return [DMA((2, n_sub, n - 1))] * 2
+
+        return [
+            pltpu.VMEM((half, 16, width), BF),
+            land(most, sub // min(n_x, n_y)),
+            land(most, sub // (n_x * n_y)),
+            land(n_z, 1),
+            pltpu.VMEM((4, *norms_shape), F32),
+            pltpu.VMEM((4, max(most, n_z) - 1, *norms_shape), F32),
+            DMA((2, n_sub)), DMA((2, n_sub)),
+            *sems(most), *sems(most), *sems(n_z), *sems(n_z), *sems(most), *sems(most),
+            DMA((2, n_sub)), DMA((2, n_sub)),
+            *[DMA((4, max(most, n_z) - 1))] * 2,
+            DMA((2, n_sub)),
+        ]
+
+    def device(self, axis, o):
+        return {
+            "x": (self.z * self.n_x + o, self.h), "y": (self.e, o * 2 + self.c), "z": (o * self.n_x + self.x, self.h)
+        }[axis]
+
+    def own(self, first, count):
+        return pl.ds(self.c * self.half + first, count)
+
+    def units(self, p, b, depth):
+        first, count = p * self.piece + b * self.sub, self.sub
+        for axis in self.orders[p][:depth]:
+            n, i = self.at[axis]
+            count = count // n
+            first = first + i * count
+        return first, count
+
+    def core_copy(self, p, b):
+        first = p * self.piece + b * self.sub
+        return rcopy(
+            self.mats.at[pl.ds((1 - self.c) * self.half + first, self.sub)], self.core_in.at[pl.ds(first, self.sub)],
+            self.c_s.at[p, b], self.c_r.at[p, b], self.sibling,
+        )
+
+    def down(self, p, b, stage, d):
+        n, i = self.at[self.orders[p][stage]]
+        first, count = self.units(p, b, stage)
+        count = count // n
+        o = lax.rem(i + d, n)
+        return rcopy(
+            self.mats.at[self.own(first + o * count, count)], self.lands[stage].at[p, b, d - 1, pl.ds(0, count)],
+            self.sends[stage].at[p, b, d - 1], self.recvs[stage].at[p, b, d - 1],
+            self.device(self.orders[p][stage], o),
+        )
+
+    def up(self, p, b, stage, d):
+        n, i = self.at[self.orders[p][stage]]
+        at = self.own(*self.units(p, b, stage + 1))
+        source = self.mats if stage == 2 else self.out
+        o = lax.rem(i + d, n)
+        return rcopy(
+            source.at[at], self.out.at[at], self.ups[stage].at[p, b, d - 1], self.upr[stage].at[p, b, d - 1],
+            self.device(self.orders[p][stage], o),
+        )
+
+    def stay(self, p, b):
+        at = self.own(*self.units(p, b, 3))
+        return pltpu.make_async_copy(self.mats.at[at], self.out.at[at], self.l_s.at[p, b])
+
+    def core_up(self, p, b):
+        region = self.out.at[self.own(p * self.piece + b * self.sub, self.sub)]
+        return rcopy(region, region, self.d_s.at[p, b], self.d_r.at[p, b], self.sibling)
+
+    def peers(self, p, stage):
+        return range(1, self.at[self.orders[p][stage]][0])
+
+    def event(self, p, b, q):
+        mats = self.mats
+        if q == 0:
+            self.core_copy(p, b).wait_recv()
+            first = p * self.piece + b * self.sub
+            at = self.own(first, self.sub)
+            mats[at] = (mats[at].astype(F32) + self.core_in[pl.ds(first, self.sub)].astype(F32)).astype(BF)
+        elif q <= 3:
+            first, count = self.units(p, b, q)
+            at = self.own(first, count)
+            total = mats[at].astype(F32)
+            for d in self.peers(p, q - 1):
+                self.down(p, b, q - 1, d).wait_recv()
+                total = total + self.lands[q - 1][p, b, d - 1, :count].astype(F32)
+            mats[at] = total.astype(BF)
+            if q == 3:
+                self.stay(p, b).start()
+        else:
+            if q == 4:
+                self.stay(p, b).wait()
+            for d in self.peers(p, 6 - q):
+                self.up(p, b, 6 - q, d).wait_recv()
+        if q < 3:
+            for d in self.peers(p, q):
+                self.down(p, b, q, d).start()
+        elif q < 6:
+            for d in self.peers(p, 5 - q):
+                self.up(p, b, 5 - q, d).start()
+        else:
+            self.core_up(p, b).start()
+
+    def begin(self, part):
+        @pl.when(self.c == 1 - part // 2)
+        def _():
+            @pl.loop(0, self.n_sub)
+            def _(b):
+                self.core_copy(part % 2, b).start()
+
+    def n_copy(self, stage, d):
+        if stage == 0:
+            dev = self.sibling
+        else:
+            n, i = self.at[self.n_axes[stage]]
+            dev = self.device(self.n_axes[stage], lax.rem(i + d, n))
+        return rcopy(
+            self.n_acc.at[stage], self.n_in.at[stage, d - 1], self.n_s.at[stage, d - 1], self.n_r.at[stage, d - 1], dev
+        )
+
+    def n_peers(self, stage):
+        return range(1, 2 if stage == 0 else self.at[self.n_axes[stage]][0])
+
+    def n_total(self, stage):
+        for d in self.n_peers(stage):
+            self.n_copy(stage, d).wait_recv()
+        own = self.n_acc[stage]
+        if stage == 0:
+            return own + self.n_in[0, 0]
+        n, i = self.at[self.n_axes[stage]]
+        total = jnp.zeros_like(own)
+        for m in range(n):
+            term = own
+            for d in range(1, n):
+                term = jnp.where(lax.rem(i + n - d, n) == m, self.n_in[stage, d - 1], term)
+            total = total + term
+        return total
+
+    def run(self, aside):
+        self.n_acc[0] = self.norms[...]
+        self.n_copy(0, 1).start()
+
+        @pl.loop(0, self.n_sub + 6)
+        def _(s):
+            for q in range(7):
+
+                @pl.when((s >= q) & (s - q < self.n_sub))
+                def _():
+                    for p in range(2):
+                        self.event(p, s - q, q)
+
+            for stage in range(1, 4):
+
+                @pl.when(s == stage)
+                def _():
+                    self.n_acc[stage] = self.n_total(stage - 1)
+                    for d in self.n_peers(stage):
+                        self.n_copy(stage, d).start()
+
+            aside(s)
+
+        self.norms[...] = self.n_total(3)
+        for stage in range(4):
+            for d in self.n_peers(stage):
+                self.n_copy(stage, d).wait_send()
+
+        @pl.loop(0, self.n_sub)
+        def _(b):
+            for p in range(2):
+                self.core_up(p, b).wait_recv()
+                self.core_copy(p, b).wait_send()
+                self.core_up(p, b).wait_send()
+                for stage in range(3):
+                    for d in self.peers(p, stage):
+                        self.down(p, b, stage, d).wait_send()
+                        self.up(p, b, stage, d).wait_send()
+
+
 def attend_back_kernel(
     n_exp, n_y, lens, slot_col, tokens_h, middle_h, cot_h, mixed_h, context_h, lse, back_h,
     gain1, shift1, w_qkv_h, w_out_h, gain2, bias_back, f_part,
-    output, g_tokens, g_mats, g_norms,
-    tokens, middle, cot, mixed, context, back, w_qkv, w_out,
-    bias, gm, gattn, gctx, gmixed, n1t, lse_t, mine_v, f_back, mine_sem, in_sem, *rest,
+    output, g_tokens, mats_out, g_norms,
+    tokens, middle, cot, mixed, context, back, w_qkv, w_out, g_mats,
+    bias, gattn, gctx, n1t, lse_t, mine_v, f_back, mine_sem, in_sem, *rest,
 ):
     tok, width = tokens.shape
     hd = width // HEADS
     e, h, y, c = place()
-    n_gather = len(Gather.scratch(1, 2, 1, 1, 1))
+    n_gather, n_sems = len(Gather.scratch(1, 2, 1, 1, 1)), len(Gather.sems(1, 1))
     lc, cap = f_back.shape[1:3]
     gather = Gather(
         n_exp, n_y, lambda k: f_part.at[:, e ^ k, :, 1 - c], lambda m, yy: mine_v[lax.rem(m, 4), :, yy],
-        *rest[:n_gather], f_back, rest[n_gather:],
+        *rest[:n_gather], f_back, rest[n_gather : n_gather + n_sems],
     )
+    total = Reduce(n_exp, n_y, g_mats, mats_out, g_norms, rest[n_gather + n_sems :])
 
     def order(m):
         return jnp.where(m < n_exp // 2, m + n_exp // 2, n_exp - 1 - m)
@@ -891,6 +1104,7 @@
 
     g_norms[...] = jnp.zeros_like(g_norms)
     n_slots = n_exp * lc * cap
+    n_quarter = width // 16
 
     def fold(values):
         return jnp.sum(values, axis=0, keepdims=True)
@@ -904,7 +1118,7 @@
         g_norms[2:3] += fold(up * unit)
         g_norms[3:4] += fold(up)
         g_mid = cot[rows].astype(F32) + norm_back(up, unit, inverse, gain2[...])
-        gm[rows] = g_mid
+        g_tokens[rows] = g_mid
         gattn[rows] = g_mid.astype(BF)
         gctx[rows] = mm_nt(gattn[rows], w_out[...]).astype(BF)
         out, _, _ = norm_rows(tokens[rows].astype(F32), gain1[...], shift1[...])
@@ -919,8 +1133,9 @@
     def _(i):
         cols = pl.ds(pl.multiple_of(i * 256, 256), 256)
         part = mm_tn(context[:, cols], gattn[...]).astype(BF)
-        g_mats[3, pl.ds(i * 16, 16)] = part.reshape(16, 16, width)
-
+        g_mats[pl.ds(3 * n_quarter + i * 16, 16)] = part.reshape(16, 16, width)
+
+    total.begin(3)
     key_i = lax.broadcasted_iota(jnp.int32, (tok, tok), 0)
     qry_i = lax.broadcasted_iota(jnp.int32, (tok, tok), 1)
     dk_, dq_ = jnp.zeros((tok, tok), jnp.int32), jnp.zeros((tok, tok), jnp.int32)
@@ -977,49 +1192,71 @@
                 dq[qb] = dq[qb] + mm_tn(ds, kh[:n])
         for b in range(2):
             rows = slice(b * half, (b + 1) * half)
-            gmixed[rows, cols(0)] = dq[b].astype(BF)
-            gmixed[rows, cols(1)] = dkey[b].astype(BF)
-            gmixed[rows, cols(2)] = dval[b].astype(BF)
-
-    gather.step_exp(order(3), bias_back[...].reshape(lc, 1, width))
+            mixed[rows, cols(0)] = dq[b].astype(BF)
+            mixed[rows, cols(1)] = dkey[b].astype(BF)
+            mixed[rows, cols(2)] = dval[b].astype(BF)
+
+    def step_exp(m):
+        gather.step_exp(order(m), bias_back[...].reshape(lc, 1, width))
+
+    step_exp(3)
+    for part in range(3):
+
+        @pl.loop(0, width // 256)
+        def _(i):
+            rows = pl.ds(pl.multiple_of(i * 256, 256), 256)
+            piece = mm(n1t[rows], mixed[:, part * width : (part + 1) * width])
+            g_mats[pl.ds(part * n_quarter + i * 16, 16)] = piece.astype(BF).reshape(16, 16, width)
+
+        total.begin(part)
+
+    @pl.loop(n_pairs + 4, max(n_exp, n_pairs + 4))
+    def _(m):
+        leave(m)
+
+    step_exp(4)
 
     @pl.loop(0, tok // 256)
     def _(i):
         rows = pl.ds(pl.multiple_of(i * 256, 256), 256)
-        up = mm_nt(gmixed[rows], w_qkv[...])
+        up = mm_nt(mixed[rows], w_qkv[...])
         _, unit, inverse = norm_rows(tokens[rows].astype(F32), gain1[...], 0.0)
         g_norms[0:1] += fold(up * unit)
         g_norms[1:2] += fold(up)
-        g_tokens[rows] = gm[rows] + norm_back(up, unit, inverse, gain1[...])
-
-    gather.step_exp(order(4), bias_back[...].reshape(lc, 1, width))
-
-    for part in range(3):
-
-        @pl.loop(0, width // 256)
-        def _(i):
-            rows = pl.ds(pl.multiple_of(i * 256, 256), 256)
-            piece = mm(n1t[rows], gmixed[:, part * width : (part + 1) * width])
-            g_mats[part, pl.ds(i * 16, 16)] = piece.astype(BF).reshape(16, 16, width)
-
-    @pl.loop(n_pairs + 4, max(n_exp, n_pairs + 4))
-    def _(m):
-        leave(m)
-
-    @pl.loop(5, n_exp)
-    def _(m):
-        gather.step_exp(order(m), bias_back[...].reshape(lc, 1, width))
+        g_tokens[rows] += norm_back(up, unit, inverse, gain1[...])
+
+    def aside(s):
+        @pl.when(s == 0)
+        def _():
+            @pl.loop(5, n_exp - 2)
+            def _(m):
+                step_exp(m)
+
+        for j in (1, 2):
+
+            @pl.when(s == j)
+            def _():
+                step_exp(n_exp - 3 + j)
+
+        @pl.when(s == 5)
+        def _():
+            @pl.loop(1, n_exp)
+            def _(k):
+                gather.over_exp(k).wait_recv()
+
+            @pl.loop(0, tok // 256)
+            def _(i):
+                rows = pl.ds(pl.multiple_of(i * 256, 256), 256)
+                table = tok_block(slot_col[rows], 0, n_slots)
+                whole = middle[rows] + mm(table, f_back[...].reshape(n_slots, width))
+                output[rows] = whole.astype(BF)
+
+    total.run(aside)
 
     @pl.loop(0, n_exp)
     def _(k):
         gather.over_core(k).wait_send()
-        gather.finish(k)
-
-    @pl.loop(0, tok // 256)
-    def _(i):
-        rows = pl.ds(pl.multiple_of(i * 256, 256), 256)
-        table = tok_block(slot_col[rows], 0, n_slots)
-        output[rows] = (middle[rows] + mm(table, f_back[...].reshape(n_slots, width))).astype(BF)
+        gather.sent(k)
 
 
 def attend_back(
@@ -1029,6 +1266,7 @@
     n_y = n_hid // 2
     tok, width = tokens.shape
     _, lc, cap, _ = back.shape
+    n_units = 4 * width // 16
     shape = jax.ShapeDtypeStruct
     return pl.pallas_call(
         functools.partial(attend_back_kernel, n_exp, n_y),
@@ -1036,18 +1274,17 @@
         out_shape=(
             shape((tok, width), BF),
             shape((tok, width), F32),
-            shape((4, width // 16, 16, width), BF),
+            shape((n_units, 16, width), BF),
             shape((8, width), F32),
         ),
         in_specs=[SM, VM, HB, HB, HB, HB, HB, VM, HB, VM, VM, HB, HB, VM, VM, HB],
-        out_specs=[VM] * 4,
+        out_specs=[VM, VM, HB, VM],
         scratch_shapes=[
             *[pltpu.VMEM(a.shape, a.dtype) for a in (tokens, middle, cot, mixed, context, back, w_qkv, w_out)],
+            pltpu.VMEM((n_units, 16, width), BF),
             pltpu.VMEM((tok, tok), F32),
-            pltpu.VMEM((tok, width), F32),
             pltpu.VMEM((tok, width), BF),
             pltpu.VMEM((tok, width), BF),
-            pltpu.VMEM((tok, 3 * width), BF),
             pltpu.VMEM((width, tok), BF),
             pltpu.VMEM((128, tok), F32),
             pltpu.VMEM((4, lc, n_y, cap, width), BF),
@@ -1056,227 +1293,15 @@
             DMA((8,)),
             *Gather.scratch(n_exp, n_y, lc, cap, width),
             *Gather.sems(n_exp, n_y),
+            *Reduce.scratch(n_exp, n_y, n_units, (8, width)),
         ],
         compiler_params=pltpu.CompilerParams(
-            collective_id=2, has_side_effects=True, vmem_limit_bytes=62 * MIB
+            collective_id=2, has_side_effects=True, vmem_limit_bytes=63 * MIB
         ),
     )(
         lens, slot_col, tokens, middle, cot, mixed, context, lse, back,
         gain1, shift1, w_qkv, w_out, gain2, bias_back, f_part,
     )
-
-
-def reduce_kernel(
-    n_x, n_y, n_z, mats, norms, out, norms_out,
-    acc, core_in, in1, in2, in3, n_acc, n_in,
-    c_s, c_r, s1, r1, s2, r2, s3, r3, t3, u3, t2, u2, t1, u1, d_s, d_r, n_s, n_r,
-):
-    e, h, y, c = place()
-    x, z = lax.rem(e, n_x), lax.div(e, n_x)
-    sub = n_x * n_y * n_z
-    half = mats.shape[0] // 2
-    piece = half // 2
-    n_sub = piece // sub
-    at = {"x": (n_x, x), "y": (n_y, y), "z": (n_z, z)}
-    orders = (("y", "x", "z"), ("x", "y", "z"))
-    sibling = (e, y * 2 + 1 - c)
-
-    def device(axis, o):
-        return {"x": (z * n_x + o, h), "y": (e, o * 2 + c), "z": (o * n_x + x, h)}[axis]
-
-    sem = pltpu.get_barrier_semaphore()
-    for axis in "xyz":
-        n, i = at[axis]
-        for d in range(1, n):
-            pl.semaphore_signal(sem, inc=1, device_id=device(axis, lax.rem(i + d, n)), device_id_type=MESH)
-    pl.semaphore_signal(sem, inc=1, device_id=sibling, device_id_type=MESH)
-    pl.semaphore_wait(sem, n_x + n_y + n_z - 2)
-
-    def units(p, b, depth):
-        first, count = p * piece + b * sub, sub
-        for axis in orders[p][:depth]:
-            n, i = at[axis]
-            count = count // n
-            first = first + i * count
-        return first, count
-
-    def core_copy(p, b):
-        first = p * piece + b * sub
-        return rcopy(
-            mats.at[pl.ds((1 - c) * half + first, sub)], core_in.at[pl.ds(first, sub)],
-            c_s.at[p, b], c_r.at[p, b], sibling,
-        )
-
-    lands = (in1, in2, in3)
-    sends, recvs = (s1, s2, s3), (r1, r2, r3)
-
-    def down(p, b, stage, d):
-        n, i = at[orders[p][stage]]
-        first, count = units(p, b, stage)
-        count = count // n
-        o = lax.rem(i + d, n)
-        return rcopy(
-            acc.at[pl.ds(first + o * count, count)], lands[stage].at[p, b, d - 1, pl.ds(0, count)],
-            sends[stage].at[p, b, d - 1], recvs[stage].at[p, b, d - 1], device(orders[p][stage], o),
-        )
-
-    ups, upr = (t1, t2, t3), (u1, u2, u3)
-
-    def up(p, b, stage, d):
-        n, i = at[orders[p][stage]]
-        first, count = units(p, b, stage + 1)
-        region = out.at[pl.ds(c * half + first, count)]
-        o = lax.rem(i + d, n)
-        return rcopy(
-            region, region, ups[stage].at[p, b, d - 1], upr[stage].at[p, b, d - 1], device(orders[p][stage], o)
-        )
-
-    def core_up(p, b):
-        region = out.at[pl.ds(c * half + p * piece + b * sub, sub)]
-        return rcopy(region, region, d_s.at[p, b], d_r.at[p, b], sibling)
-
-    def peers(p, stage):
-        return range(1, at[orders[p][stage]][0])
-
-    def event(p, b, q):
-        if q == 0:
-            core_copy(p, b).wait_recv()
-            first = p * piece + b * sub
-            mine = mats[pl.ds(c * half + first, sub)].astype(F32)
-            acc[pl.ds(first, sub)] = (mine + core_in[pl.ds(first, sub)].astype(F32)).astype(BF)
-        elif q <= 3:
-            first, count = units(p, b, q)
-            total = acc[pl.ds(first, count)].astype(F32)
-            for d in peers(p, q - 1):
-                down(p, b, q - 1, d).wait_recv()
-                total = total + lands[q - 1][p, b, d - 1, :count].astype(F32)
-            if q < 3:
-                acc[pl.ds(first, count)] = total.astype(BF)
-            else:
-                out[pl.ds(c * half + first, count)] = total.astype(BF)
-        else:
-            for d in peers(p, 6 - q):
-                up(p, b, 6 - q, d).wait_recv()
-        if q < 3:
-            for d in peers(p, q):
-                down(p, b, q, d).start()
-        elif q < 6:
-            for d in peers(p, 5 - q):
-                up(p, b, 5 - q, d).start()
-        else:
-            core_up(p, b).start()
-
-    for b in range(n_sub):
-        for p in range(2):
-            core_copy(p, b).start()
-
-    n_axes = (None, "y", "x", "z")
-
-    def n_copy(stage, d):
-        if stage == 0:
-            dev = sibling
-        else:
-            n, i = at[n_axes[stage]]
-            dev = device(n_axes[stage], lax.rem(i + d, n))
-        return rcopy(n_acc.at[stage], n_in.at[stage, d - 1], n_s.at[stage, d - 1], n_r.at[stage, d - 1], dev)
-
-    def n_peers(stage):
-        return range(1, 2 if stage == 0 else at[n_axes[stage]][0])
-
-    def n_total(stage):
-        for d in n_peers(stage):
-            n_copy(stage, d).wait_recv()
-        own = n_acc[stage]
-        if stage == 0:
-            return own + n_in[0, 0]
-        n, i = at[n_axes[stage]]
-        total = jnp.zeros_like(own)
-        for m in range(n):
-            term = own
-            for d in range(1, n):
-                term = jnp.where(lax.rem(i + n - d, n) == m, n_in[stage, d - 1], term)
-            total = total + term
-        return total
-
-    n_acc[0] = norms[...]
-    n_copy(0, 1).start()
-
-    @pl.loop(0, n_sub + 6)
-    def _(s):
-        for q in range(7):
-
-            @pl.when((s >= q) & (s - q < n_sub))
-            def _():
-                for p in range(2):
-                    event(p, s - q, q)
-
-        for stage in range(1, 4):
-
-            @pl.when(s == stage)
-            def _():
-                n_acc[stage] = n_total(stage - 1)
-                for d in n_peers(stage):
-                    n_copy(stage, d).start()
-
-    norms_out[...] = n_total(3)
-    for stage in range(4):
-        for d in n_peers(stage):
-            n_copy(stage, d).wait_send()
-
-    @pl.loop(0, n_sub)
-    def _(b):
-        for p in range(2):
-            core_up(p, b).wait_recv()
-            core_copy(p, b).wait_send()
-            core_up(p, b).wait_send()
-            for stage in range(3):
-                for d in peers(p, stage):
-                    down(p, b, stage, d).wait_send()
-                    up(p, b, stage, d).wait_send()
-
-
-def reduce_all(n_exp, n_hid, mats, norms):
-    n_y = n_hid // 2
-    n_x = n_y
-    n_z = n_exp // n_x
-    sub = n_x * n_y * n_z
-    width = norms.shape[1]
-    flat = mats.reshape(-1, 16, width)
-    half = flat.shape[0] // 2
-    n_sub = half // 2 // sub
-    most = max(n_x, n_y)
-    shape = jax.ShapeDtypeStruct
-
-    def land(n, count):
-        return pltpu.VMEM((2, n_sub, n - 1, count, 16, width), BF)
-
-    def sems(n):
-        return [DMA((2, n_sub, n - 1))] * 2
-
-    mats, norms = pl.pallas_call(
-        functools.partial(reduce_kernel, n_x, n_y, n_z),
-        name="reduce_all",
-        out_shape=(shape(flat.shape, BF), shape(norms.shape, F32)),
-        in_specs=[VM] * 2,
-        out_specs=[VM] * 2,
-        scratch_shapes=[
-            pltpu.VMEM((half, 16, width), BF),
-            pltpu.VMEM((half, 16, width), BF),
-            land(most, sub // min(n_x, n_y)),
-            land(most, sub // (n_x * n_y)),
-            land(n_z, 1),
-            pltpu.VMEM((4, *norms.shape), F32),
-            pltpu.VMEM((4, max(most, n_z) - 1, *norms.shape), F32),
-            DMA((2, n_sub)), DMA((2, n_sub)),
-            *sems(most), *sems(most), *sems(n_z), *sems(n_z), *sems(most), *sems(most),
-            DMA((2, n_sub)), DMA((2, n_sub)),
-            *[DMA((4, max(most, n_z) - 1))] * 2,
-        ],
-        compiler_params=pltpu.CompilerParams(
-            collective_id=3, has_side_effects=True, vmem_limit_bytes=50 * MIB
-        ),
-    )(flat, norms)
-    return mats, norms
 
 
 def token_slots(token_ids, hash_table, capacity, cap):
@@ -1309,7 +1334,6 @@
         n_exp, n_hid, lengths, slot[:, None], tokens, middle, cotangent, mixed, context, lse, back,
         gain1, shift1, w_qkv, w_out, gain2, bias_back, f_part,
     )
-    mats, norms = reduce_all(n_exp, n_hid, mats, norms)
     g_in, g_back, g_qkv, g_out = finish(wi, wb, mats)
     return (
         output, g_tokens, norms[0], norms[1], g_qkv, g_out, norms[2], norms[3],

time: 418 us -> 396 us (0.947)
  Pallas kernels: 406 us -> 384 us
    pallas_call x1 -> x0, Pallas kernels: 104 us -> none  [reduce_all(): pl.pallas_call(functools.partial(reduce_kernel, n_x, n_y, n_z), name='red...]
    pallas_call x1, Pallas kernels: 71.7 us -> 154 us  [attend_back(): pl.pallas_call(functools.partial(attend_back_kernel, n_exp, n_y), name='a...]
where the time goes in v5:
time: 396 us
  Pallas kernels  384 us (97%)
  local copies, waits for them, and re-layouts  9.12 us (2%)
    pallas_call x1, Pallas kernels, attend_back(): pl.pallas_call(functools.partial(attend_back_kernel, n_exp, n_y), name='a...  154 us
    pallas_call x1, Pallas kernels, experts(): pl.pallas_call(functools.partial(expert_kernel, n_exp, n_y), name='expert...  136 us
    pallas_call x1, Pallas kernels, attend(): pl.pallas_call(functools.partial(attend_kernel, n_exp, n_y), name='attend...  67.5 us
    pallas_call x1, Pallas kernels, finish(): pl.pallas_call(finish_kernel, name='finish', grid=(lc, cut), out_shape=(s...  26.8 us

profile of v5, /device:TPU:0, one launch (start us, length us, event | category | flops | bytes accessed | tf_op | source)
XLA Modules:
  0.0 396.0 jit_solution(15455191780720092893)
XLA Ops:
  0.6 0.0 copy-start
  0.7 0.7 pad_clamp_fusion
  1.4 0.1 copy-done
  1.4 3.1 gather_fusion
  4.6 0.2 convert_reduce_fusion
  4.8 0.7 select_reduce_fusion
  5.6 0.0 copy-start.4
  5.6 0.9 copy.29.slot_col
  6.4 0.0 copy-done.4
  6.4 67.5 %attend.1 = (bf16[512,3072]{1,0:T(8,128)(2,1)}, bf16[512,1024]{1,0:T(8,128)(2,1)}, f32[512,1024]{1,0:T(8,128)}, f32[512,128]{1,0:T(8,128)}, bf16[8,4,32,1024]{3,...) custom-call(s32[1,2]{1,0:T(1,128)} %lens.3, s32[1,512]{1,0:T(1,128)} %bitcast.13, bf16[512,1024]{1,0:T(8,128)(2,1)} %tokens_h.1, ...), custom_call_target="tpu_custom_call" | custom-call | tf_op jit(solution)/shard_map/attend/pallas_call | solution.py:382
  73.9 136.2 %experts.1 = (bf16[8,4,32,1024]{3,2,1,0:T(8,128)(2,1)}, bf16[4,8,2,2,32,1024]{5,4,3,2,1,0:T(8,128)(2,1)}, bf16[4,1024,1024]{2,1,0:T(8,128)(2,1)}, bf16[4,1024,10...) custom-call(bf16[8,4,32,1024]{3,2,1,0:T(8,128)(2,1)} %get-tuple-element.36.rows, ...), custom_call_target="tpu_custom_call" | custom-call | tf_op jit(solution)/shard_map/experts/pallas_call | solution.py:759
  210.2 154.0 %attend_back.1 = (bf16[512,1024]{1,0:T(8,128)(2,1)}, f32[512,1024]{1,0:T(8,128)}, bf16[256,16,1024]{2,1,0:T(8,128)(2,1)}, f32[8,1024]{1,0:T(8,128)}) custom-call(s32[1,2]{1,0:T(1,128)} %lens.3, s32[512,1]{1,0:T(8,128)} %copy.29.slot_col, bf16[512,1024]{1,0:T(8,128)(2,1)} %tokens_h.1, f32[512,1024]{1,0:T(8,128)} %get-tuple-element.32.middle_h, ...), custom_call_target="tpu_custom_call" | custom-call | tf_op jit(solution)/shard_map/attend_back/pallas_call | solution.py:1271
  364.2 1.5 fusion.1
  365.7 0.0 copy-start.5
  365.7 0.0 copy-start.1
  365.7 26.8 %finish.1 = (f32[4,1024,1024]{2,1,0:T(8,128)}, f32[4,1024,1024]{2,1,0:T(8,128)}, f32[1024,3072]{1,0:T(8,128)}, f32[1024,1024]{1,0:T(8,128)}) custom-call(bf16[4,1024,1024]{2,1,0:T(8,128)(2,1)} %get-tuple-element.43.wi, bf16[4,1024,1024]{2,1,0:T(8,128)(2,1)} %get-tuple-element.44.wb, bf16[4,64,16,1024]{3,2,1,0:T(8,128)(2,1)} %bitcast.11), custom_call_target="tpu_custom_call" | custom-call | tf_op jit(solution)/shard_map/finish/pallas_call | solution.py:812
  392.5 0.0 copy-done.3
  392.5 1.0 copy.34
  393.5 0.0 copy-done.2
  393.5 1.3 copy.35
  394.8 0.0 copy-done.6
  394.8 0.6 copy.36
  395.4 0.0 copy-done.5
  395.4 0.6 copy.37
  (5 shorter events, 0.0 us)
Async XLA Ops:
  0.6 0.8 copy-start
  5.6 0.9 copy-start.4
  365.7 26.8 %copy-start.3 = (bf16[512,1024]{1,0:T(8,128)(2,1)S(1)}, bf16[512,1024]{1,0:T(8,128)(2,1)}, u32[]{:S(2)}) copy-start(bf16[512,1024]{1,0:T(8,128)(2,1)} %get-tuple-element.68) | copy-start | bytes 3145732
  365.7 27.8 %copy-start.2 = (f32[512,1024]{1,0:T(8,128)S(1)}, f32[512,1024]{1,0:T(8,128)}, u32[]{:S(2)}) copy-start(f32[512,1024]{1,0:T(8,128)} %get-tuple-element.69) | copy-start | bytes 6291460
  365.7 29.1 %copy-start.6 = (f32[4,1024]{1,0:T(4,128)S(1)}, f32[4,1024]{1,0:T(4,128)}, u32[]{:S(2)}) copy-start(f32[4,1024]{1,0:T(4,128)} %get-tuple-element.77) | copy-start | bytes 49156
  365.7 29.7 %copy-start.5 = (f32[4,1024]{1,0:T(4,128)S(1)}, f32[4,1024]{1,0:T(4,128)}, u32[]{:S(2)}) copy-start(f32[4,1024]{1,0:T(4,128)} %get-tuple-element.79) | copy-start | bytes 49156
  365.7 30.3 %copy-start.1 = (s32[8008]{0:T(1024)S(1)}, s32[8008]{0:T(1024)}, u32[]{:S(2)}) copy-start(s32[8008]{0:T(1024)} %param.19) | copy-start | bytes 96100

commit v6 on v5

--- a/solution.py
+++ b/solution.py
@@ -73,12 +73,9 @@
             self.es.at[k], self.er.at[k], (self.e ^ k, self.h),
         )
 
-    def start(self):
-        @pl.loop(1, self.n_exp)
-        def _(i):
-            low, high = lax.div(i + 1, 2), self.n_exp // 2 + lax.div(i, 2) - 1
-            k = jnp.where(i == self.n_exp - 1, self.n_exp - 1, jnp.where(lax.rem(i, 2) == 1, low, high))
-            self.over_exp(k).start()
+    def turn(self, i):
+        low, high = lax.div(i + 1, 2), self.n_exp // 2 + lax.div(i, 2) - 1
+        return jnp.where(i == self.n_exp - 1, self.n_exp - 1, jnp.where(lax.rem(i, 2) == 1, low, high))
 
     def block(self, k, hid):
         return self.land.at[:, self.e ^ k, hid]
@@ -214,6 +211,32 @@
         - unit * jnp.mean(scaled * unit, axis=-1, keepdims=True)
     )
     return inner * inverse
+
+
+def turned(values):
+    if values.shape[1] == 1:
+        return jnp.broadcast_to(values, (values.shape[0], 128)).T
+    return jnp.broadcast_to(values, (128, values.shape[1])).T
+
+
+def token_slots(token_ids, hash_table, capacity, cap):
+    tok = token_ids.shape[1]
+    ids = turned(token_ids.astype(F32)).astype(jnp.int32)
+    row, col = lax.shift_right_logical(ids, 7), ids & 127
+    n_rows = hash_table.shape[0]
+    lanes = lax.broadcasted_iota(jnp.int32, (tok, 128), 1)
+    is_row = jnp.where(lanes[:, :n_rows] == row[:, :n_rows], 1.0, 0.0).astype(BF)
+    found = mm(is_row, hash_table.astype(F32).astype(BF))
+    chosen = jnp.sum(jnp.where(lanes == col, found, 0.0), axis=1, keepdims=True)
+    n_experts = capacity.shape[1]
+    ids_e = lax.broadcasted_iota(jnp.int32, (tok, n_experts), 1)
+    onehot = jnp.where(ids_e == chosen.astype(jnp.int32), 1.0, 0.0)
+    here = lax.broadcasted_iota(jnp.int32, (tok, tok), 0)
+    there = lax.broadcasted_iota(jnp.int32, (tok, tok), 1)
+    before = mm(jnp.where(here > there, 1.0, 0.0).astype(BF), onehot.astype(BF))
+    rank = jnp.sum(before * onehot, axis=1, keepdims=True)
+    limit = jnp.sum(capacity.astype(F32) * onehot, axis=1, keepdims=True)
+    return jnp.where(rank < limit, chosen * cap + rank, -1.0)
 
 
 def slot_block(slot_row, first, count):
@@ -241,9 +264,9 @@
 
 
 def attend_kernel(
-    n_exp, n_y, lens, slot_row, tokens, gain1, shift1, w_qkv, w_out, gain2, shift2, cot,
-    mixed_h, context_h, middle_h, lse, send_h, land,
-    mixed, context, middle, send, cot_rows, normed, bias, wq_v, wo_v, in_sem, out_sem, own_sem, *sems,
+    n_exp, n_y, lens, token_ids, hash_table, capacity, tokens, gain1, shift1, w_qkv, w_out, gain2, shift2, cot,
+    mixed_h, context_h, middle_h, lse, slot_col, send_h, land, first_rows,
+    slot_row, mixed, context, middle, send, cot_rows, normed, bias, wq_v, wo_v, in_sem, out_sem, own_sem, first_s, first_r, *sems,
 ):
     tok, width = tokens.shape
     e, h, y, c = place()
@@ -264,6 +287,10 @@
     for cp in loads:
         cp.start()
 
+    slots = token_slots(token_ids[...], hash_table[...], capacity[...], cap)
+    slot_col[...] = slots.astype(jnp.int32)
+    slot_row[...] = turned(slots)[:1].astype(jnp.int32)
+
     def pick(source, dst):
         rows = mm(slot_block(slot_row[...], dst * per, per), source)
         return rows.astype(BF).reshape(lc, cap, width)
@@ -275,14 +302,22 @@
         def _():
             spread.pass_y(k - 1)
 
-    @pl.loop(0, n_exp)
-    def _(k):
-        cot_rows[k] = pick(cot[...], k)
-
+    def first(k):
+        return rcopy(
+            send.at[e ^ k, 0], first_rows.at[e], first_s.at[k], first_r.at[k], (e ^ k, h)
+        )
+
+    cot_rows[e] = pick(cot[...], e)
     own = pltpu.make_async_copy(cot_rows.at[e], land.at[:, e, h], own_sem)
     own.start()
     greet(n_exp, n_y)
-    spread.start()
+
+    @pl.loop(1, n_exp)
+    def _(i):
+        k = spread.turn(i)
+        cot_rows[e ^ k] = pick(cot[...], e ^ k)
+        spread.over_exp(k).start()
+
     own.wait()
     spread.pass_on(0)
 
@@ -360,6 +395,12 @@
         send[k] = pick(normed[...], k)
 
     stores[3].start()
+    own_first = pltpu.make_async_copy(send.at[e, 0], first_rows.at[e], own_sem)
+    own_first.start()
+
+    @pl.loop(1, n_exp)
+    def _(k):
+        first(k).start()
 
     @pl.loop(7, n_exp)
     def _(k):
@@ -368,6 +409,12 @@
     spread.pass_y(n_exp - 1)
     for cp in stores:
         cp.wait()
+    own_first.wait()
+
+    @pl.loop(1, n_exp)
+    def _(k):
+        first(k).wait_send()
+        first(k).wait_recv()
 
     @pl.loop(0, n_exp)
     def _(k):
@@ -375,7 +422,7 @@
         spread.sent(k)
 
 
-def attend(n_exp, n_hid, lc, cap, lens, slot_row, tokens, gain1, shift1, w_qkv, w_out, gain2, shift2, cot):
+def attend(n_exp, n_hid, lc, cap, lens, token_ids, hash_table, capacity, tokens, gain1, shift1, w_qkv, w_out, gain2, shift2, cot):
     n_y = n_hid // 2
     tok, width = tokens.shape
     shape = jax.ShapeDtypeStruct
@@ -387,12 +434,15 @@
             shape((tok, width), BF),
             shape((tok, width), F32),
             shape((tok, 128), F32),
+            shape((tok, 1), jnp.int32),
             shape((n_exp, lc, cap, width), BF),
             shape((lc, n_exp, n_hid, cap, width), BF),
+            shape((n_exp, cap, width), BF),
         ),
-        in_specs=[SM, VM, VM, VM, VM, HB, HB, VM, VM, VM],
-        out_specs=[HB, HB, HB, VM, HB, HB],
+        in_specs=[SM, VM, VM, VM, VM, VM, VM, HB, HB, VM, VM, VM],
+        out_specs=[HB, HB, HB, VM, VM, HB, HB, HB],
         scratch_shapes=[
+            pltpu.VMEM((1, tok), jnp.int32),
             pltpu.VMEM((tok, 3 * width), BF),
             pltpu.VMEM((tok, width), BF),
             pltpu.VMEM((tok, width), F32),
@@ -405,12 +455,14 @@
             DMA((2,)),
             DMA((4,)),
             DMA,
+            DMA((n_exp,)),
+            DMA((n_exp,)),
             *Spread.sems(n_exp, n_y),
         ],
         compiler_params=pltpu.CompilerParams(
             collective_id=0, has_side_effects=True, vmem_limit_bytes=56 * MIB
         ),
-    )(lens, slot_row, tokens, gain1, shift1, w_qkv, w_out, gain2, shift2, cot)
+    )(lens, token_ids, hash_table, capacity, tokens, gain1, shift1, w_qkv, w_out, gain2, shift2, cot)
 
 
 STEP_W = 512
@@ -460,9 +512,10 @@
         blk = self.land.at[ex, self.range(g), hid]
         return rcopy(blk, blk, self.cs.at[ex, g, d], self.cr.at[ex, g, d], self.sibling)
 
-    def pass_on(self, ex, g):
-        for k in range(max(1, g * self.half), (g + 1) * self.half):
-            self.over_exp(ex, k).wait_recv()
+    def pass_on(self, ex, g, came=False):
+        if not came:
+            for k in range(max(1, g * self.half), (g + 1) * self.half):
+                self.over_exp(ex, k).wait_recv()
         for d in range(1, self.n_y):
             self.over_y(ex, g, d).start()
         self.over_core(ex, g, 0).start()
@@ -477,8 +530,11 @@
             self.over_core(ex, g, d).wait_recv()
 
     def sent(self, ex):
-        for k in range(1, self.n_exp):
-            self.over_exp(ex, k).wait_send()
+        @pl.when(ex > 0)
+        def _():
+            for k in range(1, self.n_exp):
+                self.over_exp(ex, k).wait_send()
+
         for g in range(2):
             for d in range(1, self.n_y):
                 self.over_y(ex, g, d).wait_send()
@@ -553,7 +609,7 @@
 
 
 def expert_kernel(
-    n_exp, n_y, rows, grads, w_in, bias_in, w_back,
+    n_exp, n_y, first_rows, rows, grads, w_in, bias_in, w_back,
     back, f_out, wi_out, wb_out, gb_in, gb_back,
     land, part, pairs, from_y, wi_v, wb_v, g_v, h_v, gp_v, f_v, wi_st, wb_st,
     w_sem, g_sem, f_sem, o_sem, own_sem, *rest,
@@ -594,11 +650,15 @@
     def sources(rb):
         return pl.ds(lax.rem(lax.div(e, n_exp // 2) * (n_rb // 2) + rb, n_rb) * n_src, n_src)
 
-    own = pltpu.make_async_copy(rows.at[e], land.at[:, e, h], own_sem)
+    own = pltpu.make_async_copy(rows.at[e, pl.ds(1, lc - 1)], land.at[pl.ds(1, lc - 1), e, h], own_sem.at[0])
+    own_first = pltpu.make_async_copy(first_rows, land.at[0, :, h], own_sem.at[1])
+    own_first.start()
     own.start()
     greet(n_exp, n_y)
-
-    spread.start(0)
+    own_first.wait()
+    spread.pass_on(0, 0, came=True)
+    spread.pass_on(0, 1, came=True)
+    spread.start(1)
     for ex in range(2):
         for cp in weights(ex):
             cp.start()
@@ -606,10 +666,8 @@
     gb_in[...] = jnp.zeros_like(gb_in)
     gb_back[...] = jnp.zeros_like(gb_back)
     own.wait()
-    spread.pass_on(0, 0)
-    spread.start(1)
-    spread.pass_on(0, 1)
     spread.pass_y(0, 0)
+    spread.start(2)
 
     def weight_grads(ex, after):
         slot = lax.rem(ex, 2)
@@ -688,9 +746,9 @@
                         def _():
                             spread.pass_y(0, 1)
 
-                        @pl.when(ex + 2 < lc)
+                        @pl.when(ex + 3 < lc)
                         def _():
-                            spread.start(ex + 2)
+                            spread.start(ex + 3)
 
                     @pl.when(ex + 1 < lc)
                     def _():
@@ -750,7 +808,7 @@
         gather.finish(ex)
 
 
-def experts(n_exp, n_hid, rows, grads, w_in, bias_in, w_back):
+def experts(n_exp, n_hid, first_rows, rows, grads, w_in, bias_in, w_back):
     n_y = n_hid // 2
     _, lc, cap, width = rows.shape
     ff = w_in.shape[2]
@@ -767,7 +825,7 @@
             shape((lc, ff), F32),
             shape((lc, width), F32),
         ),
-        in_specs=[HB, HB, HB, VM, HB],
+        in_specs=[HB, HB, HB, HB, VM, HB],
         out_specs=[HB, HB, HB, HB, VM, VM],
         scratch_shapes=[
             pltpu.VMEM((lc, n_exp, n_hid, cap, width), BF),
@@ -782,17 +840,24 @@
             pltpu.VMEM((4, n_y, 2, cap, width), BF),
             pltpu.VMEM((STEP_W, ff), BF),
             pltpu.VMEM((STEP_W, width), BF),
-            DMA((2, 2)), DMA((2,)), DMA, DMA((2,)), DMA,
+            DMA((2, 2)), DMA((2,)), DMA, DMA((2,)), DMA((2,)),
             *SpreadExpert.sems(lc, n_exp, n_y),
             *GatherExpert.sems(lc, n_exp, n_y),
         ],
         compiler_params=pltpu.CompilerParams(
             collective_id=1, has_side_effects=True, vmem_limit_bytes=63 * MIB
         ),
-    )(rows, grads, w_in, bias_in, w_back)
-
-
-def finish_kernel(wi, wb, mats, g_in, g_back, g_qkv, g_out):
+    )(first_rows, rows, grads, w_in, bias_in, w_back)
+
+
+def finish_kernel(wi, wb, mats, norms, bi, bb, g_in, g_back, g_qkv, g_out, n0, n1, n2, n3, g_bi, g_bb):
+    @pl.when((pl.program_id(0) == 0) & (pl.program_id(1) == 0))
+    def _():
+        for i, n in enumerate((n0, n1, n2, n3)):
+            n[...] = norms[i]
+        g_bi[...] = bi[...]
+        g_bb[...] = bb[...]
+
     g_in[...] = wi[...].astype(F32)
     g_back[...] = wb[...].astype(F32)
     rows, width = g_out.shape
@@ -801,14 +866,15 @@
     g_out[...] = mats[3].reshape(rows, width).astype(F32)
 
 
-def finish(wi, wb, mats):
+def finish(wi, wb, mats, norms, bi, bb):
     lc, width, ff = wi.shape
-    cut = 2
+    cut = 4
     rows = width // (lc * cut)
     mats = mats.reshape(4, width // 16, 16, width)
     shape = jax.ShapeDtypeStruct
     wi_spec = pl.BlockSpec((1, width // cut, ff), lambda i, j: (i, j, 0))
     wb_spec = pl.BlockSpec((1, ff // cut, width), lambda i, j: (i, j, 0))
+    small = [pl.BlockSpec(a.shape, lambda i, j: (0, 0)) for a in (norms, bi, bb)]
     return pl.pallas_call(
         finish_kernel,
         name="finish",
@@ -816,18 +882,22 @@
         out_shape=(
             shape(wi.shape, F32), shape(wb.shape, F32),
             shape((width, 3 * width), F32), shape((width, width), F32),
+            *[shape((width,), F32)] * 4, shape(bi.shape, F32), shape(bb.shape, F32),
         ),
         in_specs=[
             wi_spec, wb_spec,
             pl.BlockSpec((4, rows // 16, 16, width), lambda i, j: (0, i * cut + j, 0, 0)),
+            *small,
         ],
         out_specs=[
             wi_spec, wb_spec,
             pl.BlockSpec((rows, 3 * width), lambda i, j: (i * cut + j, 0)),
             pl.BlockSpec((rows, width), lambda i, j: (i * cut + j, 0)),
+            *[pl.BlockSpec((width,), lambda i, j: (0,))] * 4,
+            *small[1:],
         ],
         compiler_params=pltpu.CompilerParams(vmem_limit_bytes=56 * MIB),
-    )(wi, wb, mats)
+    )(wi, wb, mats, norms, bi, bb)
 
 
 class Reduce:
@@ -1304,16 +1374,6 @@
     )
 
 
-def token_slots(token_ids, hash_table, capacity, cap):
-    chosen = jnp.take(hash_table, token_ids, mode="clip")
-    places = jnp.arange(chosen.shape[0], dtype=jnp.int32)
-    earlier = (chosen[:, None] == chosen[None, :]) & (places[:, None] > places[None, :])
-    rank = jnp.sum(earlier.astype(jnp.int32), axis=1)
-    experts_ids = jnp.arange(capacity.shape[0], dtype=jnp.int32)
-    limit = jnp.sum(jnp.where(chosen[:, None] == experts_ids[None, :], capacity[None, :], 0), axis=1)
-    return jnp.where(rank < limit, chosen * cap + rank, -1)
-
-
 def per_device(
     tokens, token_ids, lengths, hash_table, capacity, gain_one, shift_one, w_qkv, w_out,
     gain_two, shift_two, w_in, bias_in, w_back, bias_back, cotangent,
@@ -1322,22 +1382,22 @@
     tok, width = tokens.shape
     lc, _, ff = w_in.shape
     cap = 2 * tok // capacity.shape[0]
-    slot = token_slots(token_ids, hash_table, capacity, cap)
+    table_rows = -(-hash_table.shape[0] // 1024) * 8
+    table = jnp.pad(hash_table, (0, table_rows * 128 - hash_table.shape[0])).reshape(table_rows, 128)
     gain1, shift1, gain2, shift2 = (v[None] for v in (gain_one, shift_one, gain_two, shift_two))
-    mixed, context, middle, lse, send, grads = attend(
-        n_exp, n_hid, lc, cap, lengths, slot[None], tokens, gain1, shift1, w_qkv, w_out, gain2, shift2, cotangent
+    mixed, context, middle, lse, slot, send, grads, first_rows = attend(
+        n_exp, n_hid, lc, cap, lengths, token_ids[None], table, capacity[None], tokens, gain1, shift1, w_qkv, w_out, gain2, shift2, cotangent
     )
     back, f_part, wi, wb, gb_in, gb_back = experts(
-        n_exp, n_hid, send, grads, w_in, bias_in, w_back
+        n_exp, n_hid, first_rows, send, grads, w_in, bias_in, w_back
     )
     output, g_tokens, mats, norms = attend_back(
-        n_exp, n_hid, lengths, slot[:, None], tokens, middle, cotangent, mixed, context, lse, back,
+        n_exp, n_hid, lengths, slot, tokens, middle, cotangent, mixed, context, lse, back,
         gain1, shift1, w_qkv, w_out, gain2, bias_back, f_part,
     )
-    g_in, g_back, g_qkv, g_out = finish(wi, wb, mats)
+    g_in, g_back, g_qkv, g_out, *norms, gb_in, gb_back = finish(wi, wb, mats, norms, gb_in, gb_back)
     return (
-        output, g_tokens, norms[0], norms[1], g_qkv, g_out, norms[2], norms[3],
-        g_in, gb_in, g_back, gb_back,
+        output, g_tokens, norms[0], norms[1], g_qkv, g_out, norms[2], norms[3], g_in, gb_in, g_back, gb_back,
     )
 
 

time: 396 us -> 383 us (0.967)
  Pallas kernels: 384 us -> 378 us
  local copies, waits for them, and re-layouts: 9.12 us -> 3.68 us
    pallas_call x1, Pallas kernels: 136 us -> 124 us  [experts(): pl.pallas_call(functools.partial(expert_kernel, n_exp, n_y), name='expert...]
where the time goes in v6:
time: 383 us; the launch traced here: 382 us
  Pallas kernels  378 us (99%)
    pallas_call x1, Pallas kernels, attend_back(): pl.pallas_call(functools.partial(attend_back_kernel, n_exp, n_y), name='a...  155 us
    pallas_call x1, Pallas kernels, experts(): pl.pallas_call(functools.partial(expert_kernel, n_exp, n_y), name='expert...  124 us
    pallas_call x1, Pallas kernels, attend(): pl.pallas_call(functools.partial(attend_kernel, n_exp, n_y), name='attend...  71.2 us
    pallas_call x1, Pallas kernels, finish(): pl.pallas_call(finish_kernel, name='finish', grid=(lc, cut), out_shape=(s...  27 us

profile of v6, /device:TPU:0, one launch (start us, length us, event | category | flops | bytes accessed | tf_op | source)
XLA Modules:
  0.0 382.2 jit_solution(103925917777355032)
XLA Ops:
  0.6 1.4 pad_bitcast_fusion.hash_table
  2.0 71.2 %attend.1 = (bf16[512,3072]{1,0:T(8,128)(2,1)}, bf16[512,1024]{1,0:T(8,128)(2,1)}, f32[512,1024]{1,0:T(8,128)}, f32[512,128]{1,0:T(8,128)}, s32[512,1]{1,0:T(8,1...) custom-call(s32[1,2]{1,0:T(1,128)} %lens.3, ...), custom_call_target="tpu_custom_call" | custom-call | tf_op jit(solution)/shard_map/attend/pallas_call | solution.py:429
  73.2 124.4 %experts.1 = (bf16[8,4,32,1024]{3,2,1,0:T(8,128)(2,1)}, bf16[4,8,2,2,32,1024]{5,4,3,2,1,0:T(8,128)(2,1)}, bf16[4,1024,1024]{2,1,0:T(8,128)(2,1)}, bf16[4,1024,10...) custom-call(bf16[8,32,1024]{2,1,0:T(8,128)(2,1)} %get-tuple-element.45.first_rows, ...), custom_call_target="tpu_custom_call" | custom-call | tf_op jit(solution)/shard_map/experts/pallas_call | solution.py:817
  197.6 155.3 %attend_back.1 = (bf16[512,1024]{1,0:T(8,128)(2,1)}, f32[512,1024]{1,0:T(8,128)}, bf16[256,16,1024]{2,1,0:T(8,128)(2,1)}, f32[8,1024]{1,0:T(8,128)}) custom-call(s32[1,2]{1,0:T(1,128)} %lens.3, s32[512,1]{1,0:T(8,128)} %get-tuple-element.40.slot_col, bf16[512,1024]{1,0:T(8,128)(2,1)} %tokens_h.1, f32[512,1024]{1,0:T(8,128)} %get-tuple-element.41.middle_h, ...), custom_call_target="tpu_custom_call" | custom-call | tf_op jit(solution)/shard_map/attend_back/pallas_call | solution.py:1341
  352.8 0.0 copy-start.1
  352.9 0.0 copy-start
  352.9 27.0 %finish.1 = (f32[4,1024,1024]{2,1,0:T(8,128)}, f32[4,1024,1024]{2,1,0:T(8,128)}, f32[1024,3072]{1,0:T(8,128)}, f32[1024,1024]{1,0:T(8,128)}, f32[1024]{0:T(1024)...) custom-call(bf16[4,1024,1024]{2,1,0:T(8,128)(2,1)} %get-tuple-element.52.wi, ...), custom_call_target="tpu_custom_call" | custom-call | tf_op jit(solution)/shard_map/finish/pallas_call | solution.py:878
  379.9 0.0 copy-done.1
  379.9 1.0 copy.30
  380.9 0.0 copy-done
  380.9 1.3 copy.31
Async XLA Ops:
  352.8 27.1 %copy-start.1 = (bf16[512,1024]{1,0:T(8,128)(2,1)S(1)}, bf16[512,1024]{1,0:T(8,128)(2,1)}, u32[]{:S(2)}) copy-start(bf16[512,1024]{1,0:T(8,128)(2,1)} %get-tuple-element.80) | copy-start | bytes 3145732
  352.9 28.0 %copy-start = (f32[512,1024]{1,0:T(8,128)S(1)}, f32[512,1024]{1,0:T(8,128)}, u32[]{:S(2)}) copy-start(f32[512,1024]{1,0:T(8,128)} %get-tuple-element.81) | copy-start | bytes 6291460

commit v7 on v6

--- a/solution.py
+++ b/solution.py
@@ -862,8 +862,8 @@
     g_back[...] = wb[...].astype(F32)
     rows, width = g_out.shape
     for part in range(3):
-        g_qkv[:, part * width : (part + 1) * width] = mats[part].reshape(rows, width).astype(F32)
-    g_out[...] = mats[3].reshape(rows, width).astype(F32)
+        g_qkv[:, part * width : (part + 1) * width] = mats[part + 1].reshape(rows, width).astype(F32)
+    g_out[...] = mats[0].reshape(rows, width).astype(F32)
 
 
 def finish(wi, wb, mats, norms, bi, bb):
@@ -900,7 +900,12 @@
     )(wi, wb, mats, norms, bi, bb)
 
 
+EARLY = (2,)
+
+
 class Reduce:
+    lead = 1
+
     def __init__(self, n_exp, n_y, mats, out, norms, scratch):
         (self.core_in, in1, in2, in3, self.n_acc, self.n_in, self.c_s, self.c_r,
          s1, r1, s2, r2, s3, r3, t3, u3, t2, u2, t1, u1, self.d_s, self.d_r, self.n_s, self.n_r, self.l_s) = scratch
@@ -909,7 +914,6 @@
         self.n_x, self.n_z, self.sub, self.half, self.n_sub = self.sizes(n_exp, n_y, mats.shape[0])
         x, z = lax.rem(self.e, self.n_x), lax.div(self.e, self.n_x)
         self.x, self.z = x, z
-        self.piece = self.half // 2
         self.at = {"x": (self.n_x, x), "y": (n_y, self.y), "z": (self.n_z, z)}
         self.orders = (("y", "x", "z"), ("x", "y", "z"))
         self.n_axes = (None, "y", "x", "z")
@@ -957,11 +961,11 @@
             "x": (self.z * self.n_x + o, self.h), "y": (self.e, o * 2 + self.c), "z": (o * self.n_x + self.x, self.h)
         }[axis]
 
-    def own(self, first, count):
-        return pl.ds(self.c * self.half + first, count)
+    def first(self, p, b, core):
+        return (b * 4 + core * 2 + p) * self.sub
 
     def units(self, p, b, depth):
-        first, count = p * self.piece + b * self.sub, self.sub
+        first, count = self.first(p, b, self.c), self.sub
         for axis in self.orders[p][:depth]:
             n, i = self.at[axis]
             count = count // n
@@ -969,9 +973,9 @@
         return first, count
 
     def core_copy(self, p, b):
-        first = p * self.piece + b * self.sub
         return rcopy(
-            self.mats.at[pl.ds((1 - self.c) * self.half + first, self.sub)], self.core_in.at[pl.ds(first, self.sub)],
+            self.mats.at[pl.ds(self.first(p, b, 1 - self.c), self.sub)],
+            self.core_in.at[pl.ds((b * 2 + p) * self.sub, self.sub)],
             self.c_s.at[p, b], self.c_r.at[p, b], self.sibling,
         )
 
@@ -981,14 +985,14 @@
         count = count // n
         o = lax.rem(i + d, n)
         return rcopy(
-            self.mats.at[self.own(first + o * count, count)], self.lands[stage].at[p, b, d - 1, pl.ds(0, count)],
+            self.mats.at[pl.ds(first + o * count, count)], self.lands[stage].at[p, b, d - 1, pl.ds(0, count)],
             self.sends[stage].at[p, b, d - 1], self.recvs[stage].at[p, b, d - 1],
             self.device(self.orders[p][stage], o),
         )
 
     def up(self, p, b, stage, d):
         n, i = self.at[self.orders[p][stage]]
-        at = self.own(*self.units(p, b, stage + 1))
+        at = pl.ds(*self.units(p, b, stage + 1))
         source = self.mats if stage == 2 else self.out
         o = lax.rem(i + d, n)
         return rcopy(
@@ -997,11 +1001,11 @@
         )
 
     def stay(self, p, b):
-        at = self.own(*self.units(p, b, 3))
+        at = pl.ds(*self.units(p, b, 3))
         return pltpu.make_async_copy(self.mats.at[at], self.out.at[at], self.l_s.at[p, b])
 
     def core_up(self, p, b):
-        region = self.out.at[self.own(p * self.piece + b * self.sub, self.sub)]
+        region = self.out.at[pl.ds(*self.units(p, b, 0))]
         return rcopy(region, region, self.d_s.at[p, b], self.d_r.at[p, b], self.sibling)
 
     def peers(self, p, stage):
@@ -1011,12 +1015,12 @@
         mats = self.mats
         if q == 0:
             self.core_copy(p, b).wait_recv()
-            first = p * self.piece + b * self.sub
-            at = self.own(first, self.sub)
-            mats[at] = (mats[at].astype(F32) + self.core_in[pl.ds(first, self.sub)].astype(F32)).astype(BF)
+            at = pl.ds(*self.units(p, b, 0))
+            other = self.core_in[pl.ds((b * 2 + p) * self.sub, self.sub)]
+            mats[at] = (mats[at].astype(F32) + other.astype(F32)).astype(BF)
         elif q <= 3:
             first, count = self.units(p, b, q)
-            at = self.own(first, count)
+            at = pl.ds(first, count)
             total = mats[at].astype(F32)
             for d in self.peers(p, q - 1):
                 self.down(p, b, q - 1, d).wait_recv()
@@ -1038,12 +1042,19 @@
         else:
             self.core_up(p, b).start()
 
-    def begin(self, part):
-        @pl.when(self.c == 1 - part // 2)
-        def _():
-            @pl.loop(0, self.n_sub)
-            def _(b):
-                self.core_copy(part % 2, b).start()
+    def begin(self, quarter):
+        if self.n_sub == 4:
+            for p in range(2):
+                self.core_copy(p, quarter).start()
+        elif quarter == 3:
+            for b in range(self.n_sub):
+                for p in range(2):
+                    self.core_copy(p, b).start()
+
+    def early(self, q):
+        if self.n_sub == 4:
+            for p in range(2):
+                self.event(p, 0, q)
 
     def n_copy(self, stage, d):
         if stage == 0:
@@ -1077,14 +1088,24 @@
         self.n_acc[0] = self.norms[...]
         self.n_copy(0, 1).start()
 
-        @pl.loop(0, self.n_sub + 6)
+        ahead = self.n_sub == 4
+
+        @pl.loop(0, self.n_sub - 1 + 6 + (not ahead))
         def _(s):
             for q in range(7):
-
-                @pl.when((s >= q) & (s - q < self.n_sub))
+                if ahead and q >= self.lead:
+
+                    @pl.when(s == q - self.lead)
+                    def _():
+                        for p in range(2):
+                            self.event(p, 0, q)
+
+                b = s - q + (1 if ahead else 0)
+
+                @pl.when((b >= (1 if ahead else 0)) & (b < self.n_sub))
                 def _():
                     for p in range(2):
-                        self.event(p, s - q, q)
+                        self.event(p, b, q)
 
             for stage in range(1, 4):
 
@@ -1203,9 +1224,9 @@
     def _(i):
         cols = pl.ds(pl.multiple_of(i * 256, 256), 256)
         part = mm_tn(context[:, cols], gattn[...]).astype(BF)
-        g_mats[pl.ds(3 * n_quarter + i * 16, 16)] = part.reshape(16, 16, width)
-
-    total.begin(3)
+        g_mats[pl.ds(i * 16, 16)] = part.reshape(16, 16, width)
+
+    total.begin(0)
     key_i = lax.broadcasted_iota(jnp.int32, (tok, tok), 0)
     qry_i = lax.broadcasted_iota(jnp.int32, (tok, tok), 1)
     dk_, dq_ = jnp.zeros((tok, tok), jnp.int32), jnp.zeros((tok, tok), jnp.int32)
@@ -1231,6 +1252,12 @@
         @pl.when((p >= 2) & (lax.rem(p, 2) == 0))
         def _():
             gather.step_exp(order(lax.div(p, 2) - 1), bias_back[...].reshape(lc, 1, width))
+
+        for q_step, at in enumerate(EARLY):
+
+            @pl.when(p == at)
+            def _():
+                total.early(q_step)
 
         def cols(part):
             return pl.ds(pl.multiple_of(part * width + p * 128, 128), 128)
@@ -1276,9 +1303,9 @@
         def _(i):
             rows = pl.ds(pl.multiple_of(i * 256, 256), 256)
             piece = mm(n1t[rows], mixed[:, part * width : (part + 1) * width])
-            g_mats[pl.ds(part * n_quarter + i * 16, 16)] = piece.astype(BF).reshape(16, 16, width)
-
-        total.begin(part)
+            g_mats[pl.ds((part + 1) * n_quarter + i * 16, 16)] = piece.astype(BF).reshape(16, 16, width)
+
+        total.begin(part + 1)
 
     @pl.loop(n_pairs + 4, max(n_exp, n_pairs + 4))
     def _(m):

time: 383 us -> 373 us (0.974)
  Pallas kernels: 378 us -> 368 us
    pallas_call x1, Pallas kernels: 155 us -> 145 us  [attend_back(): pl.pallas_call(functools.partial(attend_back_kernel, n_exp, n_y), name='a...]
where the time goes in v7:
time: 373 us; the launch traced here: 372 us
  Pallas kernels  368 us (99%)
    pallas_call x1, Pallas kernels, attend_back(): pl.pallas_call(functools.partial(attend_back_kernel, n_exp, n_y), name='a...  145 us
    pallas_call x1, Pallas kernels, experts(): pl.pallas_call(functools.partial(expert_kernel, n_exp, n_y), name='expert...  124 us
    pallas_call x1, Pallas kernels, attend(): pl.pallas_call(functools.partial(attend_kernel, n_exp, n_y), name='attend...  71.2 us
    pallas_call x1, Pallas kernels, finish(): pl.pallas_call(finish_kernel, name='finish', grid=(lc, cut), out_shape=(s...  27 us

profile of v7, /device:TPU:0, one launch (start us, length us, event | category | flops | bytes accessed | tf_op | source)
XLA Modules:
  0.0 372.0 jit_solution(11698452956748956272)
XLA Ops:
  0.6 1.4 pad_bitcast_fusion.hash_table
  2.0 71.2 %attend.1 = (bf16[512,3072]{1,0:T(8,128)(2,1)}, bf16[512,1024]{1,0:T(8,128)(2,1)}, f32[512,1024]{1,0:T(8,128)}, f32[512,128]{1,0:T(8,128)}, s32[512,1]{1,0:T(8,1...) custom-call(s32[1,2]{1,0:T(1,128)} %lens.3, ...), custom_call_target="tpu_custom_call" | custom-call | tf_op jit(solution)/shard_map/attend/pallas_call | solution.py:429
  73.2 124.4 %experts.1 = (bf16[8,4,32,1024]{3,2,1,0:T(8,128)(2,1)}, bf16[4,8,2,2,32,1024]{5,4,3,2,1,0:T(8,128)(2,1)}, bf16[4,1024,1024]{2,1,0:T(8,128)(2,1)}, bf16[4,1024,10...) custom-call(bf16[8,32,1024]{2,1,0:T(8,128)(2,1)} %get-tuple-element.45.first_rows, ...), custom_call_target="tpu_custom_call" | custom-call | tf_op jit(solution)/shard_map/experts/pallas_call | solution.py:817
  197.6 145.1 %attend_back.1 = (bf16[512,1024]{1,0:T(8,128)(2,1)}, f32[512,1024]{1,0:T(8,128)}, bf16[256,16,1024]{2,1,0:T(8,128)(2,1)}, f32[8,1024]{1,0:T(8,128)}) custom-call(s32[1,2]{1,0:T(1,128)} %lens.3, s32[512,1]{1,0:T(8,128)} %get-tuple-element.40.slot_col, bf16[512,1024]{1,0:T(8,128)(2,1)} %tokens_h.1, f32[512,1024]{1,0:T(8,128)} %get-tuple-element.41.middle_h, ...), custom_call_target="tpu_custom_call" | custom-call | tf_op jit(solution)/shard_map/attend_back/pallas_call | solution.py:1368
  342.7 0.0 copy-start.1
  342.7 0.0 copy-start
  342.7 27.0 %finish.1 = (f32[4,1024,1024]{2,1,0:T(8,128)}, f32[4,1024,1024]{2,1,0:T(8,128)}, f32[1024,3072]{1,0:T(8,128)}, f32[1024,1024]{1,0:T(8,128)}, f32[1024]{0:T(1024)...) custom-call(bf16[4,1024,1024]{2,1,0:T(8,128)(2,1)} %get-tuple-element.52.wi, ...), custom_call_target="tpu_custom_call" | custom-call | tf_op jit(solution)/shard_map/finish/pallas_call | solution.py:878
  369.7 0.0 copy-done.1
  369.8 1.0 copy.30
  370.7 0.0 copy-done
  370.7 1.3 copy.31
Async XLA Ops:
  342.7 27.1 %copy-start.1 = (bf16[512,1024]{1,0:T(8,128)(2,1)S(1)}, bf16[512,1024]{1,0:T(8,128)(2,1)}, u32[]{:S(2)}) copy-start(bf16[512,1024]{1,0:T(8,128)(2,1)} %get-tuple-element.80) | copy-start | bytes 3145732
  342.7 28.0 %copy-start = (f32[512,1024]{1,0:T(8,128)S(1)}, f32[512,1024]{1,0:T(8,128)}, u32[]{:S(2)}) copy-start(f32[512,1024]{1,0:T(8,128)} %get-tuple-element.81) | copy-start | bytes 6291460

commit v8 on v7

--- a/solution.py
+++ b/solution.py
@@ -298,9 +298,9 @@
     def advance(k):
         spread.pass_on(k)
 
-        @pl.when(k > 0)
-        def _():
-            spread.pass_y(k - 1)
+        @pl.when(k > 1)
+        def _():
+            spread.pass_y(k - 2)
 
     def first(k):
         return rcopy(
@@ -406,6 +406,7 @@
     def _(k):
         advance(k)
 
+    spread.pass_y(n_exp - 2)
     spread.pass_y(n_exp - 1)
     for cp in stores:
         cp.wait()
@@ -785,21 +786,26 @@
             for cp in weights(ex + 2):
                 cp.start()
 
-        @pl.when(ex > 0)
+        @pl.when((ex > 0) & (ex < lc - 1))
         def _():
             weight_grads(ex - 1, lambda i: None)
 
         @pl.when(ex + 1 < lc)
         def _():
             g_copy(ex + 1).start()
+
+    def nearly(i):
+        @pl.when(i == 1)
+        def _():
+            gather.step_exp(lc - 1, 0)
 
     def last(i):
         @pl.when(i == 0)
         def _():
-            gather.step_exp(lc - 1, 0)
-
+            gather.step_exp(lc - 1, 1)
+
+    weight_grads(lc - 2, nearly)
     weight_grads(lc - 1, last)
-    gather.step_exp(lc - 1, 1)
     f_copy(lc - 1, 0).wait()
 
     @pl.loop(0, lc)

time: 373 us -> 371 us (level)
  no operation moved by 1% of the time
where the time goes in v8:
time: 371 us; the launch traced here: 370 us
  Pallas kernels  366 us (99%)
    pallas_call x1, Pallas kernels, attend_back(): pl.pallas_call(functools.partial(attend_back_kernel, n_exp, n_y), name='a...  146 us
    pallas_call x1, Pallas kernels, experts(): pl.pallas_call(functools.partial(expert_kernel, n_exp, n_y), name='expert...  125 us
    pallas_call x1, Pallas kernels, attend(): pl.pallas_call(functools.partial(attend_kernel, n_exp, n_y), name='attend...  67.5 us
    pallas_call x1, Pallas kernels, finish(): pl.pallas_call(finish_kernel, name='finish', grid=(lc, cut), out_shape=(s...  27 us

profile of v8, /device:TPU:0, one launch (start us, length us, event | category | flops | bytes accessed | tf_op | source)
XLA Modules:
  0.0 370.4 jit_solution(13669759016197550939)
XLA Ops:
  0.6 1.4 pad_bitcast_fusion.hash_table
  2.0 67.5 %attend.1 = (bf16[512,3072]{1,0:T(8,128)(2,1)}, bf16[512,1024]{1,0:T(8,128)(2,1)}, f32[512,1024]{1,0:T(8,128)}, f32[512,128]{1,0:T(8,128)}, s32[512,1]{1,0:T(8,1...) custom-call(s32[1,2]{1,0:T(1,128)} %lens.3, ...), custom_call_target="tpu_custom_call" | custom-call | tf_op jit(solution)/shard_map/attend/pallas_call | solution.py:430
  69.6 124.9 %experts.1 = (bf16[8,4,32,1024]{3,2,1,0:T(8,128)(2,1)}, bf16[4,8,2,2,32,1024]{5,4,3,2,1,0:T(8,128)(2,1)}, bf16[4,1024,1024]{2,1,0:T(8,128)(2,1)}, bf16[4,1024,10...) custom-call(bf16[8,32,1024]{2,1,0:T(8,128)(2,1)} %get-tuple-element.45.first_rows, ...), custom_call_target="tpu_custom_call" | custom-call | tf_op jit(solution)/shard_map/experts/pallas_call | solution.py:823
  194.5 146.5 %attend_back.1 = (bf16[512,1024]{1,0:T(8,128)(2,1)}, f32[512,1024]{1,0:T(8,128)}, bf16[256,16,1024]{2,1,0:T(8,128)(2,1)}, f32[8,1024]{1,0:T(8,128)}) custom-call(s32[1,2]{1,0:T(1,128)} %lens.3, s32[512,1]{1,0:T(8,128)} %get-tuple-element.40.slot_col, bf16[512,1024]{1,0:T(8,128)(2,1)} %tokens_h.1, f32[512,1024]{1,0:T(8,128)} %get-tuple-element.41.middle_h, ...), custom_call_target="tpu_custom_call" | custom-call | tf_op jit(solution)/shard_map/attend_back/pallas_call | solution.py:1374
  341.0 0.0 copy-start.1
  341.0 0.0 copy-start
  341.0 27.0 %finish.1 = (f32[4,1024,1024]{2,1,0:T(8,128)}, f32[4,1024,1024]{2,1,0:T(8,128)}, f32[1024,3072]{1,0:T(8,128)}, f32[1024,1024]{1,0:T(8,128)}, f32[1024]{0:T(1024)...) custom-call(bf16[4,1024,1024]{2,1,0:T(8,128)(2,1)} %get-tuple-element.52.wi, ...), custom_call_target="tpu_custom_call" | custom-call | tf_op jit(solution)/shard_map/finish/pallas_call | solution.py:884
  368.1 0.0 copy-done.1
  368.1 1.0 copy.30
  369.1 0.0 copy-done
  369.1 1.3 copy.31
Async XLA Ops:
  341.0 27.1 %copy-start.1 = (bf16[512,1024]{1,0:T(8,128)(2,1)S(1)}, bf16[512,1024]{1,0:T(8,128)(2,1)}, u32[]{:S(2)}) copy-start(bf16[512,1024]{1,0:T(8,128)(2,1)} %get-tuple-element.80) | copy-start | bytes 3145732
  341.0 28.0 %copy-start = (f32[512,1024]{1,0:T(8,128)S(1)}, f32[512,1024]{1,0:T(8,128)}, u32[]{:S(2)}) copy-start(f32[512,1024]{1,0:T(8,128)} %get-tuple-element.81) | copy-start | bytes 6291460

commit v9 on v8

--- a/solution.py
+++ b/solution.py
@@ -906,7 +906,7 @@
     )(wi, wb, mats, norms, bi, bb)
 
 
-EARLY = (2,)
+EARLY = (1,)
 
 
 class Reduce:
@@ -1251,9 +1251,9 @@
 
     @pl.loop(0, n_pairs)
     def _(p):
-        @pl.when(p + 4 < n_exp)
-        def _():
-            leave(p + 4)
+        @pl.when((p >= 1) & (p + 3 < n_exp))
+        def _():
+            leave(p + 3)
 
         @pl.when((p >= 2) & (lax.rem(p, 2) == 0))
         def _():
@@ -1313,7 +1313,7 @@
 
         total.begin(part + 1)
 
-    @pl.loop(n_pairs + 4, max(n_exp, n_pairs + 4))
+    @pl.loop(n_pairs + 3, max(n_exp, n_pairs + 3))
     def _(m):
         leave(m)
 

time: 371 us -> 371 us (level)
  no operation moved by 1% of the time
where the time goes in v9:
time: 371 us; the launch traced here: 370 us
  Pallas kernels  366 us (99%)
    pallas_call x1, Pallas kernels, attend_back(): pl.pallas_call(functools.partial(attend_back_kernel, n_exp, n_y), name='a...  146 us
    pallas_call x1, Pallas kernels, experts(): pl.pallas_call(functools.partial(expert_kernel, n_exp, n_y), name='expert...  125 us
    pallas_call x1, Pallas kernels, attend(): pl.pallas_call(functools.partial(attend_kernel, n_exp, n_y), name='attend...  67.5 us
    pallas_call x1, Pallas kernels, finish(): pl.pallas_call(finish_kernel, name='finish', grid=(lc, cut), out_shape=(s...  27 us

profile of v9, /device:TPU:0, one launch (start us, length us, event | category | flops | bytes accessed | tf_op | source)
XLA Modules:
  0.0 370.3 jit_solution(4798782675687537746)
XLA Ops:
  0.6 1.4 pad_bitcast_fusion.hash_table
  2.0 67.5 %attend.1 = (bf16[512,3072]{1,0:T(8,128)(2,1)}, bf16[512,1024]{1,0:T(8,128)(2,1)}, f32[512,1024]{1,0:T(8,128)}, f32[512,128]{1,0:T(8,128)}, s32[512,1]{1,0:T(8,1...) custom-call(s32[1,2]{1,0:T(1,128)} %lens.3, ...), custom_call_target="tpu_custom_call" | custom-call | tf_op jit(solution)/shard_map/attend/pallas_call | solution.py:430
  69.6 124.9 %experts.1 = (bf16[8,4,32,1024]{3,2,1,0:T(8,128)(2,1)}, bf16[4,8,2,2,32,1024]{5,4,3,2,1,0:T(8,128)(2,1)}, bf16[4,1024,1024]{2,1,0:T(8,128)(2,1)}, bf16[4,1024,10...) custom-call(bf16[8,32,1024]{2,1,0:T(8,128)(2,1)} %get-tuple-element.45.first_rows, ...), custom_call_target="tpu_custom_call" | custom-call | tf_op jit(solution)/shard_map/experts/pallas_call | solution.py:823
  194.5 146.4 %attend_back.1 = (bf16[512,1024]{1,0:T(8,128)(2,1)}, f32[512,1024]{1,0:T(8,128)}, bf16[256,16,1024]{2,1,0:T(8,128)(2,1)}, f32[8,1024]{1,0:T(8,128)}) custom-call(s32[1,2]{1,0:T(1,128)} %lens.3, s32[512,1]{1,0:T(8,128)} %get-tuple-element.40.slot_col, bf16[512,1024]{1,0:T(8,128)(2,1)} %tokens_h.1, f32[512,1024]{1,0:T(8,128)} %get-tuple-element.41.middle_h, ...), custom_call_target="tpu_custom_call" | custom-call | tf_op jit(solution)/shard_map/attend_back/pallas_call | solution.py:1374
  341.0 0.0 copy-start.1
  341.0 0.0 copy-start
  341.0 27.0 %finish.1 = (f32[4,1024,1024]{2,1,0:T(8,128)}, f32[4,1024,1024]{2,1,0:T(8,128)}, f32[1024,3072]{1,0:T(8,128)}, f32[1024,1024]{1,0:T(8,128)}, f32[1024]{0:T(1024)...) custom-call(bf16[4,1024,1024]{2,1,0:T(8,128)(2,1)} %get-tuple-element.52.wi, ...), custom_call_target="tpu_custom_call" | custom-call | tf_op jit(solution)/shard_map/finish/pallas_call | solution.py:884
  368.0 0.0 copy-done.1
  368.0 1.0 copy.30
  369.0 0.0 copy-done
  369.0 1.3 copy.31
Async XLA Ops:
  341.0 27.1 %copy-start.1 = (bf16[512,1024]{1,0:T(8,128)(2,1)S(1)}, bf16[512,1024]{1,0:T(8,128)(2,1)}, u32[]{:S(2)}) copy-start(bf16[512,1024]{1,0:T(8,128)(2,1)} %get-tuple-element.80) | copy-start | bytes 3145732
  341.0 28.0 %copy-start = (f32[512,1024]{1,0:T(8,128)S(1)}, f32[512,1024]{1,0:T(8,128)}, u32[]{:S(2)}) copy-start(f32[512,1024]{1,0:T(8,128)} %get-tuple-element.81) | copy-start | bytes 6291460
